TPU v7x, 32 devices: a whole 2x2x4 slice. The times are simulated.
32 devices in a mesh: dp: 2 (over x), graph: 16 (over z, y, core).
Axes of the slice: x: 2, y: 2, z: 4, core: 2. Of those that a mesh axis runs over, the one named last changes fastest.
Arguments:
- node_feats: bfloat16 [2, 128, 25, 128], P('dp', 'graph'), may hold values from -6 to 6
- node_cot: bfloat16 [2, 128, 25, 128], P('dp', 'graph'), may hold values from -6 to 6
- wigner: bfloat16 [2, 19, 25, 4096], P('dp', None, None, 'graph'), may hold values from -4 to 4, as said below
- radial: bfloat16 [2, 4096, 128], P('dp', 'graph'), may hold values from 0.049804688 to 0.5
- source_atom: int32 [2, 4096], P('dp', 'graph'), may hold values from 0 to 127, as said below
- target_index: int32 [2, 4096], P('dp', 'graph'), may hold values from 0 to 7
- edge_counts: int32 [2, 16], P('dp', 'graph'), may hold values from 128 to 256
- merged_weights: bfloat16 [2, 1228800], P('dp', 'graph'), may hold values from -0.25 to 0.25
- mixing: float32 [2, 32], replicated, may hold values from 0.005 to 0.2
Outputs:
- atom_grads: float32 [2, 128, 25, 128], P('dp', 'graph')
- expert_grads: float32 [32, 1228800], P('dp', 'graph')
Inputs may be any that keep to these rules, and one draw needn't show every extreme that they name: `source_atom`: an edge slot held by shard q has its source among the atoms of shards q - 1, q and q + 1 of its system: indices from 8 * max(q - 1, 0) to 8 * min(q + 2, 16) - 1. `edge_counts`: slots of a shard from its count on are padding. `wigner`: an entry is zero where the degree of its frame row differs from the degree of its node coefficient.
All inputs are finite; a program needn't handle non-finite values.
Results may differ from a plain program's by a relative error of at most 0.005.
Values may be sent and summed in bfloat16 or wider, within the bound.
No kernel may reach another device: no remote copies, remote signals or barrier semaphores. Data moves between devices by JAX's collectives and lax.ppermute only.
A program may use at most 128 MiB of HBM per device.

v0:
```python
import functools

import jax
import jax.numpy as jnp
from jax import lax
from jax.experimental import pallas as pl
from jax.experimental.pallas import tpu as pltpu
from jax.sharding import PartitionSpec as P

BF16 = jnp.bfloat16
F32 = jnp.float32
LANES = 128
GROUPS = ((0, 5), (5, 9), (9, 13), (13, 16), (16, 19))
FRAME_ROWS = tuple(
    tuple(
        first + degree - order
        for first, order in ((0, 0), (5, 1), (9, 1), (13, 2), (16, 2))
        if degree >= order
    )
    for degree in range(5)
)
NODE_COLS = tuple(tuple(range(l * l, (l + 1) * (l + 1))) for l in range(5))
WEIGHTS = (5, 4, 4, 3, 3)


def first_rows():
    rows, out = 0, []
    for group_rows in WEIGHTS:
        out.append(rows)
        rows += group_rows * group_rows * LANES
    return out


def place(row):
    if row < 5:
        return 0, row, 0
    if row < 13:
        return 1, (row - 5) % 4, (row - 5) // 4
    return 2, (row - 13) % 3, (row - 13) // 3


def for_chunks(channels, edges, size, body):
    for edge_first in range(0, edges, LANES):

        def step(turn, unused, edge_first=edge_first):
            body(pl.multiple_of(turn * size, size), edge_first)
            return unused

        lax.fori_loop(0, channels // size, step, 0)


def nt(left, right):
    return lax.dot_general(left, right, (((1,), (1,)), ((), ())), preferred_element_type=F32)


def tn(left, right):
    return lax.dot_general(left, right, (((0,), (0,)), ((), ())), preferred_element_type=F32)


def forward_kernel(
    info, source, target, feats_up, feats_own, feats_down, cot, wigner, radial,
    b0, b1, b1i, b2, b2i, keep, send,
    rot, gate, flat, picked, a0, a1, a2, grad,
):
    atoms, coefs, channels = feats_own.shape
    edges = source.shape[1]
    rot[...] = wigner[...].astype(F32)
    gate[...] = radial[...].astype(F32).T
    amat = (a0, a1, a2)
    bmat = (b0, b1, b2)
    bimag = (None, b1i, b2i)
    pitch = flat.shape[0] // (3 * atoms)

    def gather(pieces, pick):
        for place_of, piece in enumerate(pieces):
            for atom in range(atoms):
                at = (place_of * atoms + atom) * pitch
                flat[at : at + coefs, :] = piece[atom].astype(F32)
        count = len(pieces) * atoms
        for coef in range(coefs):
            block = flat[pl.ds(coef, count, stride=pitch), :].astype(BF16)
            picked[coef] = tn(block, pick)

    def rotate(emit):
        def body(at, edge_first):
            lanes = slice(edge_first, edge_first + LANES)
            for rows, cols in zip(FRAME_ROWS, NODE_COLS):
                totals = [None] * len(rows)
                for col in cols:
                    value = picked[col, pl.ds(at, 32), lanes]
                    for n, row in enumerate(rows):
                        term = rot[row, col : col + 1, lanes] * value
                        totals[n] = term if totals[n] is None else totals[n] + term
                for row, total in zip(rows, totals):
                    emit(row, at, edge_first, total)

        for_chunks(channels, edges, 32, body)

    live = lax.broadcasted_iota(jnp.int32, (1, edges), 1) < info[1]
    wanted = jnp.where(live, target[...], -1)
    pick = lax.broadcasted_iota(jnp.int32, (atoms, edges), 0) == wanted
    gather((cot,), pick.astype(F32).astype(BF16))

    def emit_b(row, at, edge_first, total):
        which, block, half = place(row)
        rows = pl.ds(pl.multiple_of(block * channels + at, 32), 32)
        value = total.astype(BF16)
        lanes = slice(half * edges + edge_first, half * edges + edge_first + LANES)
        bmat[which][rows, lanes] = value
        if which:
            other = 1 - half
            lanes = slice(other * edges + edge_first, other * edges + edge_first + LANES)
            bimag[which][rows, lanes] = value if half else (-total).astype(BF16)

    rotate(emit_b)

    nearest = source[...] - (info[0] - 1) * atoms
    pick = lax.broadcasted_iota(jnp.int32, (3 * atoms, edges), 0) == nearest
    gather((feats_up, feats_own, feats_down), pick.astype(F32).astype(BF16))

    def emit_a(row, at, edge_first, total):
        which, block, half = place(row)
        rows = pl.ds(pl.multiple_of(block * channels + at, 32), 32)
        gated = total * gate[pl.ds(at, 32), edge_first : edge_first + LANES]
        lanes = slice(half * edges + edge_first, half * edges + edge_first + LANES)
        amat[which][rows, lanes] = gated.astype(BF16)

    rotate(emit_a)

    rights = (b0, b1, b1i, b2, b2i)
    lefts = (a0, a1, a1, a2, a2)
    for left, right, blocks, first in zip(lefts, rights, WEIGHTS, first_rows()):
        extent = blocks * LANES
        for block in range(0, blocks, 2):
            width = min(2, blocks - block)
            product = nt(left[...], right[block * LANES : (block + width) * LANES, :])
            for n in range(width):
                grad[pl.ds(first + block + n, extent, stride=blocks), :] = product[
                    :, n * LANES : (n + 1) * LANES
                ]
    shards, rows = keep.shape[0], keep.shape[1]
    parity = lax.rem(info[0], 2)
    for n in range(shards):
        keep[n] = grad[pl.ds((2 * n + parity) * rows, rows), :]
        send[n] = grad[pl.ds((2 * n + 1 - parity) * rows, rows), :].astype(BF16)


def backward_kernel(
    info, source, weights, b0, b1, b1i, b2, b2i, wigner, radial,
    out,
    rot, gate, flat, w0, w1r, w1i, w2r, w2i, back, spread,
):
    parts, atoms, coefs, channels = out.shape
    edges = source.shape[1]
    shards, shard_rows = weights.shape[0], weights.shape[1]
    rot[...] = wigner[...].astype(F32)
    gate[...] = radial[...].astype(F32).T
    for n in range(shards):
        flat[n * shard_rows : (n + 1) * shard_rows, :] = weights[n].astype(F32)
    for matrix, blocks, first in zip((w0, w1r, w1i, w2r, w2i), WEIGHTS, first_rows()):
        for block in range(blocks):
            matrix[:, block * LANES : (block + 1) * LANES] = flat[
                pl.ds(first + block, blocks * LANES, stride=blocks), :
            ].astype(BF16)

    dot = functools.partial(jnp.dot, preferred_element_type=F32)
    for row in range(5):
        rows = slice(row * channels, (row + 1) * channels)
        back[row] = dot(w0[rows, :], b0[...]) * gate[...]
    for first, real, imag, upper, lower, blocks in (
        (5, w1r, w1i, b1, b1i, 4),
        (13, w2r, w2i, b2, b2i, 3),
    ):
        for block in range(blocks):
            rows = slice(block * channels, (block + 1) * channels)
            both = dot(real[rows, :], upper[...]) + dot(imag[rows, :], lower[...])
            back[first + block] = both[:, :edges] * gate[...]
            back[first + blocks + block] = both[:, edges:] * gate[...]

    def body(at, edge_first):
        lanes = slice(edge_first, edge_first + LANES)
        for rows, cols in zip(FRAME_ROWS, NODE_COLS):
            totals = [None] * len(cols)
            for row in rows:
                value = back[row, pl.ds(at, 16), lanes]
                for n, col in enumerate(cols):
                    term = rot[row, col : col + 1, lanes] * value
                    totals[n] = term if totals[n] is None else totals[n] + term
            for col, total in zip(cols, totals):
                spread[col, pl.ds(at, 16), lanes] = total.astype(BF16)

    for_chunks(channels, edges, 16, body)
    nearest = source[...] - (info[0] - 1) * atoms
    pick = lax.broadcasted_iota(jnp.int32, (3 * atoms, edges), 0) == nearest
    pick = pick.astype(F32).astype(BF16)
    for col in range(coefs):
        out[:, :, col, :] = nt(pick, spread[col]).reshape(parts, atoms, channels)


def expert_kernel(columns, own_rows, *refs):
    others, out = refs[:-1], refs[-1]
    experts = out.shape[0]
    rows = own_rows.shape[0]
    systems = 1 + len(others)
    scales = [
        jnp.broadcast_to(columns[s], (experts, LANES)) for s in range(systems)
    ]
    group = 12

    def step(turn, unused):
        for n in range(group):
            row = turn * group + n
            total = own_rows[pl.ds(row, 1), :] * scales[0]
            for other, scale in zip(others, scales[1:]):
                total = total + other[pl.ds(row, 1), :] * scale
            out[:, pl.ds(pl.multiple_of(row * LANES, LANES), LANES)] = total
        return unused

    lax.fori_loop(0, rows // group, step, 0)


def spec(space=pltpu.VMEM):
    return pl.BlockSpec(memory_space=space)


PARAMS = pltpu.CompilerParams(vmem_limit_bytes=56 * 1024 * 1024)


def swap(x, axis, bit):
    size = lax.axis_size(axis)
    return lax.ppermute(x, axis, [(i, i ^ bit) for i in range(size)])


def on_device(
    node_feats, node_cot, wigner, radial, source_atom, target_index, edge_counts,
    merged_weights, mixing,
):
    atoms, coefs, channels = node_feats.shape[1:]
    edges = source_atom.shape[1]
    size = lax.axis_size("graph")
    bits = size.bit_length() - 1
    index = lax.axis_index("graph")
    shard_rows = merged_weights.shape[1] // LANES
    total_rows = shard_rows * size

    feats = node_feats[0]
    feats_up = lax.ppermute(feats, "graph", [(i, i + 1) for i in range(size - 1)])
    feats_down = lax.ppermute(feats, "graph", [(i + 1, i) for i in range(size - 1)])

    gathered = merged_weights.reshape(1, shard_rows, LANES)
    for bit in reversed(range(bits)):
        other = swap(gathered, "graph", 1 << bit)
        mine = ((index >> bit) & 1) == 0
        low = jnp.where(mine, gathered, other)
        high = jnp.where(mine, other, gathered)
        gathered = jnp.stack([low, high], axis=1).reshape(-1, shard_rows, LANES)

    info = jnp.stack([index.astype(jnp.int32), edge_counts[0, 0]])
    shapes = [(5, 1), (4, 2), (4, 2), (3, 2), (3, 2)]
    half = size // 2
    smem = spec(pltpu.SMEM)
    outs = pl.pallas_call(
        forward_kernel,
        out_shape=[
            jax.ShapeDtypeStruct((g * channels, h * edges), BF16) for g, h in shapes
        ]
        + [
            jax.ShapeDtypeStruct((half, shard_rows, LANES), F32),
            jax.ShapeDtypeStruct((half, shard_rows, LANES), BF16),
        ],
        in_specs=[smem] + [spec()] * 8,
        out_specs=[spec()] * 7,
        scratch_shapes=[
            pltpu.VMEM((19, coefs, edges), F32),
            pltpu.VMEM((channels, edges), F32),
            pltpu.VMEM((3 * atoms * 32, channels), F32),
            pltpu.VMEM((coefs, channels, edges), F32),
            pltpu.VMEM((5 * channels, edges), BF16),
            pltpu.VMEM((4 * channels, 2 * edges), BF16),
            pltpu.VMEM((3 * channels, 2 * edges), BF16),
            pltpu.VMEM((total_rows, LANES), F32),
        ],
        compiler_params=PARAMS,
        cost_estimate=pl.CostEstimate(
            flops=3 * 10**9, bytes_accessed=10 * 10**6, transcendentals=0
        ),
        name="forward",
    )(
        info, source_atom, target_index, feats_up, feats, feats_down, node_cot[0],
        wigner[0], radial[0],
    )
    bmats, keep, send = outs[:5], outs[5], outs[6]

    total = keep + swap(send, "graph", 1).astype(F32)
    for bit in range(1, bits):
        total = total.reshape(-1, 2, shard_rows, LANES)
        side = (index >> bit) & 1
        away = lax.dynamic_index_in_dim(total, 1 - side, 1, keepdims=False)
        stay = lax.dynamic_index_in_dim(total, side, 1, keepdims=False)
        total = stay + swap(away.astype(BF16), "graph", 1 << bit).astype(F32)
    share = total[0]

    systems = lax.axis_size("dp")
    place_dp = lax.axis_index("dp")
    rounded = share.astype(BF16)
    others = [
        lax.ppermute(rounded, "dp", [(i, (i + n) % systems) for i in range(systems)])
        .astype(F32)
        for n in range(1, systems)
    ]
    own_experts = mixing.shape[1] // systems
    columns = lax.dynamic_slice_in_dim(mixing, place_dp * own_experts, own_experts, 1)
    order = jnp.stack([(place_dp - n) % systems for n in range(systems)])
    columns = jnp.take(columns, order, axis=0)[:, :, None]
    expert_part = pl.pallas_call(
        expert_kernel,
        out_shape=jax.ShapeDtypeStruct((own_experts, shard_rows * LANES), F32),
        in_specs=[spec()] * (1 + systems),
        out_specs=spec(),
        compiler_params=PARAMS,
        cost_estimate=pl.CostEstimate(
            flops=5 * 10**6, bytes_accessed=6 * 10**6, transcendentals=0
        ),
        name="experts",
    )(columns, share, *others)

    atom_total = pl.pallas_call(
        backward_kernel,
        out_shape=jax.ShapeDtypeStruct((3, atoms, coefs, channels), F32),
        in_specs=[smem] + [spec()] * 9,
        out_specs=spec(),
        scratch_shapes=[
            pltpu.VMEM((19, coefs, edges), F32),
            pltpu.VMEM((channels, edges), F32),
            pltpu.VMEM((total_rows, LANES), F32),
        ]
        + [pltpu.VMEM((g * channels, g * channels), BF16) for g in WEIGHTS]
        + [
            pltpu.VMEM((19, channels, edges), F32),
            pltpu.VMEM((coefs, channels, edges), BF16),
        ],
        compiler_params=PARAMS,
        cost_estimate=pl.CostEstimate(
            flops=3 * 10**9, bytes_accessed=10 * 10**6, transcendentals=0
        ),
        name="backward",
    )(info, source_atom, gathered, *bmats, wigner[0], radial[0])
    from_up = lax.ppermute(atom_total[2], "graph", [(i, i + 1) for i in range(size - 1)])
    from_down = lax.ppermute(atom_total[0], "graph", [(i + 1, i) for i in range(size - 1)])
    atom_grads = (atom_total[1] + from_up + from_down)[None]
    return (atom_grads, expert_part)


def solution(mesh):
    in_specs = (
        P("dp", "graph", None, None),
        P("dp", "graph", None, None),
        P("dp", None, None, "graph"),
        P("dp", "graph", None),
        P("dp", "graph"),
        P("dp", "graph"),
        P("dp", "graph"),
        P("dp", "graph"),
        P(),
    )
    out_specs = (P("dp", "graph", None, None), P("dp", "graph"))
    return jax.shard_map(
        on_device, mesh=mesh, in_specs=in_specs, out_specs=out_specs, check_vma=False
    )
```

profile of v0, /device:TPU:1, one launch (start us, length us, event | category | flops | bytes accessed | tf_op | source)
XLA Modules:
  0.0 102.2 jit_solution(2318370882769222473)
XLA Ops:
  0.6 0.8 copy.44
  1.5 4.5 %collective-permute-start.4 = (bf16[8,25,128]{2,1,0:T(8,128)(2,1)S(1)}, bf16[8,25,128]{2,1,0:T(8,128)(2,1)S(1)}, u32[]{:S(2)}, u32[]{:S(2)}) collective-permute-start(bf16[8,25,128]{2,1,0:T(8,128)(2,1)S(1)} %bitcast.98), channel_id=1, source_target_pairs={{0,1},{1,2},{2,3},{3,4},{4,5},{5,6},{6,7},{7,8},{8,9},{9,10},{10,1... | collective-permute-start | bytes 153608 | tf_op jit(solution)/shard_map/ppermute | solution.py:247
  6.0 1.9 %collective-permute-start.5 = (bf16[8,25,128]{2,1,0:T(8,128)(2,1)S(1)}, bf16[8,25,128]{2,1,0:T(8,128)(2,1)S(1)}, u32[]{:S(2)}, u32[]{:S(2)}) collective-permute-start(bf16[8,25,128]{2,1,0:T(8,128)(2,1)S(1)} %bitcast.99), channel_id=1, source_target_pairs={{1,0},{2,1},{3,2},{4,3},{5,4},{6,5},{7,6},{8,7},{9,8},{10,9},{11,1... | collective-permute-start | bytes 153608 | tf_op jit(solution)/shard_map/ppermute | solution.py:248
  8.0 1.8 %reduce = bf16[76800]{0:T(1024)(128)(2,1)S(1)} reduce(bf16[1,76800]{1,0:T(2,128)(2,1)} %param.16, bf16[]{:T(256)} %constant.78), dimensions={0}, to_apply=%param.16.reduce_sub_computation | reduce | bytes 307202 | tf_op args[7]
  9.8 2.4 %collective-permute-start = (bf16[1,600,128]{2,1,0:T(8,128)(2,1)S(1)}, bf16[1,600,128]{2,1,0:T(8,128)(2,1)S(1)}, u32[]{:S(2)}, u32[]{:S(2)}) collective-permute-start(bf16[1,600,128]{2,1,0:T(8,128)(2,1)S(1)} %bitcast.95), channel_id=1, source_target_pairs={{0,8},{1,9},{2,10},{3,11},{4,12},{5,13},{6,14},{7,15},{8,0},{9,1},... | collective-permute-start | bytes 460808 | tf_op jit(solution)/shard_map/ppermute | solution.py:231
  12.8 0.6 pad_add_fusion.info
  13.4 1.4 %copy.43 = bf16[1,8,25,128]{3,2,1,0:T(8,128)(2,1)} copy(bf16[1,8,25,128]{3,1,2,0:T(8,128)(2,1)} %param.10) | data formatting | bytes 102400 | tf_op args[1]
  14.8 1.8 %copy.42 = bf16[1,19,25,256]{3,2,1,0:T(8,128)(2,1)} copy(bf16[1,19,25,256]{3,1,2,0:T(8,128)(2,1)} %param.11) | data formatting | bytes 486400 | tf_op args[2]
  16.6 0.6 copy-done.4
  17.2 8.9 %forward.1 = (bf16[640,256]{1,0:T(8,128)(2,1)}, bf16[512,512]{1,0:T(8,128)(2,1)}, bf16[512,512]{1,0:T(8,128)(2,1)}, bf16[384,512]{1,0:T(8,128)(2,1)}, bf16[384,5...) custom-call(s32[2]{0:T(128)} %pad_add_fusion.info, s32[1,256]{1,0:T(1,128)} %source.3, ...), custom_call_target="tpu_custom_call" | custom-call | flops 3000000000 | bytes 10000000 | tf_op jit(solution)/shard_map/forward/pallas_call | solution.py:262
  26.1 1.8 %collective-permute-start.8 = (bf16[8,600,128]{2,1,0:T(8,128)(2,1)}, bf16[8,600,128]{2,1,0:T(8,128)(2,1)S(1)}, u32[]{:S(2)}, u32[]{:S(2)}) collective-permute-start(bf16[8,600,128]{2,1,0:T(8,128)(2,1)} %get-tuple-element.15), channel_id=1, source_target_pairs={{0,1},{1,0},{2,3},{3,2},{4,5},{5,4},{6,7},{7,6},{8,9},{9,8},{10,11... | collective-permute-start | bytes 3686408 | tf_op jit(solution)/shard_map/ppermute | solution.py:231
  27.9 1.4 %collective-permute-start.1 = (bf16[2,600,128]{2,1,0:T(8,128)(2,1)S(1)}, bf16[2,600,128]{2,1,0:T(8,128)(2,1)S(1)}, u32[]{:S(2)}, u32[]{:S(2)}) collective-permute-start(bf16[2,600,128]{2,1,0:T(8,128)(2,1)S(1)} %maximum_bitcast_fusion), channel_id=1, source_target_pairs={{0,4},{1,5},{2,6},{3,7},{4,0},{5,1},{6,2},{7,3},{8,12},{9,13},{10,... | collective-permute-start | bytes 921608 | tf_op jit(solution)/shard_map/ppermute | solution.py:231
  29.3 7.6 %collective-permute-done.1 = bf16[2,600,128]{2,1,0:T(8,128)(2,1)S(1)} collective-permute-done((bf16[2,600,128]{2,1,0:T(8,128)(2,1)S(1)}, bf16[2,600,128]{2,1,0:T(8,128)(2,1)S(1)}, u32[]{:S(2)}, u32[]{:S(2)}) %collective-permute-start.1) | collective-permute-done | bytes 307232 | tf_op jit(solution)/shard_map/ppermute | solution.py:231
  37.0 0.4 collective-permute-start.2
  37.5 1.1 %copy-done.2 = bf16[8,600,128]{2,1,0:T(8,128)(2,1)} copy-done((bf16[8,600,128]{2,1,0:T(8,128)(2,1)}, bf16[8,600,128]{2,1,0:T(8,128)(2,1)S(1)}, u32[]{:S(2)}) %copy-start.2) | copy-done | bytes 1228824
  38.6 1.5 %convert_add_fusion = f32[8,600,128]{2,1,0:T(8,128)S(1)} fusion(f32[8,600,128]{2,1,0:T(8,128)S(1)} %copy-done.1, bf16[8,600,128]{2,1,0:T(8,128)(2,1)} %copy-done.2), kind=kLoop, calls=%fused_computation.2 | loop fusion | flops 1228800 | bytes 6144000 | tf_op jit(solution)/shard_map/add | solution.py:294
  40.1 0.9 fusion
  41.1 1.1 %collective-permute-start.9 = (bf16[4,600,128]{2,1,0:T(8,128)(2,1)}, bf16[4,600,128]{2,1,0:T(8,128)(2,1)S(1)}, u32[]{:S(2)}, u32[]{:S(2)}) collective-permute-start(bf16[4,600,128]{2,1,0:T(8,128)(2,1)} %fusion), channel_id=1, source_target_pairs={{0,2},{1,3},{2,0},{3,1},{4,6},{5,7},{6,4},{7,5},{8,10},{9,11},{10,... | collective-permute-start | bytes 1843208 | tf_op jit(solution)/shard_map/ppermute | solution.py:231
  42.2 9.5 %collective-permute-done.2 = bf16[4,600,128]{2,1,0:T(8,128)(2,1)S(1)} collective-permute-done((bf16[4,600,128]{2,1,0:T(8,128)(2,1)S(1)}, bf16[4,600,128]{2,1,0:T(8,128)(2,1)S(1)}, u32[]{:S(2)}, u32[]{:S(2)}) %collective-permute-start.2) | collective-permute-done | bytes 614432 | tf_op jit(solution)/shard_map/ppermute | solution.py:231
  51.7 0.2 select_bitcast_fusion.3
  51.9 0.1 pad_maximum_fusion.1
  52.0 1.1 %copy.28 = bf16[4,2,600,128]{3,2,1,0:T(8,128)(2,1)} copy(bf16[4,2,600,128]{3,2,0,1:T(8,128)(2,1)S(1)} %pad_maximum_fusion.1) | data formatting | bytes 2457600 | tf_op jit(solution)/shard_map/stack | solution.py:256
  53.1 3.0 %collective-permute-start.3 = (bf16[8,600,128]{2,1,0:T(8,128)(2,1)}, bf16[8,600,128]{2,1,0:T(8,128)(2,1)}, u32[]{:S(2)}, u32[]{:S(2)}) collective-permute-start(bf16[8,600,128]{2,1,0:T(8,128)(2,1)} %bitcast.11), channel_id=1, source_target_pairs={{0,1},{1,0},{2,3},{3,2},{4,5},{5,4},{6,7},{7,6},{8,9},{9,8},{10,11... | collective-permute-start | bytes 3686408 | tf_op jit(solution)/shard_map/ppermute | solution.py:231
  56.1 0.1 fusion.5
  56.1 0.6 gather_fusion
  56.7 0.1 copy.33
  56.8 8.0 %collective-permute-done.9 = bf16[4,600,128]{2,1,0:T(8,128)(2,1)S(1)} collective-permute-done((bf16[4,600,128]{2,1,0:T(8,128)(2,1)}, bf16[4,600,128]{2,1,0:T(8,128)(2,1)S(1)}, u32[]{:S(2)}, u32[]{:S(2)}) %collective-permute-start.9) | collective-permute-done | bytes 614432 | tf_op jit(solution)/shard_map/ppermute | solution.py:231
  64.8 0.1 bitcast_add_fusion
  65.0 1.4 %collective-permute-start.10 = (bf16[2,600,128]{2,1,0:T(8,128)(2,1)S(1)}, bf16[2,600,128]{2,1,0:T(8,128)(2,1)S(1)}, u32[]{:S(2)}, u32[]{:S(2)}) collective-permute-start(bf16[2,600,128]{2,1,0:T(8,128)(2,1)S(1)} %fusion.1), channel_id=1, source_target_pairs={{0,4},{1,5},{2,6},{3,7},{4,0},{5,1},{6,2},{7,3},{8,12},{9,13},{10,... | collective-permute-start | bytes 921608 | tf_op jit(solution)/shard_map/ppermute | solution.py:231
  66.4 0.1 compare_and_fusion
  66.5 0.7 broadcast_select_fusion.columns
  67.1 5.0 %collective-permute-done.10 = bf16[2,600,128]{2,1,0:T(8,128)(2,1)S(1)} collective-permute-done((bf16[2,600,128]{2,1,0:T(8,128)(2,1)S(1)}, bf16[2,600,128]{2,1,0:T(8,128)(2,1)S(1)}, u32[]{:S(2)}, u32[]{:S(2)}) %collective-permute-start.10) | collective-permute-done | bytes 307232 | tf_op jit(solution)/shard_map/ppermute | solution.py:231
  72.3 0.2 collective-permute-start.11
  72.5 1.8 %select_bitcast_fusion.1 = (bf16[8,1,600,128]{3,2,0,1:T(8,128)(2,1)S(1)}, bf16[8,1,600,128]{3,2,0,1:T(8,128)(2,1)S(1)}) fusion(bf16[8,600,128]{2,1,0:T(8,128)(2,1)} %collective-permute-done.3, pred[]{:T(512)S(6)} %eq.15, bf16[4,2,600,128]{3,2,1,0:T(8,128)(2,1)} %copy.28), kind=kLoop, calls=%fused_computation.7 | loop fusion | flops 1228800 | bytes 4915201 | tf_op jit(solution)/shard_map/stack | solution.py:256
  74.3 0.2 pad_maximum_fusion
  74.5 1.6 %copy.29 = bf16[8,2,600,128]{3,2,1,0:T(8,128)(2,1)} copy(bf16[8,2,600,128]{3,2,0,1:T(8,128)(2,1)S(1)} %pad_maximum_fusion) | data formatting | bytes 4915200 | tf_op jit(solution)/shard_map/stack | solution.py:256
  76.2 7.0 %backward.1 = f32[3,8,25,128]{3,2,1,0:T(8,128)} custom-call(s32[2]{0:T(128)} %pad_add_fusion.info, s32[1,256]{1,0:T(1,128)} %source.3, bf16[16,600,128]{2,1,0:T(8,128)(2,1)} %bitcast.93, bf16[640,256]{1,0:T(8,128)(2,1)} %get-tuple-element.9.b0, bf16[512,512]{1,0:T(8,128)(2,1)} %get-tuple-element.10.b1, bf16[512,512]{1,0:T(8,128)(2,1)} %get-tuple-element.11.b1i, ...), custom_call_target="tpu_custom_call" | custom-call | flops 3000000000 | bytes 10000000 | tf_op jit(solution)/shard_map/backward/pallas_call | solution.py:327
  83.2 1.0 slice_bitcast_fusion.1
  84.2 4.7 %collective-permute-start.7 = (f32[8,25,128]{2,1,0:T(8,128)S(1)}, f32[8,25,128]{2,1,0:T(8,128)S(1)}, u32[]{:S(2)}, u32[]{:S(2)}) collective-permute-start(f32[8,25,128]{2,1,0:T(8,128)S(1)} %get-tuple-element.31), channel_id=1, source_target_pairs={{1,0},{2,1},{3,2},{4,3},{5,4},{6,5},{7,6},{8,7},{9,8},{10,9},{11,1... | collective-permute-start | bytes 307208 | tf_op jit(solution)/shard_map/ppermute | solution.py:349
  88.9 2.1 %collective-permute-start.6 = (f32[8,25,128]{2,1,0:T(8,128)S(1)}, f32[8,25,128]{2,1,0:T(8,128)S(1)}, u32[]{:S(2)}, u32[]{:S(2)}) collective-permute-start(f32[8,25,128]{2,1,0:T(8,128)S(1)} %get-tuple-element.30), channel_id=1, source_target_pairs={{0,1},{1,2},{2,3},{3,4},{4,5},{5,6},{6,7},{7,8},{8,9},{9,10},{10,1... | collective-permute-start | bytes 307208 | tf_op jit(solution)/shard_map/ppermute | solution.py:348
  91.1 0.8 fusion.6
  91.8 1.2 %collective-permute-start.12 = (bf16[600,128]{1,0:T(8,128)(2,1)S(1)}, bf16[600,128]{1,0:T(8,128)(2,1)S(1)}, u32[]{:S(2)}, u32[]{:S(2)}) collective-permute-start(bf16[600,128]{1,0:T(8,128)(2,1)S(1)} %get-tuple-element.22), channel_id=1, source_target_pairs={{0,16},{16,0},{1,17},{17,1},{2,18},{18,2},{3,19},{19,3},{4,20},{20... | collective-permute-start | bytes 460808 | tf_op jit(solution)/shard_map/ppermute | solution.py:307
  93.0 0.4 collective-permute-done.6
  93.5 0.9 fusion.4
  94.4 0.7 copy.36
  95.1 2.0 %collective-permute-done.12 = bf16[600,128]{1,0:T(8,128)(2,1)S(1)} collective-permute-done((bf16[600,128]{1,0:T(8,128)(2,1)S(1)}, bf16[600,128]{1,0:T(8,128)(2,1)S(1)}, u32[]{:S(2)}, u32[]{:S(2)}) %collective-permute-start.12) | collective-permute-done | bytes 153632 | tf_op jit(solution)/shard_map/ppermute | solution.py:307
  97.1 0.7 convert_element_type.45.refs_0_
  97.9 4.4 %experts.1 = f32[16,76800]{1,0:T(8,128)} custom-call(f32[2,16,1]{2,1,0:T(8,128)} %broadcast_select_fusion.columns, f32[600,128]{1,0:T(8,128)} %get-tuple-element.23.own_rows, f32[600,128]{1,0:T(8,128)} %convert_element_type.45.refs_0_), custom_call_target="tpu_custom_call" | custom-call | flops 5000000 | bytes 6000000 | tf_op jit(solution)/shard_map/experts/pallas_call | solution.py:315
  (26 shorter events, 0.5 us)
Async XLA Ops:
  0.6 36.8 %copy-start = (f32[2,32]{1,0:T(2,128)S(1)}, f32[2,32]{1,0:T(2,128)}, u32[]{:S(2)}) copy-start(f32[2,32]{1,0:T(2,128)} %param.17) | copy-start | bytes 772
  1.5 15.1 %copy-start.3 = (bf16[1,8,25,128]{3,2,1,0:T(8,128)(2,1)}, bf16[1,8,25,128]{3,2,1,0:T(8,128)(2,1)S(1)}, u32[]{:S(2)}) copy-start(bf16[1,8,25,128]{3,2,1,0:T(8,128)(2,1)S(1)} %copy.44) | copy-start | bytes 153604
  1.5 15.1 %collective-permute-start.4 = (bf16[8,25,128]{2,1,0:T(8,128)(2,1)S(1)}, bf16[8,25,128]{2,1,0:T(8,128)(2,1)S(1)}, u32[]{:S(2)}, u32[]{:S(2)}) collective-permute-start(bf16[8,25,128]{2,1,0:T(8,128)(2,1)S(1)} %bitcast.98), channel_id=1, source_target_pairs={{0,1},{1,2},{2,3},{3,4},{4,5},{5,6},{6,7},{7,8},{8,9},{9,10},{10,1... | collective-permute-start | bytes 153608 | tf_op jit(solution)/shard_map/ppermute | solution.py:247
  6.0 10.5 %collective-permute-start.5 = (bf16[8,25,128]{2,1,0:T(8,128)(2,1)S(1)}, bf16[8,25,128]{2,1,0:T(8,128)(2,1)S(1)}, u32[]{:S(2)}, u32[]{:S(2)}) collective-permute-start(bf16[8,25,128]{2,1,0:T(8,128)(2,1)S(1)} %bitcast.99), channel_id=1, source_target_pairs={{1,0},{2,1},{3,2},{4,3},{5,4},{6,5},{7,6},{8,7},{9,8},{10,9},{11,1... | collective-permute-start | bytes 153608 | tf_op jit(solution)/shard_map/ppermute | solution.py:248
  9.8 18.1 %collective-permute-start = (bf16[1,600,128]{2,1,0:T(8,128)(2,1)S(1)}, bf16[1,600,128]{2,1,0:T(8,128)(2,1)S(1)}, u32[]{:S(2)}, u32[]{:S(2)}) collective-permute-start(bf16[1,600,128]{2,1,0:T(8,128)(2,1)S(1)} %bitcast.95), channel_id=1, source_target_pairs={{0,8},{1,9},{2,10},{3,11},{4,12},{5,13},{6,14},{7,15},{8,0},{9,1},... | collective-permute-start | bytes 460808 | tf_op jit(solution)/shard_map/ppermute | solution.py:231
  16.5 0.6 copy-start.4
  16.6 0.6 copy-start.5
  26.1 11.4 %collective-permute-start.8 = (bf16[8,600,128]{2,1,0:T(8,128)(2,1)}, bf16[8,600,128]{2,1,0:T(8,128)(2,1)S(1)}, u32[]{:S(2)}, u32[]{:S(2)}) collective-permute-start(bf16[8,600,128]{2,1,0:T(8,128)(2,1)} %get-tuple-element.15), channel_id=1, source_target_pairs={{0,1},{1,0},{2,3},{3,2},{4,5},{5,4},{6,7},{7,6},{8,9},{9,8},{10,11... | collective-permute-start | bytes 3686408 | tf_op jit(solution)/shard_map/ppermute | solution.py:231
  27.9 9.0 %collective-permute-start.1 = (bf16[2,600,128]{2,1,0:T(8,128)(2,1)S(1)}, bf16[2,600,128]{2,1,0:T(8,128)(2,1)S(1)}, u32[]{:S(2)}, u32[]{:S(2)}) collective-permute-start(bf16[2,600,128]{2,1,0:T(8,128)(2,1)S(1)} %maximum_bitcast_fusion), channel_id=1, source_target_pairs={{0,4},{1,5},{2,6},{3,7},{4,0},{5,1},{6,2},{7,3},{8,12},{9,13},{10,... | collective-permute-start | bytes 921608 | tf_op jit(solution)/shard_map/ppermute | solution.py:231
  29.3 9.3 %copy-start.1 = (f32[8,600,128]{2,1,0:T(8,128)S(1)}, f32[8,600,128]{2,1,0:T(8,128)}, u32[]{:S(2)}) copy-start(f32[8,600,128]{2,1,0:T(8,128)} %get-tuple-element.14) | copy-start | bytes 7372804
  37.0 14.7 %collective-permute-start.2 = (bf16[4,600,128]{2,1,0:T(8,128)(2,1)S(1)}, bf16[4,600,128]{2,1,0:T(8,128)(2,1)S(1)}, u32[]{:S(2)}, u32[]{:S(2)}) collective-permute-start(bf16[4,600,128]{2,1,0:T(8,128)(2,1)S(1)} %bitcast.94), channel_id=1, source_target_pairs={{0,2},{1,3},{2,0},{3,1},{4,6},{5,7},{6,4},{7,5},{8,10},{9,11},{10,... | collective-permute-start | bytes 1843208 | tf_op jit(solution)/shard_map/ppermute | solution.py:231
  37.5 1.1 %copy-start.2 = (bf16[8,600,128]{2,1,0:T(8,128)(2,1)}, bf16[8,600,128]{2,1,0:T(8,128)(2,1)S(1)}, u32[]{:S(2)}) copy-start(bf16[8,600,128]{2,1,0:T(8,128)(2,1)S(1)} %collective-permute-done.8) | copy-start | bytes 3686404
  41.1 23.8 %collective-permute-start.9 = (bf16[4,600,128]{2,1,0:T(8,128)(2,1)}, bf16[4,600,128]{2,1,0:T(8,128)(2,1)S(1)}, u32[]{:S(2)}, u32[]{:S(2)}) collective-permute-start(bf16[4,600,128]{2,1,0:T(8,128)(2,1)} %fusion), channel_id=1, source_target_pairs={{0,2},{1,3},{2,0},{3,1},{4,6},{5,7},{6,4},{7,5},{8,10},{9,11},{10,... | collective-permute-start | bytes 1843208 | tf_op jit(solution)/shard_map/ppermute | solution.py:231
  53.1 19.4 %collective-permute-start.3 = (bf16[8,600,128]{2,1,0:T(8,128)(2,1)}, bf16[8,600,128]{2,1,0:T(8,128)(2,1)}, u32[]{:S(2)}, u32[]{:S(2)}) collective-permute-start(bf16[8,600,128]{2,1,0:T(8,128)(2,1)} %bitcast.11), channel_id=1, source_target_pairs={{0,1},{1,0},{2,3},{3,2},{4,5},{5,4},{6,7},{7,6},{8,9},{9,8},{10,11... | collective-permute-start | bytes 3686408 | tf_op jit(solution)/shard_map/ppermute | solution.py:231
  65.0 7.2 %collective-permute-start.10 = (bf16[2,600,128]{2,1,0:T(8,128)(2,1)S(1)}, bf16[2,600,128]{2,1,0:T(8,128)(2,1)S(1)}, u32[]{:S(2)}, u32[]{:S(2)}) collective-permute-start(bf16[2,600,128]{2,1,0:T(8,128)(2,1)S(1)} %fusion.1), channel_id=1, source_target_pairs={{0,4},{1,5},{2,6},{3,7},{4,0},{5,1},{6,2},{7,3},{8,12},{9,13},{10,... | collective-permute-start | bytes 921608 | tf_op jit(solution)/shard_map/ppermute | solution.py:231
  72.3 18.8 %collective-permute-start.11 = (bf16[1,600,128]{2,1,0:T(8,128)(2,1)S(1)}, bf16[1,600,128]{2,1,0:T(8,128)(2,1)S(1)}, u32[]{:S(2)}, u32[]{:S(2)}) collective-permute-start(bf16[1,600,128]{2,1,0:T(8,128)(2,1)S(1)} %dynamic-slice_convert_fusion), channel_id=1, source_target_pairs={{0,8},{1,9},{2,10},{3,11},{4,12},{5,13},{6,14},{7,15},{8,0},{9,1},... | collective-permute-start | bytes 460808 | tf_op jit(solution)/shard_map/ppermute | solution.py:231
  84.2 8.9 %collective-permute-start.7 = (f32[8,25,128]{2,1,0:T(8,128)S(1)}, f32[8,25,128]{2,1,0:T(8,128)S(1)}, u32[]{:S(2)}, u32[]{:S(2)}) collective-permute-start(f32[8,25,128]{2,1,0:T(8,128)S(1)} %get-tuple-element.31), channel_id=1, source_target_pairs={{1,0},{2,1},{3,2},{4,3},{5,4},{6,5},{7,6},{8,7},{9,8},{10,9},{11,1... | collective-permute-start | bytes 307208 | tf_op jit(solution)/shard_map/ppermute | solution.py:349
  88.9 4.6 %collective-permute-start.6 = (f32[8,25,128]{2,1,0:T(8,128)S(1)}, f32[8,25,128]{2,1,0:T(8,128)S(1)}, u32[]{:S(2)}, u32[]{:S(2)}) collective-permute-start(f32[8,25,128]{2,1,0:T(8,128)S(1)} %get-tuple-element.30), channel_id=1, source_target_pairs={{0,1},{1,2},{2,3},{3,4},{4,5},{5,6},{6,7},{7,8},{8,9},{9,10},{10,1... | collective-permute-start | bytes 307208 | tf_op jit(solution)/shard_map/ppermute | solution.py:348
  91.8 5.3 %collective-permute-start.12 = (bf16[600,128]{1,0:T(8,128)(2,1)S(1)}, bf16[600,128]{1,0:T(8,128)(2,1)S(1)}, u32[]{:S(2)}, u32[]{:S(2)}) collective-permute-start(bf16[600,128]{1,0:T(8,128)(2,1)S(1)} %get-tuple-element.22), channel_id=1, source_target_pairs={{0,16},{16,0},{1,17},{17,1},{2,18},{18,2},{3,19},{19,3},{4,20},{20... | collective-permute-start | bytes 460808 | tf_op jit(solution)/shard_map/ppermute | solution.py:307
where the time goes:
time: 104 us; the launch traced here: 102 us
  waiting for transfers between devices  32.6 us (31%)
  starting transfers between devices  26.1 us (25%)
  Pallas kernels  20.3 us (20%)
  local copies, waits for them, and re-layouts  11.8 us (11%)
  other arithmetic  9.9 us (10%)
  between operations  1.45 us (1%)
    ppermute x8, waiting for transfers between devices, swap(): return lax.ppermute(x, axis, [(i, i ^ bit) for i in range(size)])  30.2 us
    ppermute x8, starting transfers between devices, swap(): return lax.ppermute(x, axis, [(i, i ^ bit) for i in range(size)])  11.6 us
    pallas_call x1, Pallas kernels, on_device(): pl.pallas_call(forward_kernel, out_shape=[jax.ShapeDtypeStruct((g * chann...  8.88 us
    pallas_call x1, Pallas kernels, on_device(): pl.pallas_call(backward_kernel, out_shape=jax.ShapeDtypeStruct((3, atoms,...  7.05 us
    unnamed x16, local copies, waits for them, and re-layouts  6.42 us
    ppermute x1, starting transfers between devices, on_device(): lax.ppermute(atom_total[0], 'graph', [(i + 1, i) for i in range(size - 1)])  4.69 us
    ppermute x1, starting transfers between devices, on_device(): lax.ppermute(feats, 'graph', [(i, i + 1) for i in range(size - 1)])  4.54 us
    pallas_call x1, Pallas kernels, on_device(): pl.pallas_call(expert_kernel, out_shape=jax.ShapeDtypeStruct((own_experts...  4.36 us
  transfers between devices with their start and end apart: 13, of which 6 were waited for; matrix products, arithmetic and copies ran while one was open for 18% of the time, Pallas kernels for 16%

commit v1 on v0

v1 whole, which is shorter than its diff:
```python
import functools

import jax
import jax.numpy as jnp
from jax import lax
from jax.experimental import pallas as pl
from jax.experimental.pallas import tpu as pltpu
from jax.sharding import PartitionSpec as P

BF16 = jnp.bfloat16
F32 = jnp.float32
LANES = 128
GROUPS = ((0, 5), (5, 9), (9, 13), (13, 16), (16, 19))
FRAME_ROWS = tuple(
    tuple(
        first + degree - order
        for first, order in ((0, 0), (5, 1), (9, 1), (13, 2), (16, 2))
        if degree >= order
    )
    for degree in range(5)
)
NODE_COLS = tuple(tuple(range(l * l, (l + 1) * (l + 1))) for l in range(5))
WEIGHTS = (5, 4, 4, 3, 3)


def first_rows():
    rows, out = 0, []
    for group_rows in WEIGHTS:
        out.append(rows)
        rows += group_rows * group_rows * LANES
    return out


def place(row):
    if row < 5:
        return 0, row, 0
    if row < 13:
        return 1, (row - 5) % 4, (row - 5) // 4
    return 2, (row - 13) % 3, (row - 13) // 3


def for_chunks(channels, edges, size, body):
    for edge_first in range(0, edges, LANES):

        def step(turn, unused, edge_first=edge_first):
            body(pl.multiple_of(turn * size, size), edge_first)
            return unused

        lax.fori_loop(0, channels // size, step, 0)


def nt(left, right):
    return lax.dot_general(left, right, (((1,), (1,)), ((), ())), preferred_element_type=F32)


def tn(left, right):
    return lax.dot_general(left, right, (((0,), (0,)), ((), ())), preferred_element_type=F32)


def one_hot(count, wanted):
    edges = wanted.shape[1]
    hit = lax.broadcasted_iota(jnp.int32, (count, edges), 0) == wanted
    return hit.astype(F32).astype(BF16)


def near_pick(source, atoms):
    index = lax.axis_index("graph")
    shard = lax.div(source[...], atoms)
    slot = jnp.where(shard == index, 1, jnp.where(shard == (index ^ 1), 0, 2))
    return one_hot(3 * atoms, (slot - shard) * atoms + source[...])


def gather(pieces, pick, picked):
    for coef in range(picked.shape[0]):
        parts = [piece[coef].astype(F32) for piece in pieces]
        block = parts[0] if len(parts) == 1 else jnp.concatenate(parts, axis=0)
        picked[coef] = tn(block.astype(BF16), pick)


def rotate(rot, picked, emit):
    channels, edges = picked.shape[1:]

    def body(at, edge_first):
        lanes = slice(edge_first, edge_first + LANES)
        for rows, cols in zip(FRAME_ROWS, NODE_COLS):
            totals = [None] * len(rows)
            for col in cols:
                value = picked[col, pl.ds(at, 32), lanes]
                for n, row in enumerate(rows):
                    term = rot[col, row : row + 1, lanes] * value
                    totals[n] = term if totals[n] is None else totals[n] + term
            for row, total in zip(rows, totals):
                emit(row, at, edge_first, total)

    for_chunks(channels, edges, 32, body)


def cot_kernel(target, counts, cot, wigner, b0, b1, b2, rot, picked):
    atoms, channels = cot.shape[1:]
    edges = target.shape[1]
    rot[...] = wigner[...].astype(F32)
    bmat = (b0, b1, b2)
    live = lax.broadcasted_iota(jnp.int32, (1, edges), 1) < counts[0, 0]
    gather((cot,), one_hot(atoms, jnp.where(live, target[...], -1)), picked)

    def emit(row, at, edge_first, total):
        which, block, half = place(row)
        rows = pl.ds(pl.multiple_of(block * channels + at, 32), 32)
        lanes = slice(half * edges + edge_first, half * edges + edge_first + LANES)
        bmat[which][rows, lanes] = total.astype(BF16)

    rotate(rot, picked, emit)


def grad_kernel(
    source, feats_core, feats_own, feats_far, wigner, radial, b0, b1, b2,
    keep_a, keep_b, send_a, send_b,
    rot, gate, picked, a0, a1, a2, grad,
):
    atoms, channels = feats_own.shape[1:]
    edges = source.shape[1]
    rot[...] = wigner[...].astype(F32)
    gate[...] = radial[...].astype(F32).T
    amat = (a0, a1, a2)
    gather((feats_core, feats_own, feats_far), near_pick(source, atoms), picked)

    def emit(row, at, edge_first, total):
        which, block, half = place(row)
        rows = pl.ds(pl.multiple_of(block * channels + at, 32), 32)
        gated = total * gate[pl.ds(at, 32), edge_first : edge_first + LANES]
        lanes = slice(half * edges + edge_first, half * edges + edge_first + LANES)
        amat[which][rows, lanes] = gated.astype(BF16)

    rotate(rot, picked, emit)

    def put(first, blocks, block, product):
        for n in range(product.shape[1] // LANES):
            grad[pl.ds(first + block + n, blocks * LANES, stride=blocks), :] = product[
                :, n * LANES : (n + 1) * LANES
            ]

    firsts = first_rows()
    for order, (left, right) in enumerate(((a0, b0), (a1, b1), (a2, b2))):
        blocks = 5 - order
        first = firsts[max(2 * order - 1, 0)]
        for block in range(0, blocks, 2):
            width = min(2, blocks - block)
            part = right[block * LANES : (block + width) * LANES, :]
            put(first, blocks, block, nt(left[...], part))
            if order:
                product = nt(left[:, :edges], part[:, edges:]) - nt(left[:, edges:], part[:, :edges])
                put(firsts[2 * order], blocks, block, product)
    shards, rows_a, rows_b = keep_a.shape[0], keep_a.shape[1], keep_b.shape[1]
    rows = rows_a + rows_b
    parity = lax.rem(lax.axis_index("graph"), 2)
    for n in range(shards):
        at = (2 * n + 1 - parity) * rows
        send_a[n] = grad[pl.ds(at, rows_a), :].astype(BF16)
        send_b[n] = grad[pl.ds(at + rows_a, rows_b), :].astype(BF16)
        at = (2 * n + parity) * rows
        keep_a[n] = grad[pl.ds(at, rows_a), :]
        keep_b[n] = grad[pl.ds(at + rows_a, rows_b), :]


def backward_kernel(
    source, near, far, b0, b1, b2, wigner, radial,
    out_core, out_own, out_far,
    rot, gate, flat, w0, w1r, w1i, w2r, w2i, back, spread,
):
    coefs, atoms, channels = out_own.shape
    edges = source.shape[1]
    rot[...] = wigner[...].astype(F32)
    gate[...] = radial[...].astype(F32).T
    index = lax.axis_index("graph")
    pieces_each, rows = near.shape[:2]
    order = gather_order(pieces_each.bit_length())[:-1]
    for first, pieces in ((0, near), (1, far)):
        for n in range(pieces_each):
            offset = sum(((n >> j) & 1) << order[j] for j in range(len(order)))
            shard = index ^ (offset + first)
            flat[pl.ds(shard * rows, rows), :] = pieces[n].astype(F32)
    for matrix, blocks, first in zip((w0, w1r, w1i, w2r, w2i), WEIGHTS, first_rows()):
        for block in range(blocks):
            matrix[:, block * LANES : (block + 1) * LANES] = flat[
                pl.ds(first + block, blocks * LANES, stride=blocks), :
            ].astype(BF16)

    dot = functools.partial(jnp.dot, preferred_element_type=F32)
    for row in range(5):
        rows = slice(row * channels, (row + 1) * channels)
        back[row] = dot(w0[rows, :], b0[...]) * gate[...]
    for first, real, imag, both, blocks in ((5, w1r, w1i, b1, 4), (13, w2r, w2i, b2, 3)):
        for block in range(blocks):
            rows = slice(block * channels, (block + 1) * channels)
            straight = dot(real[rows, :], both[...])
            crossed = dot(imag[rows, :], both[...])
            back[first + block] = (straight[:, :edges] + crossed[:, edges:]) * gate[...]
            back[first + blocks + block] = (straight[:, edges:] - crossed[:, :edges]) * gate[...]

    def body(at, edge_first):
        lanes = slice(edge_first, edge_first + LANES)
        for rows, cols in zip(FRAME_ROWS, NODE_COLS):
            totals = [None] * len(cols)
            for row in rows:
                value = back[row, pl.ds(at, 16), lanes]
                for n, col in enumerate(cols):
                    term = rot[col, row : row + 1, lanes] * value
                    totals[n] = term if totals[n] is None else totals[n] + term
            for col, total in zip(cols, totals):
                spread[col, pl.ds(at, 16), lanes] = total.astype(BF16)

    for_chunks(channels, edges, 16, body)
    pick = near_pick(source, atoms)
    for col in range(coefs):
        block = nt(pick, spread[col])
        out_core[col] = block[:atoms].astype(BF16)
        out_own[col] = block[atoms : 2 * atoms]
        out_far[col] = block[2 * atoms :].astype(BF16)


def expert_kernel(mixing, own_rows, *refs):
    systems, experts_all = mixing.shape
    others, out, wide = refs[: systems - 1], refs[systems - 1], refs[systems]
    experts, columns = out.shape
    rows = columns // LANES
    position = lax.axis_index("dp")

    @pl.when(pl.program_id(0) == 0)
    def _():
        for n, other in enumerate(others):
            wide[n] = other[...].astype(F32)

    spot = lax.broadcasted_iota(jnp.int32, (experts, experts_all), 1)
    mine = lax.broadcasted_iota(jnp.int32, (experts, experts_all), 0) + position * experts
    scales = []
    for n in range(systems):
        system = lax.rem(position - n + systems, systems)
        row = mixing[pl.ds(system, 1), :]
        column = jnp.sum(jnp.where(spot == mine, row, 0.0), axis=1, keepdims=True)
        scales.append(jnp.broadcast_to(column, (experts, LANES)))
    base = pl.program_id(0) * rows
    group = 12

    def step(turn, unused):
        for n in range(group):
            at = turn * group + n
            total = own_rows[pl.ds(base + at, 1), :] * scales[0]
            for other in range(systems - 1):
                total = total + wide[other, pl.ds(base + at, 1), :] * scales[other + 1]
            out[:, pl.ds(pl.multiple_of(at * LANES, LANES), LANES)] = total
        return unused

    lax.fori_loop(0, rows // group, step, 0)


def spec(space=pltpu.VMEM):
    return pl.BlockSpec(memory_space=space)


KCOST = 1000
PARAMS = pltpu.CompilerParams(vmem_limit_bytes=56 * 1024 * 1024)


def cost(flops, size):
    return pl.CostEstimate(flops=flops, bytes_accessed=size, transcendentals=0)


def gather_order(bits):
    return list(reversed(range(bits)))


def swap(x, bit):
    size = lax.axis_size("graph")
    return lax.ppermute(x, "graph", [(i, i ^ (1 << bit)) for i in range(size)])


def across(x):
    size = lax.axis_size("graph")
    pairs = [(i, i + 1) for i in range(1, size - 1, 2)]
    return lax.ppermute(x, "graph", pairs + [(j, i) for i, j in pairs])


def after(x, *others):
    return lax.optimization_barrier((x,) + others)[0]


def on_device(
    node_feats, node_cot, wigner, radial, source_atom, target_index, edge_counts,
    merged_weights, mixing,
):
    atoms, coefs, channels = node_feats.shape[1:]
    edges = source_atom.shape[1]
    size = lax.axis_size("graph")
    bits = size.bit_length() - 1
    index = lax.axis_index("graph")
    shard_rows = merged_weights.shape[1] // LANES
    total_rows = shard_rows * size
    half = size // 2
    rows_a = (shard_rows // 2 + 7) // 8 * 8
    split = (rows_a, shard_rows - rows_a)

    weight_bits = gather_order(bits)
    held = merged_weights.reshape(1, shard_rows, LANES)
    came = swap(held, weight_bits[0])

    feats = jnp.transpose(node_feats[0], (1, 0, 2))
    feats_far = across(feats)
    feats_core = swap(feats, 0)
    rotation = jnp.transpose(wigner[0], (1, 0, 2))

    shapes = [(5, 1), (4, 2), (3, 2)]
    rot_scratch = pltpu.VMEM((coefs, 19, edges), F32)
    gate_scratch = pltpu.VMEM((channels, edges), F32)
    picked_scratch = pltpu.VMEM((coefs, channels, edges), F32)
    bmats = pl.pallas_call(
        cot_kernel,
        out_shape=[
            jax.ShapeDtypeStruct((g * channels, h * edges), BF16) for g, h in shapes
        ],
        in_specs=[spec(), spec(pltpu.SMEM), spec(), spec()],
        out_specs=[spec()] * 3,
        scratch_shapes=[rot_scratch, picked_scratch],
        compiler_params=PARAMS,
        cost_estimate=cost(KCOST, KCOST),
        name="cotangents",
    )(target_index, edge_counts, jnp.transpose(node_cot[0], (1, 0, 2)), rotation)
    came = after(came, bmats[0])
    held = jnp.concatenate([held, came], axis=0)
    came, held, feats_far = lax.optimization_barrier((came, held, feats_far))
    came = swap(held, weight_bits[1])

    keeps_sends = pl.pallas_call(
        grad_kernel,
        out_shape=[
            jax.ShapeDtypeStruct((half, rows, LANES), kind)
            for kind in (F32, BF16)
            for rows in split
        ],
        in_specs=[spec()] * 9,
        out_specs=[spec()] * 4,
        scratch_shapes=[
            rot_scratch,
            gate_scratch,
            picked_scratch,
            pltpu.VMEM((5 * channels, edges), BF16),
            pltpu.VMEM((4 * channels, 2 * edges), BF16),
            pltpu.VMEM((3 * channels, 2 * edges), BF16),
            pltpu.VMEM((total_rows, LANES), F32),
        ],
        compiler_params=PARAMS,
        cost_estimate=cost(KCOST, KCOST),
        name="gradients",
    )(source_atom, feats_core, feats, feats_far, rotation, radial[0], *bmats)
    keeps, sends = keeps_sends[:2], keeps_sends[2:]
    *sends, came = lax.optimization_barrier((*sends, came))

    held = jnp.concatenate([held, came], axis=0)
    came = swap(held, weight_bits[2])

    halving = list(range(1, bits))
    halving = halving[1:2] + halving[:1] + halving[2:]
    totals = [
        (keep + swap(send, 0).astype(F32)).reshape((2,) * (bits - 1) + keep.shape[1:])
        for keep, send in zip(keeps, sends)
    ]
    left = list(reversed(range(1, bits)))
    for turn, bit in enumerate(halving):
        axis = left.index(bit)
        left.remove(bit)
        side = (index >> bit) & 1
        moved = []
        for total in totals:
            pick = functools.partial(
                lax.dynamic_index_in_dim, total, axis=axis, keepdims=False
            )
            moved.append((pick(side), pick(1 - side).astype(BF16)))
        if turn > 0 and turn + 2 < len(weight_bits):
            came = after(came, moved[0][1])
            held = jnp.concatenate([held, came], axis=0)
            came = swap(held, weight_bits[turn + 2])
        totals = [stay + swap(away, bit).astype(F32) for stay, away in moved]
    came = after(came, moved[1][1])
    share = jnp.concatenate(totals, axis=0)

    systems = lax.axis_size("dp")
    rounded = share.astype(BF16)
    others = [
        lax.ppermute(rounded, "dp", [(i, (i + n) % systems) for i in range(systems)])
        for n in range(1, systems)
    ]
    own_experts = mixing.shape[1] // systems
    blocks = 5
    expert_part = pl.pallas_call(
        expert_kernel,
        grid=(blocks,),
        out_shape=jax.ShapeDtypeStruct((own_experts, shard_rows * LANES), F32),
        in_specs=[spec()] * (1 + systems),
        out_specs=pl.BlockSpec((own_experts, shard_rows * LANES // blocks), lambda i: (0, i)),
        scratch_shapes=[pltpu.VMEM((max(systems - 1, 1), shard_rows, LANES), F32)],
        compiler_params=PARAMS,
        cost_estimate=cost(KCOST, KCOST),
        name="experts",
    )(mixing, share, *others)

    grads_core, grads_own, grads_far = pl.pallas_call(
        backward_kernel,
        out_shape=[
            jax.ShapeDtypeStruct((coefs, atoms, channels), kind) for kind in (BF16, F32, BF16)
        ],
        in_specs=[spec()] * 8,
        out_specs=[spec()] * 3,
        scratch_shapes=[
            rot_scratch,
            gate_scratch,
            pltpu.VMEM((total_rows, LANES), F32),
        ]
        + [pltpu.VMEM((g * channels, g * channels), BF16) for g in WEIGHTS]
        + [
            pltpu.VMEM((19, channels, edges), F32),
            pltpu.VMEM((coefs, channels, edges), BF16),
        ],
        compiler_params=PARAMS,
        cost_estimate=cost(KCOST, KCOST),
        name="backward",
    )(source_atom, held, came, *bmats, rotation, radial[0])
    total = grads_own + swap(grads_core, 0).astype(F32) + across(grads_far).astype(F32)
    atom_grads = jnp.transpose(total, (1, 0, 2))[None]
    return (atom_grads, expert_part)


def solution(mesh):
    in_specs = (
        P("dp", "graph", None, None),
        P("dp", "graph", None, None),
        P("dp", None, None, "graph"),
        P("dp", "graph", None),
        P("dp", "graph"),
        P("dp", "graph"),
        P("dp", "graph"),
        P("dp", "graph"),
        P(),
    )
    out_specs = (P("dp", "graph", None, None), P("dp", "graph"))
    return jax.shard_map(
        on_device, mesh=mesh, in_specs=in_specs, out_specs=out_specs, check_vma=False
    )
```

time: 104 us -> 74.1 us (0.71); the launches traced: 102 us -> 73.8 us
  waiting for transfers between devices: 32.6 us -> 21.6 us
  local copies, waits for them, and re-layouts: 11.8 us -> 3.11 us
  other arithmetic: 9.9 us -> 3.75 us
  starting transfers between devices: 26.1 us -> 21.7 us
  Pallas kernels: 20.3 us -> 22.1 us
    ppermute x12 -> x16, waiting for transfers between devices: 30.6 us -> 21.6 us  [the longest x14 21.6 us: swap(): return lax.ppermute(x, 'graph', [(i, i ^ 1 << bit) for i in range(size)])]
    ppermute x12 -> x16, starting transfers between devices: 24.9 us -> 20.4 us  [the longest x14 14.1 us: swap(): return lax.ppermute(x, 'graph', [(i, i ^ 1 << bit) for i in range(size)])]
    unnamed x16 -> x20, local copies, waits for them, and re-layouts: 6.42 us -> 2.83 us
    another operation x8 -> x0, other arithmetic: 3.08 us -> none  [the longest x7 2.53 us: on_device(): gathered = jnp.stack([low, high], axis=1).reshape(-1, shard_rows, LANES)]
    another operation x2 -> x0, local copies, waits for them, and re-layouts: 2.71 us -> none  [on_device(): gathered = jnp.stack([low, high], axis=1).reshape(-1, shard_rows, LANES)]
    ppermute x1, waiting for transfers between devices: 2.02 us -> 0.01 us  [on_device(): lax.ppermute(rounded, 'dp', [(i, (i + n) % systems) for i in range(system...]
    pallas_call x3 -> x4, Pallas kernels: 20.3 us -> 22.1 us  [the longest x1 7.27 us: on_device(): pl.pallas_call(grad_kernel, out_shape=[jax.ShapeDtypeStruct((half, rows,...]
    add x3 -> x8, other arithmetic: 1.71 us -> 0.43 us  [the longest x2 0.23 us: on_device(): keep + swap(send, 0).astype(F32)]
  transfers between devices with their start and end apart: 13 -> 17, of which waited for: 6 -> 7; matrix products, arithmetic and copies ran while one was open for 18% -> 2% of each run, Pallas kernels for 16% -> 30%
where the time goes in v1:
time: 74.1 us; the launch traced here: 73.8 us
  Pallas kernels  22.1 us (30%)
  starting transfers between devices  21.7 us (29%)
  waiting for transfers between devices  21.6 us (29%)
  other arithmetic  3.75 us (5%)
  local copies, waits for them, and re-layouts  3.11 us (4%)
  between operations  1.47 us (2%)
    ppermute x14, waiting for transfers between devices, swap(): return lax.ppermute(x, 'graph', [(i, i ^ 1 << bit) for i in range(size)])  21.6 us
    ppermute x14, starting transfers between devices, swap(): return lax.ppermute(x, 'graph', [(i, i ^ 1 << bit) for i in range(size)])  14.1 us
    pallas_call x1, Pallas kernels, on_device(): pl.pallas_call(grad_kernel, out_shape=[jax.ShapeDtypeStruct((half, rows,...  7.27 us
    pallas_call x1, Pallas kernels, on_device(): pl.pallas_call(backward_kernel, out_shape=[jax.ShapeDtypeStruct((coefs, a...  6.42 us
    ppermute x2, starting transfers between devices, across(): return lax.ppermute(x, 'graph', pairs + [(j, i) for i, j in pairs])  6.3 us
    pallas_call x1, Pallas kernels, on_device(): pl.pallas_call(expert_kernel, grid=(blocks,), out_shape=jax.ShapeDtypeStr...  4.63 us
    pallas_call x1, Pallas kernels, on_device(): pl.pallas_call(cot_kernel, out_shape=[jax.ShapeDtypeStruct((g * channels,...  3.82 us
    unnamed x20, local copies, waits for them, and re-layouts  2.83 us
  transfers between devices with their start and end apart: 17, of which 7 were waited for; matrix products, arithmetic and copies ran while one was open for 2% of the time, Pallas kernels for 30%

profile of v1, /device:TPU:1, one launch (start us, length us, event | category | flops | bytes accessed | tf_op | source)
XLA Modules:
  0.0 73.8 jit_solution(2158562087435109799)
XLA Ops:
  0.6 0.0 copy-start.6
  0.6 1.8 %reduce = bf16[76800]{0:T(1024)(128)(2,1)S(1)} reduce(bf16[1,76800]{1,0:T(2,128)(2,1)} %param.16, bf16[]{:T(256)} %constant.58), dimensions={0}, to_apply=%param.16.reduce_sub_computation | reduce | bytes 307202 | tf_op args[7]
  2.5 3.2 %collective-permute-start = (bf16[1,600,128]{2,1,0:T(8,128)(2,1)S(1)}, bf16[1,600,128]{2,1,0:T(8,128)(2,1)S(1)}, u32[]{:S(2)}, u32[]{:S(2)}) collective-permute-start(bf16[1,600,128]{2,1,0:T(8,128)(2,1)S(1)} %bitcast.48), channel_id=1, source_target_pairs={{0,8},{1,9},{2,10},{3,11},{4,12},{5,13},{6,14},{7,15},{8,0},{9,1},... | collective-permute-start | bytes 460808 | tf_op jit(solution)/shard_map/ppermute | solution.py:274
  5.7 4.0 %collective-permute-start.1 = (bf16[25,8,128]{2,1,0:T(8,128)(2,1)}, bf16[25,8,128]{2,1,0:T(8,128)(2,1)S(1)}, u32[]{:S(2)}, u32[]{:S(2)}) collective-permute-start(bf16[25,8,128]{2,1,0:T(8,128)(2,1)} %bitcast.53), channel_id=1, source_target_pairs={{1,2},{3,4},{5,6},{7,8},{9,10},{11,12},{13,14},{2,1},{4,3},{6,5},{... | collective-permute-start | bytes 153608 | tf_op jit(solution)/shard_map/ppermute | solution.py:280
  10.3 3.8 %cotangents.1 = (bf16[640,256]{1,0:T(8,128)(2,1)}, bf16[512,512]{1,0:T(8,128)(2,1)}, bf16[384,512]{1,0:T(8,128)(2,1)}) custom-call(s32[1,256]{1,0:T(1,128)} %target.1, s32[1,1]{1,0:T(1,128)S(6)} %copy.27.counts, bf16[25,8,128]{2,1,0:T(8,128)(2,1)} %bitcast.52, bf16[25,19,256]{2,1,0:T(8,128)(2,1)} %bitcast.45), custom_call_target="tpu_custom_call" | custom-call | flops 1000 | bytes 1000 | tf_op jit(solution)/shard_map/cotangents/pallas_call | solution.py:315
  14.2 1.4 %collective-permute-start.3 = (bf16[2,600,128]{2,1,0:T(8,128)(2,1)S(1)}, bf16[2,600,128]{2,1,0:T(8,128)(2,1)S(1)}, u32[]{:S(2)}, u32[]{:S(2)}) collective-permute-start(bf16[2,600,128]{2,1,0:T(8,128)(2,1)S(1)} %pad_maximum_fusion.1), channel_id=1, source_target_pairs={{0,4},{1,5},{2,6},{3,7},{4,0},{5,1},{6,2},{7,3},{8,12},{9,13},{10,... | collective-permute-start | bytes 921608 | tf_op jit(solution)/shard_map/ppermute | solution.py:274
  15.5 1.2 %collective-permute-done.2.feats_core = bf16[25,8,128]{2,1,0:T(8,128)(2,1)S(1)} collective-permute-done((bf16[25,8,128]{2,1,0:T(8,128)(2,1)S(1)}, bf16[25,8,128]{2,1,0:T(8,128)(2,1)S(1)}, u32[]{:S(2)}, u32[]{:S(2)}) %collective-permute-start.2) | collective-permute-done | bytes 51232 | tf_op jit(solution)/shard_map/ppermute | solution.py:274
  16.8 0.6 copy-done.8
  17.4 7.3 %gradients.1 = (f32[8,304,128]{2,1,0:T(8,128)}, f32[8,296,128]{2,1,0:T(8,128)}, bf16[8,304,128]{2,1,0:T(8,128)(2,1)}, bf16[8,296,128]{2,1,0:T(8,128)(2,1)}) custom-call(s32[1,256]{1,0:T(1,128)} %source.3, bf16[25,8,128]{2,1,0:T(8,128)(2,1)} %copy-done.8, bf16[25,8,128]{2,1,0:T(8,128)(2,1)} %bitcast.54, bf16[25,8,128]{2,1,0:T(8,128)(2,1)} %copy-done.7, ...), custom_call_target="tpu_custom_call" | custom-call | flops 1000 | bytes 1000 | tf_op jit(solution)/shard_map/gradients/pallas_call | solution.py:332
  24.7 0.0 collective-permute-done.3
  24.7 0.1 collective-permute-start.8
  24.8 0.5 collective-permute-start.5
  25.3 0.1 pad_maximum_fusion
  25.3 0.4 collective-permute-start.4
  25.7 1.2 %collective-permute-done.8 = bf16[8,296,128]{2,1,0:T(8,128)(2,1)S(1)} collective-permute-done((bf16[8,296,128]{2,1,0:T(8,128)(2,1)}, bf16[8,296,128]{2,1,0:T(8,128)(2,1)S(1)}, u32[]{:S(2)}, u32[]{:S(2)}) %collective-permute-start.8) | collective-permute-done | bytes 606240 | tf_op jit(solution)/shard_map/ppermute | solution.py:274
  26.9 0.1 convert_add_fusion.1
  27.0 0.1 fusion.1
  27.1 0.2 collective-permute-start.9
  27.3 0.5 collective-permute-done.5
  27.8 0.4 copy-done.1
  28.2 0.1 convert_add_fusion
  28.3 0.1 fusion
  28.4 0.5 collective-permute-start.6
  28.9 6.9 %collective-permute-done.9 = bf16[2,2,296,128]{3,2,0,1:T(8,128)(2,1)S(1)} collective-permute-done((bf16[2,2,296,128]{3,2,0,1:T(8,128)(2,1)S(1)}, bf16[2,2,296,128]{3,2,0,1:T(8,128)(2,1)S(1)}, u32[]{:S(2)}, u32[]{:S(2)}) %collective-permute-start.9) | collective-permute-done | bytes 303136 | tf_op jit(solution)/shard_map/ppermute | solution.py:274
  35.8 0.1 bitcast_add_fusion.1
  35.9 0.3 collective-permute-start.10
  36.2 6.3 %collective-permute-done.6 = bf16[2,2,304,128]{3,2,0,1:T(8,128)(2,1)S(1)} collective-permute-done((bf16[2,2,304,128]{3,2,0,1:T(8,128)(2,1)S(1)}, bf16[2,2,304,128]{3,2,0,1:T(8,128)(2,1)S(1)}, u32[]{:S(2)}, u32[]{:S(2)}) %collective-permute-start.6) | collective-permute-done | bytes 311328 | tf_op jit(solution)/shard_map/ppermute | solution.py:274
  42.5 0.1 bitcast_add_fusion
  42.6 0.3 collective-permute-start.13
  42.9 0.0 collective-permute-done.4
  42.9 0.1 constant_dynamic-update-slice_fusion.near
  43.0 0.0 copy-start
  43.0 1.4 %collective-permute-start.7 = (bf16[8,600,128]{2,1,0:T(8,128)(2,1)S(1)}, bf16[8,600,128]{2,1,0:T(8,128)(2,1)S(1)}, u32[]{:S(2)}, u32[]{:S(2)}) collective-permute-start(bf16[8,600,128]{2,1,0:T(8,128)(2,1)S(1)} %constant_dynamic-update-slice_fusion.near), channel_id=1, source_target_pairs={{0,1},{1,0},{2,3},{3,2},{4,5},{5,4},{6,7},{7,6},{8,9},{9,8},{10,11... | collective-permute-start | bytes 3686408 | tf_op jit(solution)/shard_map/ppermute | solution.py:274
  44.4 3.1 %collective-permute-start.15 = (bf16[296,128]{1,0:T(8,128)(2,1)S(1)}, bf16[296,128]{1,0:T(8,128)(2,1)S(1)}, u32[]{:S(2)}, u32[]{:S(2)}) collective-permute-start(bf16[296,128]{1,0:T(8,128)(2,1)S(1)} %fusion.5), channel_id=1, source_target_pairs={{0,8},{1,9},{2,10},{3,11},{4,12},{5,13},{6,14},{7,15},{8,0},{9,1},... | collective-permute-start | bytes 227336 | tf_op jit(solution)/shard_map/ppermute | solution.py:274
  47.5 1.7 %collective-permute-start.14 = (bf16[304,128]{1,0:T(8,128)(2,1)S(1)}, bf16[304,128]{1,0:T(8,128)(2,1)S(1)}, u32[]{:S(2)}, u32[]{:S(2)}) collective-permute-start(bf16[304,128]{1,0:T(8,128)(2,1)S(1)} %fusion.4), channel_id=1, source_target_pairs={{0,8},{1,9},{2,10},{3,11},{4,12},{5,13},{6,14},{7,15},{8,0},{9,1},... | collective-permute-start | bytes 233480 | tf_op jit(solution)/shard_map/ppermute | solution.py:274
  49.2 3.3 %collective-permute-done.15 = bf16[296,128]{1,0:T(8,128)(2,1)S(1)} collective-permute-done((bf16[296,128]{1,0:T(8,128)(2,1)S(1)}, bf16[296,128]{1,0:T(8,128)(2,1)S(1)}, u32[]{:S(2)}, u32[]{:S(2)}) %collective-permute-start.15) | collective-permute-done | bytes 75808 | tf_op jit(solution)/shard_map/ppermute | solution.py:274
  52.5 2.2 %collective-permute-done.14 = bf16[304,128]{1,0:T(8,128)(2,1)S(1)} collective-permute-done((bf16[304,128]{1,0:T(8,128)(2,1)S(1)}, bf16[304,128]{1,0:T(8,128)(2,1)S(1)}, u32[]{:S(2)}, u32[]{:S(2)}) %collective-permute-start.14) | collective-permute-done | bytes 77856 | tf_op jit(solution)/shard_map/ppermute | solution.py:274
  54.8 1.3 %collective-permute-start.16 = (bf16[600,128]{1,0:T(8,128)(2,1)S(1)}, bf16[600,128]{1,0:T(8,128)(2,1)S(1)}, u32[]{:S(2)}, u32[]{:S(2)}) collective-permute-start(bf16[600,128]{1,0:T(8,128)(2,1)S(1)} %fusion.6), channel_id=1, source_target_pairs={{0,16},{16,0},{1,17},{17,1},{2,18},{18,2},{3,19},{19,3},{4,20},{20... | collective-permute-start | bytes 460808 | tf_op jit(solution)/shard_map/ppermute | solution.py:388
  56.1 1.1 %copy-done.2 = bf16[8,600,128]{2,1,0:T(8,128)(2,1)} copy-done((bf16[8,600,128]{2,1,0:T(8,128)(2,1)}, bf16[8,600,128]{2,1,0:T(8,128)(2,1)S(1)}, u32[]{:S(2)}) %copy-start.2) | copy-done | bytes 1228824
  57.1 6.4 %backward.1 = (bf16[25,8,128]{2,1,0:T(8,128)(2,1)}, f32[25,8,128]{2,1,0:T(8,128)}, bf16[25,8,128]{2,1,0:T(8,128)(2,1)}) custom-call(s32[1,256]{1,0:T(1,128)} %source.3, bf16[8,600,128]{2,1,0:T(8,128)(2,1)} %copy-done, bf16[8,600,128]{2,1,0:T(8,128)(2,1)} %copy-done.2, bf16[640,256]{1,0:T(8,128)(2,1)} %get-tuple-element.20.b0, ...), custom_call_target="tpu_custom_call" | custom-call | flops 1000 | bytes 1000 | tf_op jit(solution)/shard_map/backward/pallas_call | solution.py:405
  63.5 1.2 %collective-permute-start.11 = (bf16[25,8,128]{2,1,0:T(8,128)(2,1)}, bf16[25,8,128]{2,1,0:T(8,128)(2,1)S(1)}, u32[]{:S(2)}, u32[]{:S(2)}) collective-permute-start(bf16[25,8,128]{2,1,0:T(8,128)(2,1)} %get-tuple-element.36), channel_id=1, source_target_pairs={{0,1},{1,0},{2,3},{3,2},{4,5},{5,4},{6,7},{7,6},{8,9},{9,8},{10,11... | collective-permute-start | bytes 153608 | tf_op jit(solution)/shard_map/ppermute | solution.py:274
  64.8 2.3 %collective-permute-start.12 = (bf16[25,8,128]{2,1,0:T(8,128)(2,1)}, bf16[25,8,128]{2,1,0:T(8,128)(2,1)S(1)}, u32[]{:S(2)}, u32[]{:S(2)}) collective-permute-start(bf16[25,8,128]{2,1,0:T(8,128)(2,1)} %get-tuple-element.37), channel_id=1, source_target_pairs={{1,2},{3,4},{5,6},{7,8},{9,10},{11,12},{13,14},{2,1},{4,3},{6,5},{... | collective-permute-start | bytes 153608 | tf_op jit(solution)/shard_map/ppermute | solution.py:280
  67.1 0.7 pad_maximum_fusion.2.own_rows
  67.8 0.0 collective-permute-done.16.refs_0_
  67.8 0.7 copy-done.4
  68.5 4.6 %experts.1 = f32[16,76800]{1,0:T(8,128)} custom-call(f32[2,32]{1,0:T(2,128)} %mixing.1, f32[600,128]{1,0:T(8,128)} %pad_maximum_fusion.2.own_rows, bf16[600,128]{1,0:T(8,128)(2,1)} %copy-done.4), custom_call_target="tpu_custom_call" | custom-call | flops 1000 | bytes 1000 | tf_op jit(solution)/shard_map/experts/pallas_call | solution.py:393
  73.1 0.0 collective-permute-done.11
  73.1 0.7 add_bitcast_fusion
  (31 shorter events, 0.3 us)
Async XLA Ops:
  0.6 14.9 %copy-start.6 = (bf16[1,8,25,128]{3,1,2,0:T(8,128)(2,1)S(1)}, bf16[1,8,25,128]{3,1,2,0:T(8,128)(2,1)}, u32[]{:S(2)}) copy-start(bf16[1,8,25,128]{3,1,2,0:T(8,128)(2,1)} %param.9) | copy-start | bytes 153604
  2.5 11.7 %collective-permute-start = (bf16[1,600,128]{2,1,0:T(8,128)(2,1)S(1)}, bf16[1,600,128]{2,1,0:T(8,128)(2,1)S(1)}, u32[]{:S(2)}, u32[]{:S(2)}) collective-permute-start(bf16[1,600,128]{2,1,0:T(8,128)(2,1)S(1)} %bitcast.48), channel_id=1, source_target_pairs={{0,8},{1,9},{2,10},{3,11},{4,12},{5,13},{6,14},{7,15},{8,0},{9,1},... | collective-permute-start | bytes 460808 | tf_op jit(solution)/shard_map/ppermute | solution.py:274
  5.7 8.5 %collective-permute-start.1 = (bf16[25,8,128]{2,1,0:T(8,128)(2,1)}, bf16[25,8,128]{2,1,0:T(8,128)(2,1)S(1)}, u32[]{:S(2)}, u32[]{:S(2)}) collective-permute-start(bf16[25,8,128]{2,1,0:T(8,128)(2,1)} %bitcast.53), channel_id=1, source_target_pairs={{1,2},{3,4},{5,6},{7,8},{9,10},{11,12},{13,14},{2,1},{4,3},{6,5},{... | collective-permute-start | bytes 153608 | tf_op jit(solution)/shard_map/ppermute | solution.py:280
  14.2 2.6 %copy-start.7 = (bf16[25,8,128]{2,1,0:T(8,128)(2,1)}, bf16[25,8,128]{2,1,0:T(8,128)(2,1)S(1)}, u32[]{:S(2)}) copy-start(bf16[25,8,128]{2,1,0:T(8,128)(2,1)S(1)} %collective-permute-done.1.feats_far) | copy-start | bytes 153604
  14.2 10.5 %collective-permute-start.3 = (bf16[2,600,128]{2,1,0:T(8,128)(2,1)S(1)}, bf16[2,600,128]{2,1,0:T(8,128)(2,1)S(1)}, u32[]{:S(2)}, u32[]{:S(2)}) collective-permute-start(bf16[2,600,128]{2,1,0:T(8,128)(2,1)S(1)} %pad_maximum_fusion.1), channel_id=1, source_target_pairs={{0,4},{1,5},{2,6},{3,7},{4,0},{5,1},{6,2},{7,3},{8,12},{9,13},{10,... | collective-permute-start | bytes 921608 | tf_op jit(solution)/shard_map/ppermute | solution.py:274
  15.5 1.2 %collective-permute-start.2 = (bf16[25,8,128]{2,1,0:T(8,128)(2,1)S(1)}, bf16[25,8,128]{2,1,0:T(8,128)(2,1)S(1)}, u32[]{:S(2)}, u32[]{:S(2)}) collective-permute-start(bf16[25,8,128]{2,1,0:T(8,128)(2,1)S(1)} %bitcast.55), channel_id=1, source_target_pairs={{0,1},{1,0},{2,3},{3,2},{4,5},{5,4},{6,7},{7,6},{8,9},{9,8},{10,11... | collective-permute-start | bytes 153608 | tf_op jit(solution)/shard_map/ppermute | solution.py:274
  16.8 0.6 copy-start.8
  24.7 2.2 %collective-permute-start.8 = (bf16[8,296,128]{2,1,0:T(8,128)(2,1)}, bf16[8,296,128]{2,1,0:T(8,128)(2,1)S(1)}, u32[]{:S(2)}, u32[]{:S(2)}) collective-permute-start(bf16[8,296,128]{2,1,0:T(8,128)(2,1)} %get-tuple-element.33), channel_id=1, source_target_pairs={{0,1},{1,0},{2,3},{3,2},{4,5},{5,4},{6,7},{7,6},{8,9},{9,8},{10,11... | collective-permute-start | bytes 1818632 | tf_op jit(solution)/shard_map/ppermute | solution.py:274
  24.8 2.1 %copy-start.3 = (f32[8,296,128]{2,1,0:T(8,128)S(1)}, f32[8,296,128]{2,1,0:T(8,128)}, u32[]{:S(2)}) copy-start(f32[8,296,128]{2,1,0:T(8,128)} %get-tuple-element.32) | copy-start | bytes 3637252
  24.8 3.0 %collective-permute-start.5 = (bf16[8,304,128]{2,1,0:T(8,128)(2,1)}, bf16[8,304,128]{2,1,0:T(8,128)(2,1)S(1)}, u32[]{:S(2)}, u32[]{:S(2)}) collective-permute-start(bf16[8,304,128]{2,1,0:T(8,128)(2,1)} %get-tuple-element.30), channel_id=1, source_target_pairs={{0,1},{1,0},{2,3},{3,2},{4,5},{5,4},{6,7},{7,6},{8,9},{9,8},{10,11... | collective-permute-start | bytes 1867784 | tf_op jit(solution)/shard_map/ppermute | solution.py:274
  25.3 17.5 %collective-permute-start.4 = (bf16[4,600,128]{2,1,0:T(8,128)(2,1)S(1)}, bf16[4,600,128]{2,1,0:T(8,128)(2,1)S(1)}, u32[]{:S(2)}, u32[]{:S(2)}) collective-permute-start(bf16[4,600,128]{2,1,0:T(8,128)(2,1)S(1)} %pad_maximum_fusion), channel_id=1, source_target_pairs={{0,2},{1,3},{2,0},{3,1},{4,6},{5,7},{6,4},{7,5},{8,10},{9,11},{10,... | collective-permute-start | bytes 1843208 | tf_op jit(solution)/shard_map/ppermute | solution.py:274
  26.9 1.3 %copy-start.1 = (f32[8,304,128]{2,1,0:T(8,128)S(1)}, f32[8,304,128]{2,1,0:T(8,128)}, u32[]{:S(2)}) copy-start(f32[8,304,128]{2,1,0:T(8,128)} %get-tuple-element.29) | copy-start | bytes 3735556
  27.1 8.7 %collective-permute-start.9 = (bf16[2,2,296,128]{3,2,0,1:T(8,128)(2,1)S(1)}, bf16[2,2,296,128]{3,2,0,1:T(8,128)(2,1)S(1)}, u32[]{:S(2)}, u32[]{:S(2)}) collective-permute-start(bf16[2,2,296,128]{3,2,0,1:T(8,128)(2,1)S(1)} %fusion.1), channel_id=1, source_target_pairs={{0,4},{1,5},{2,6},{3,7},{4,0},{5,1},{6,2},{7,3},{8,12},{9,13},{10,... | collective-permute-start | bytes 909320 | tf_op jit(solution)/shard_map/ppermute | solution.py:274
  28.4 14.1 %collective-permute-start.6 = (bf16[2,2,304,128]{3,2,0,1:T(8,128)(2,1)S(1)}, bf16[2,2,304,128]{3,2,0,1:T(8,128)(2,1)S(1)}, u32[]{:S(2)}, u32[]{:S(2)}) collective-permute-start(bf16[2,2,304,128]{3,2,0,1:T(8,128)(2,1)S(1)} %fusion), channel_id=1, source_target_pairs={{0,4},{1,5},{2,6},{3,7},{4,0},{5,1},{6,2},{7,3},{8,12},{9,13},{10,... | collective-permute-start | bytes 933896 | tf_op jit(solution)/shard_map/ppermute | solution.py:274
  35.9 8.4 %collective-permute-start.10 = (bf16[2,296,128]{2,1,0:T(8,128)(2,1)S(1)}, bf16[2,296,128]{2,1,0:T(8,128)(2,1)S(1)}, u32[]{:S(2)}, u32[]{:S(2)}) collective-permute-start(bf16[2,296,128]{2,1,0:T(8,128)(2,1)S(1)} %fusion.3), channel_id=1, source_target_pairs={{0,2},{1,3},{2,0},{3,1},{4,6},{5,7},{6,4},{7,5},{8,10},{9,11},{10,... | collective-permute-start | bytes 454664 | tf_op jit(solution)/shard_map/ppermute | solution.py:274
  42.6 4.9 %collective-permute-start.13 = (bf16[2,304,128]{2,1,0:T(8,128)(2,1)S(1)}, bf16[2,304,128]{2,1,0:T(8,128)(2,1)S(1)}, u32[]{:S(2)}, u32[]{:S(2)}) collective-permute-start(bf16[2,304,128]{2,1,0:T(8,128)(2,1)S(1)} %fusion.2), channel_id=1, source_target_pairs={{0,2},{1,3},{2,0},{3,1},{4,6},{5,7},{6,4},{7,5},{8,10},{9,11},{10,... | collective-permute-start | bytes 466952 | tf_op jit(solution)/shard_map/ppermute | solution.py:274
  43.0 11.8 %copy-start = (bf16[8,600,128]{2,1,0:T(8,128)(2,1)}, bf16[8,600,128]{2,1,0:T(8,128)(2,1)S(1)}, u32[]{:S(2)}) copy-start(bf16[8,600,128]{2,1,0:T(8,128)(2,1)S(1)} %constant_dynamic-update-slice_fusion.near) | copy-start | bytes 3686404
  43.0 13.1 %collective-permute-start.7 = (bf16[8,600,128]{2,1,0:T(8,128)(2,1)S(1)}, bf16[8,600,128]{2,1,0:T(8,128)(2,1)S(1)}, u32[]{:S(2)}, u32[]{:S(2)}) collective-permute-start(bf16[8,600,128]{2,1,0:T(8,128)(2,1)S(1)} %constant_dynamic-update-slice_fusion.near), channel_id=1, source_target_pairs={{0,1},{1,0},{2,3},{3,2},{4,5},{5,4},{6,7},{7,6},{8,9},{9,8},{10,11... | collective-permute-start | bytes 3686408 | tf_op jit(solution)/shard_map/ppermute | solution.py:274
  44.4 8.1 %collective-permute-start.15 = (bf16[296,128]{1,0:T(8,128)(2,1)S(1)}, bf16[296,128]{1,0:T(8,128)(2,1)S(1)}, u32[]{:S(2)}, u32[]{:S(2)}) collective-permute-start(bf16[296,128]{1,0:T(8,128)(2,1)S(1)} %fusion.5), channel_id=1, source_target_pairs={{0,8},{1,9},{2,10},{3,11},{4,12},{5,13},{6,14},{7,15},{8,0},{9,1},... | collective-permute-start | bytes 227336 | tf_op jit(solution)/shard_map/ppermute | solution.py:274
  47.5 7.2 %collective-permute-start.14 = (bf16[304,128]{1,0:T(8,128)(2,1)S(1)}, bf16[304,128]{1,0:T(8,128)(2,1)S(1)}, u32[]{:S(2)}, u32[]{:S(2)}) collective-permute-start(bf16[304,128]{1,0:T(8,128)(2,1)S(1)} %fusion.4), channel_id=1, source_target_pairs={{0,8},{1,9},{2,10},{3,11},{4,12},{5,13},{6,14},{7,15},{8,0},{9,1},... | collective-permute-start | bytes 233480 | tf_op jit(solution)/shard_map/ppermute | solution.py:274
  54.8 13.1 %collective-permute-start.16 = (bf16[600,128]{1,0:T(8,128)(2,1)S(1)}, bf16[600,128]{1,0:T(8,128)(2,1)S(1)}, u32[]{:S(2)}, u32[]{:S(2)}) collective-permute-start(bf16[600,128]{1,0:T(8,128)(2,1)S(1)} %fusion.6), channel_id=1, source_target_pairs={{0,16},{16,0},{1,17},{17,1},{2,18},{18,2},{3,19},{19,3},{4,20},{20... | collective-permute-start | bytes 460808 | tf_op jit(solution)/shard_map/ppermute | solution.py:388
  56.1 1.1 %copy-start.2 = (bf16[8,600,128]{2,1,0:T(8,128)(2,1)}, bf16[8,600,128]{2,1,0:T(8,128)(2,1)S(1)}, u32[]{:S(2)}) copy-start(bf16[8,600,128]{2,1,0:T(8,128)(2,1)S(1)} %collective-permute-done.7.far) | copy-start | bytes 3686404
  63.5 9.6 %collective-permute-start.11 = (bf16[25,8,128]{2,1,0:T(8,128)(2,1)}, bf16[25,8,128]{2,1,0:T(8,128)(2,1)S(1)}, u32[]{:S(2)}, u32[]{:S(2)}) collective-permute-start(bf16[25,8,128]{2,1,0:T(8,128)(2,1)} %get-tuple-element.36), channel_id=1, source_target_pairs={{0,1},{1,0},{2,3},{3,2},{4,5},{5,4},{6,7},{7,6},{8,9},{9,8},{10,11... | collective-permute-start | bytes 153608 | tf_op jit(solution)/shard_map/ppermute | solution.py:274
  64.8 8.4 %collective-permute-start.12 = (bf16[25,8,128]{2,1,0:T(8,128)(2,1)}, bf16[25,8,128]{2,1,0:T(8,128)(2,1)S(1)}, u32[]{:S(2)}, u32[]{:S(2)}) collective-permute-start(bf16[25,8,128]{2,1,0:T(8,128)(2,1)} %get-tuple-element.37), channel_id=1, source_target_pairs={{1,2},{3,4},{5,6},{7,8},{9,10},{11,12},{13,14},{2,1},{4,3},{6,5},{... | collective-permute-start | bytes 153608 | tf_op jit(solution)/shard_map/ppermute | solution.py:280
  67.8 5.3 %copy-start.5 = (f32[25,8,128]{2,1,0:T(8,128)S(1)}, f32[25,8,128]{2,1,0:T(8,128)}, u32[]{:S(2)}) copy-start(f32[25,8,128]{2,1,0:T(8,128)} %get-tuple-element.35) | copy-start | bytes 307204
  67.8 0.7 copy-start.4

commit v2 on v1

v2 whole, which is shorter than its diff:
```python
import functools
import itertools

import jax
import jax.numpy as jnp
from jax import lax
from jax.experimental import pallas as pl
from jax.experimental.pallas import tpu as pltpu
from jax.sharding import PartitionSpec as P

BF16 = jnp.bfloat16
F32 = jnp.float32
LANES = 128
GROUPS = ((0, 5), (5, 9), (9, 13), (13, 16), (16, 19))
FRAME_ROWS = tuple(
    tuple(
        first + degree - order
        for first, order in ((0, 0), (5, 1), (9, 1), (13, 2), (16, 2))
        if degree >= order
    )
    for degree in range(5)
)
NODE_COLS = tuple(tuple(range(l * l, (l + 1) * (l + 1))) for l in range(5))
WEIGHTS = (5, 4, 4, 3, 3)


def first_rows():
    rows, out = 0, []
    for group_rows in WEIGHTS:
        out.append(rows)
        rows += group_rows * group_rows * LANES
    return out


def place(row):
    if row < 5:
        return 0, row, 0
    if row < 13:
        return 1, (row - 5) % 4, (row - 5) // 4
    return 2, (row - 13) % 3, (row - 13) // 3


def for_chunks(channels, edges, size, body):
    for edge_first in range(0, edges, LANES):

        def step(turn, unused, edge_first=edge_first):
            body(pl.multiple_of(turn * size, size), edge_first)
            return unused

        lax.fori_loop(0, channels // size, step, 0)


def nt(left, right):
    return lax.dot_general(left, right, (((1,), (1,)), ((), ())), preferred_element_type=F32)


def tn(left, right):
    return lax.dot_general(left, right, (((0,), (0,)), ((), ())), preferred_element_type=F32)


def one_hot(count, wanted):
    edges = wanted.shape[1]
    hit = lax.broadcasted_iota(jnp.int32, (count, edges), 0) == wanted
    return hit.astype(F32).astype(BF16)


def near_pick(source, atoms):
    index = lax.axis_index("graph")
    shard = lax.div(source[...], atoms)
    slot = jnp.where(shard == index, 1, jnp.where(shard == (index ^ 1), 0, 2))
    return one_hot(3 * atoms, (slot - shard) * atoms + source[...])


def gather(pieces, pick, picked):
    for coef in range(picked.shape[0]):
        parts = [piece[coef].astype(F32) for piece in pieces]
        block = parts[0] if len(parts) == 1 else jnp.concatenate(parts, axis=0)
        picked[coef] = tn(block.astype(BF16), pick)


def rotate(rot, picked, emit):
    channels, edges = picked.shape[1:]

    def body(at, edge_first):
        lanes = slice(edge_first, edge_first + LANES)
        for rows, cols in zip(FRAME_ROWS, NODE_COLS):
            totals = [None] * len(rows)
            for col in cols:
                value = picked[col, pl.ds(at, 32), lanes]
                for n, row in enumerate(rows):
                    term = rot[col, row : row + 1, lanes] * value
                    totals[n] = term if totals[n] is None else totals[n] + term
            for row, total in zip(rows, totals):
                emit(row, at, edge_first, total)

    for_chunks(channels, edges, 32, body)


def cot_kernel(
    source, target, counts, cot, feats, wigner, radial,
    b0, b1, b2, rot, gate, pick, feats_near,
    source_v, target_v, cot_v, wigner_v, radial_v, sems, picked,
):
    pairs = (
        (target, target_v), (cot, cot_v), (wigner, wigner_v), (radial, radial_v),
        (source, source_v), (feats, feats_near),
    )
    copies = [pltpu.make_async_copy(*pair, sems.at[n]) for n, pair in enumerate(pairs)]
    for copy in copies:
        copy.start()
    atoms, channels = cot.shape[1:]
    edges = target.shape[1]
    copies[0].wait()
    copies[1].wait()
    bmat = (b0, b1, b2)
    live = lax.broadcasted_iota(jnp.int32, (1, edges), 1) < counts[0, 0]
    gather((cot_v,), one_hot(atoms, jnp.where(live, target_v[...], -1)), picked)
    copies[2].wait()
    rot[...] = wigner_v[...].astype(F32)

    def emit(row, at, edge_first, total):
        which, block, half = place(row)
        rows = pl.ds(pl.multiple_of(block * channels + at, 32), 32)
        lanes = slice(half * edges + edge_first, half * edges + edge_first + LANES)
        bmat[which][rows, lanes] = total.astype(BF16)

    rotate(rot, picked, emit)
    for copy in copies[3:]:
        copy.wait()
    gate[...] = radial_v[...].astype(F32).T
    pick[...] = near_pick(source_v, atoms)


def grad_kernel(
    feats_core, feats_own, feats_far, rot, gate, pick, b0, b1, b2,
    keep_a, keep_b, send_a, send_b,
    picked, a0, a1, a2, grad,
):
    channels, edges = gate.shape
    amat = (a0, a1, a2)
    gather((feats_core, feats_own, feats_far), pick[...], picked)

    def emit(row, at, edge_first, total):
        which, block, half = place(row)
        rows = pl.ds(pl.multiple_of(block * channels + at, 32), 32)
        gated = total * gate[pl.ds(at, 32), edge_first : edge_first + LANES]
        lanes = slice(half * edges + edge_first, half * edges + edge_first + LANES)
        amat[which][rows, lanes] = gated.astype(BF16)

    rotate(rot, picked, emit)

    def put(first, blocks, block, product):
        for n in range(product.shape[1] // LANES):
            grad[pl.ds(first + block + n, blocks * LANES, stride=blocks), :] = product[
                :, n * LANES : (n + 1) * LANES
            ]

    firsts = first_rows()
    for order, (left, right) in enumerate(((a0, b0), (a1, b1), (a2, b2))):
        blocks = 5 - order
        first = firsts[max(2 * order - 1, 0)]
        for block in range(0, blocks, 2):
            width = min(2, blocks - block)
            part = right[block * LANES : (block + width) * LANES, :]
            put(first, blocks, block, nt(left[...], part))
            if order:
                product = nt(left[:, :edges], part[:, edges:]) - nt(left[:, edges:], part[:, :edges])
                put(firsts[2 * order], blocks, block, product)
    rows_a, rows_b = keep_a.shape[-2], keep_b.shape[-2]
    rows = rows_a + rows_b
    parity = lax.rem(lax.axis_index("graph"), 2)
    for n, spot in enumerate(spots(keep_a)):
        at = (2 * n + 1 - parity) * rows
        send_a[spot] = grad[pl.ds(at, rows_a), :].astype(BF16)
        send_b[spot] = grad[pl.ds(at + rows_a, rows_b), :].astype(BF16)
        at = (2 * n + parity) * rows
        keep_a[spot] = grad[pl.ds(at, rows_a), :]
        keep_b[spot] = grad[pl.ds(at + rows_a, rows_b), :]


def spots(ref):
    return itertools.product(*(range(n) for n in ref.shape[:-2]))


def halve_kernel(axis, bit, keep, came, stay, away):
    side = (lax.axis_index("graph") >> bit) & 1
    for spot in spots(stay):
        here = (*spot[:axis], side, *spot[axis:])
        there = (*spot[:axis], 1 - side, *spot[axis:])
        at = spot or Ellipsis
        stay[at] = keep[here] + came[here].astype(F32)
        away[at] = (keep[there] + came[there].astype(F32)).astype(BF16)


def finish_kernel(keep, came, share, rounded):
    total = keep[...] + came[...].astype(F32)
    share[...] = total
    rounded[...] = total.astype(BF16)


def backward_kernel(masks, high, *refs):
    pieces, refs = refs[: len(masks)], refs[len(masks) :]
    b0, b1, b2, rot, gate, pick, out_core, out_own, out_far = refs[:9]
    flat, w0, w1r, w1i, w2r, w2i, back, spread = refs[9:]
    coefs, atoms, channels = out_own.shape
    edges = gate.shape[1]
    index = lax.axis_index("graph")
    rows = pieces[0].shape[1]
    for mask, piece in zip(masks, pieces):
        for n in range(2):
            shard = index ^ (mask + n * high)
            flat[pl.ds(shard * rows, rows), :] = piece[n].astype(F32)
    for matrix, blocks, first in zip((w0, w1r, w1i, w2r, w2i), WEIGHTS, first_rows()):
        for block in range(blocks):
            matrix[:, block * LANES : (block + 1) * LANES] = flat[
                pl.ds(first + block, blocks * LANES, stride=blocks), :
            ].astype(BF16)

    dot = functools.partial(jnp.dot, preferred_element_type=F32)
    for row in range(5):
        rows = slice(row * channels, (row + 1) * channels)
        back[row] = dot(w0[rows, :], b0[...]) * gate[...]
    for first, real, imag, both, blocks in ((5, w1r, w1i, b1, 4), (13, w2r, w2i, b2, 3)):
        for block in range(blocks):
            rows = slice(block * channels, (block + 1) * channels)
            straight = dot(real[rows, :], both[...])
            crossed = dot(imag[rows, :], both[...])
            back[first + block] = (straight[:, :edges] + crossed[:, edges:]) * gate[...]
            back[first + blocks + block] = (straight[:, edges:] - crossed[:, :edges]) * gate[...]

    def body(at, edge_first):
        lanes = slice(edge_first, edge_first + LANES)
        for rows, cols in zip(FRAME_ROWS, NODE_COLS):
            totals = [None] * len(cols)
            for row in rows:
                value = back[row, pl.ds(at, 16), lanes]
                for n, col in enumerate(cols):
                    term = rot[col, row : row + 1, lanes] * value
                    totals[n] = term if totals[n] is None else totals[n] + term
            for col, total in zip(cols, totals):
                spread[col, pl.ds(at, 16), lanes] = total.astype(BF16)

    for_chunks(channels, edges, 16, body)
    for col in range(coefs):
        block = nt(pick[...], spread[col])
        out_core[col] = block[:atoms].astype(BF16)
        out_own[col] = block[atoms : 2 * atoms]
        out_far[col] = block[2 * atoms :].astype(BF16)


def expert_kernel(first_row, mixing, own_rows, *refs):
    systems, experts_all = mixing.shape
    others, (out, wide, block, sems) = refs[: systems - 1], refs[-4:]
    experts = out.shape[0]
    rows = own_rows.shape[0]
    position = lax.axis_index("dp")
    for n, other in enumerate(others):
        wide[n] = other[...].astype(F32)
    spot = lax.broadcasted_iota(jnp.int32, (experts, experts_all), 1)
    mine = lax.broadcasted_iota(jnp.int32, (experts, experts_all), 0) + position * experts
    scales = []
    for n in range(systems):
        system = lax.rem(position - n + systems, systems)
        row = mixing[pl.ds(system, 1), :]
        column = jnp.sum(jnp.where(spot == mine, row, 0.0), axis=1, keepdims=True)
        scales.append(jnp.broadcast_to(column, (experts, LANES)))
    chunk = rows // 2
    group = max(g for g in range(1, 9) if chunk % g == 0)
    copies = []
    for part in range(2):

        def step(turn, unused, part=part):
            for n in range(group):
                at = part * chunk + turn * group + n
                total = own_rows[pl.ds(at, 1), :] * scales[0]
                for other in range(systems - 1):
                    total = total + wide[other, pl.ds(at, 1), :] * scales[other + 1]
                block[:, pl.ds(pl.multiple_of(at * LANES, LANES), LANES)] = total
            return unused

        lax.fori_loop(0, chunk // group, step, 0)
        here = slice(part * chunk * LANES, (part + 1) * chunk * LANES)
        there = slice(here.start + first_row * LANES, here.stop + first_row * LANES)
        copy = pltpu.make_async_copy(block.at[:, here], out.at[:, there], sems.at[part])
        copy.start()
        copies.append(copy)
    for copy in copies:
        copy.wait()


def spec(space=pltpu.VMEM):
    return pl.BlockSpec(memory_space=space)


KCOST = 1000


def limit(mebibytes):
    return pltpu.CompilerParams(vmem_limit_bytes=mebibytes * 1024 * 1024)


def cost(flops, size):
    return pl.CostEstimate(flops=flops, bytes_accessed=size, transcendentals=0)


def swap(x, bit):
    size = lax.axis_size("graph")
    return lax.ppermute(x, "graph", [(i, i ^ (1 << bit)) for i in range(size)])


def across(x):
    size = lax.axis_size("graph")
    pairs = [(i, i + 1) for i in range(1, size - 1, 2)]
    return lax.ppermute(x, "graph", pairs + [(j, i) for i, j in pairs])


def in_hbm(x):
    return pltpu.with_memory_space_constraint(x, pltpu.HBM)


def after(x, *others):
    return lax.optimization_barrier((x,) + others)[0]


def on_device(
    node_feats, node_cot, wigner, radial, source_atom, target_index, edge_counts,
    merged_weights, mixing,
):
    atoms, coefs, channels = node_feats.shape[1:]
    edges = source_atom.shape[1]
    size = lax.axis_size("graph")
    bits = size.bit_length() - 1
    shard_rows = merged_weights.shape[1] // LANES
    total_rows = shard_rows * size
    rows_a = (shard_rows // 2 + 7) // 8 * 8
    split = (rows_a, shard_rows - rows_a)

    feats = jnp.transpose(node_feats[0], (1, 0, 2))
    feats_far = across(feats)
    feats_core = swap(feats, 0)
    target, feats_core = lax.optimization_barrier((target_index, feats_core))

    held = merged_weights.reshape(1, shard_rows, LANES)
    came = swap(held, bits - 1)

    hbm = spec(pltpu.HBM)
    picked_scratch = pltpu.VMEM((coefs, channels, edges), F32)
    *bmats, rot, gate, pick, feats_near = pl.pallas_call(
        cot_kernel,
        out_shape=[
            pltpu.VMEM((5 * channels, edges), BF16),
            pltpu.VMEM((4 * channels, 2 * edges), BF16),
            pltpu.VMEM((3 * channels, 2 * edges), BF16),
            pltpu.VMEM((coefs, 19, edges), F32),
            pltpu.VMEM((channels, edges), F32),
            jax.ShapeDtypeStruct((3 * atoms, edges), BF16),
            pltpu.VMEM((coefs, atoms, channels), BF16),
        ],
        in_specs=[hbm, hbm, spec(pltpu.SMEM), hbm, hbm, hbm, hbm],
        out_specs=[spec()] * 7,
        scratch_shapes=[
            pltpu.VMEM((1, edges), jnp.int32),
            pltpu.VMEM((1, edges), jnp.int32),
            pltpu.VMEM((coefs, atoms, channels), BF16),
            pltpu.VMEM((coefs, 19, edges), BF16),
            pltpu.VMEM((edges, channels), BF16),
            pltpu.SemaphoreType.DMA((6,)),
            picked_scratch,
        ],
        compiler_params=limit(12),
        cost_estimate=cost(KCOST, KCOST),
        name="cotangents",
    )(
        in_hbm(source_atom), in_hbm(target), edge_counts,
        in_hbm(jnp.transpose(node_cot[0], (1, 0, 2))), in_hbm(feats),
        in_hbm(jnp.transpose(wigner[0], (1, 0, 2))), in_hbm(radial[0]),
    )

    came = after(came, pick)
    held = jnp.concatenate([held, came], axis=0)
    held, feats_far = lax.optimization_barrier((held, feats_far))
    near, up = bits - 2, bits - 3
    pieces = {0: held, 1 << near: swap(held, near), 1 << up: swap(held, up)}

    keeps_sends = pl.pallas_call(
        grad_kernel,
        out_shape=[
            kind((2,) * (bits - 1) + (rows, LANES), dtype)
            for kind, dtype in ((pltpu.VMEM, F32), (jax.ShapeDtypeStruct, BF16))
            for rows in split
        ],
        in_specs=[spec()] * 9,
        out_specs=[spec()] * 4,
        scratch_shapes=[
            picked_scratch,
            pltpu.VMEM((5 * channels, edges), BF16),
            pltpu.VMEM((4 * channels, 2 * edges), BF16),
            pltpu.VMEM((3 * channels, 2 * edges), BF16),
            pltpu.VMEM((total_rows, LANES), F32),
        ],
        compiler_params=limit(17),
        cost_estimate=cost(KCOST, KCOST),
        name="gradients",
    )(feats_core, feats_near, feats_far, rot, gate, pick, *bmats)
    keeps, sends = keeps_sends[:2], list(keeps_sends[2:])
    *sends, pieces[1 << near], pieces[1 << up] = lax.optimization_barrier(
        (*sends, pieces[1 << near], pieces[1 << up])
    )
    pieces[1 << near | 1 << up] = swap(pieces[1 << near], up)

    low_to_high = list(range(1, bits))
    orders = [low_to_high, low_to_high[1:] + low_to_high[:1]]
    left = [list(reversed(low_to_high)) for _ in orders]

    def halve(turn, keeps, cames):
        stays, aways = [], []
        for part, (keep, came) in enumerate(zip(keeps, cames)):
            bit = orders[part][turn]
            axis = left[part].index(bit)
            left[part].remove(bit)
            shape = (2,) * len(left[part]) + came.shape[-2:]
            stay, away = pl.pallas_call(
                functools.partial(halve_kernel, axis, bit),
                out_shape=[pltpu.VMEM(shape, F32), jax.ShapeDtypeStruct(shape, BF16)],
                in_specs=[spec()] * 2,
                out_specs=[spec()] * 2,
                compiler_params=limit(6),
                cost_estimate=cost(KCOST, KCOST),
                name="halve",
            )(keep, came)
            stays.append(stay)
            aways.append(away)
        return stays, aways

    def exchange(turn, aways):
        return [swap(away, orders[part][turn]) for part, away in enumerate(aways)]

    stays, aways = halve(0, keeps, [swap(send, 0) for send in sends])

    def fan_out(some):
        some = dict(some)
        for bit in reversed(range(up)):
            some.update({mask | 1 << bit: swap(some[mask], bit) for mask in list(some)})
        return some

    last = pieces.pop(1 << near | 1 << up)
    pieces = fan_out(pieces)
    cames = exchange(0, aways)
    for turn in range(1, bits - 1):
        stays, aways = halve(turn, stays, cames)
        masks = list(pieces)
        together = lax.optimization_barrier((*aways, *pieces.values()))
        aways, pieces = together[:2], dict(zip(masks, together[2:]))
        if turn == bits - 2:
            pieces.update(fan_out({1 << near | 1 << up: after(last, *aways)}))
        cames = exchange(turn, aways)
    cames = lax.optimization_barrier(cames)

    systems = lax.axis_size("dp")
    shares, roundeds = [], []
    for stay, came in zip(stays, cames):
        share, rounded = pl.pallas_call(
            finish_kernel,
            out_shape=[pltpu.VMEM(came.shape, F32), jax.ShapeDtypeStruct(came.shape, BF16)],
            in_specs=[spec()] * 2,
            out_specs=[spec()] * 2,
            compiler_params=limit(6),
            cost_estimate=cost(KCOST, KCOST),
            name="finish",
        )(stay, came)
        shares.append(share)
        roundeds.append(rounded)

    masks = list(pieces)
    ready = list(pieces.values())
    grads_core, grads_own, grads_far = pl.pallas_call(
        functools.partial(backward_kernel, masks, 1 << (bits - 1)),
        out_shape=[
            jax.ShapeDtypeStruct((coefs, atoms, channels), kind) for kind in (BF16, F32, BF16)
        ],
        in_specs=[spec()] * (6 + len(masks)),
        out_specs=[spec()] * 3,
        scratch_shapes=[pltpu.VMEM((total_rows, LANES), F32)]
        + [pltpu.VMEM((g * channels, g * channels), BF16) for g in WEIGHTS]
        + [
            pltpu.VMEM((19, channels, edges), F32),
            pltpu.VMEM((coefs, channels, edges), BF16),
        ],
        compiler_params=limit(18),
        cost_estimate=cost(KCOST, KCOST),
        name="backward",
    )(*ready[: len(masks)], *bmats, rot, gate, pick)
    total = grads_own + swap(grads_core, 0).astype(F32) + across(grads_far).astype(F32)
    atom_grads = jnp.transpose(total, (1, 0, 2))[None]

    own_experts = mixing.shape[1] // systems
    expert_part = None
    for first_row, share, rounded in zip((0, rows_a), shares, roundeds):
        others = [
            lax.ppermute(rounded, "dp", [(i, (i + n) % systems) for i in range(systems)])
            for n in range(1, systems)
        ]
        rows = share.shape[0]
        before = [] if expert_part is None else [expert_part]
        expert_part = pl.pallas_call(
            functools.partial(expert_kernel, first_row),
            out_shape=jax.ShapeDtypeStruct((own_experts, shard_rows * LANES), F32),
            in_specs=[spec()] * (1 + systems) + [spec(pl.ANY)] * len(before),
            out_specs=spec(pl.ANY),
            input_output_aliases={1 + systems: 0} if before else {},
            scratch_shapes=[
                pltpu.VMEM((max(systems - 1, 1), rows, LANES), F32),
                pltpu.VMEM((own_experts, rows * LANES), F32),
                pltpu.SemaphoreType.DMA((2,)),
            ],
            compiler_params=limit(4),
            cost_estimate=cost(KCOST, KCOST),
            name="experts",
        )(mixing, share, *others, *before)
    return (atom_grads, expert_part)


def solution(mesh):
    in_specs = (
        P("dp", "graph", None, None),
        P("dp", "graph", None, None),
        P("dp", None, None, "graph"),
        P("dp", "graph", None),
        P("dp", "graph"),
        P("dp", "graph"),
        P("dp", "graph"),
        P("dp", "graph"),
        P(),
    )
    out_specs = (P("dp", "graph", None, None), P("dp", "graph"))
    return jax.shard_map(
        on_device, mesh=mesh, in_specs=in_specs, out_specs=out_specs, check_vma=False
    )
```

time: 74.1 us -> 67.9 us (0.916)
  starting transfers between devices: 21.7 us -> 31.3 us
  Pallas kernels: 22.1 us -> 14.3 us
  waiting for transfers between devices: 21.6 us -> 18 us
  local copies, waits for them, and re-layouts: 3.11 us -> 0.01 us
  other arithmetic: 3.75 us -> 2.51 us
    pallas_call x4 -> x13, Pallas kernels: 22.1 us -> 14.3 us  [the longest x1 3.86 us: on_device(): pl.pallas_call(grad_kernel, out_shape=[kind((2,) * (bits - 1) + (rows, LA...]
    ppermute x14 -> x18, starting transfers between devices: 14.1 us -> 21.8 us  [swap(): return lax.ppermute(x, 'graph', [(i, i ^ 1 << bit) for i in range(size)])]
    ppermute x14 -> x18, waiting for transfers between devices: 21.6 us -> 18 us  [swap(): return lax.ppermute(x, 'graph', [(i, i ^ 1 << bit) for i in range(size)])]
    unnamed x20 -> x2, local copies, waits for them, and re-layouts: 2.83 us -> 0.01 us
    ppermute x2, starting transfers between devices: 6.3 us -> 7.93 us  [across(): return lax.ppermute(x, 'graph', pairs + [(j, i) for i, j in pairs])]
    ppermute x1 -> x2, starting transfers between devices: 1.27 us -> 1.6 us  [on_device(): lax.ppermute(rounded, 'dp', [(i, (i + n) % systems) for i in range(system...]
  transfers between devices with their start and end apart: 17 -> 22, of which waited for: 7 -> 7; matrix products, arithmetic and copies ran while one was open for 2% -> 0% of each run, Pallas kernels for 30% -> 21%
where the time goes in v2:
time: 67.9 us; the launch traced here: 67.7 us
  starting transfers between devices  31.3 us (46%)
  waiting for transfers between devices  18 us (27%)
  Pallas kernels  14.3 us (21%)
  other arithmetic  2.51 us (4%)
  between operations  1.48 us (2%)
    ppermute x18, starting transfers between devices, swap(): return lax.ppermute(x, 'graph', [(i, i ^ 1 << bit) for i in range(size)])  21.8 us
    ppermute x18, waiting for transfers between devices, swap(): return lax.ppermute(x, 'graph', [(i, i ^ 1 << bit) for i in range(size)])  18 us
    ppermute x2, starting transfers between devices, across(): return lax.ppermute(x, 'graph', pairs + [(j, i) for i, j in pairs])  7.93 us
    pallas_call x1, Pallas kernels, on_device(): pl.pallas_call(grad_kernel, out_shape=[kind((2,) * (bits - 1) + (rows, LA...  3.86 us
    pallas_call x2, Pallas kernels, on_device(): pl.pallas_call(functools.partial(expert_kernel, first_row), out_shape=jax...  3.74 us
    pallas_call x1, Pallas kernels, on_device(): pl.pallas_call(functools.partial(backward_kernel, masks, 1 << bits - 1),...  3.53 us
    pallas_call x1, Pallas kernels, on_device(): pl.pallas_call(cot_kernel, out_shape=[pltpu.VMEM((5 * channels, edges), B...  2.7 us
    unnamed x1, other arithmetic  1.81 us
  transfers between devices with their start and end apart: 22, of which 7 were waited for; matrix products, arithmetic and copies ran while one was open for 0% of the time, Pallas kernels for 21%

profile of v2, /device:TPU:1, one launch (start us, length us, event | category | flops | bytes accessed | tf_op | source)
XLA Modules:
  0.0 67.7 jit_solution(15281654845515264263)
XLA Ops:
  0.6 1.8 %reduce = bf16[76800]{0:T(1024)(128)(2,1)S(1)} reduce(bf16[1,76800]{1,0:T(2,128)(2,1)} %param.16, bf16[]{:T(256)} %constant.8), dimensions={0}, to_apply=%param.16.reduce_sub_computation | reduce | bytes 307202 | tf_op args[7]
  2.4 3.2 %collective-permute-start.1 = (bf16[1,600,128]{2,1,0:T(8,128)(2,1)S(1)}, bf16[1,600,128]{2,1,0:T(8,128)(2,1)S(1)}, u32[]{:S(2)}, u32[]{:S(2)}) collective-permute-start(bf16[1,600,128]{2,1,0:T(8,128)(2,1)S(1)} %bitcast.15), channel_id=1, source_target_pairs={{0,8},{1,9},{2,10},{3,11},{4,12},{5,13},{6,14},{7,15},{8,0},{9,1},... | collective-permute-start | bytes 460808 | tf_op jit(solution)/shard_map/ppermute | solution.py:308
  5.7 1.0 %collective-permute-start = (bf16[25,8,128]{2,1,0:T(8,128)(2,1)}, bf16[25,8,128]{2,1,0:T(8,128)(2,1)S(1)}, u32[]{:S(2)}, u32[]{:S(2)}) collective-permute-start(bf16[25,8,128]{2,1,0:T(8,128)(2,1)} %bitcast.20), channel_id=1, source_target_pairs={{0,1},{1,0},{2,3},{3,2},{4,5},{5,4},{6,7},{7,6},{8,9},{9,8},{10,11... | collective-permute-start | bytes 153608 | tf_op jit(solution)/shard_map/ppermute | solution.py:308
  6.6 3.0 %collective-permute-start.2 = (bf16[25,8,128]{2,1,0:T(8,128)(2,1)}, bf16[25,8,128]{2,1,0:T(8,128)(2,1)S(1)}, u32[]{:S(2)}, u32[]{:S(2)}) collective-permute-start(bf16[25,8,128]{2,1,0:T(8,128)(2,1)} %bitcast.21), channel_id=1, source_target_pairs={{1,2},{3,4},{5,6},{7,8},{9,10},{11,12},{13,14},{2,1},{4,3},{6,5},{... | collective-permute-start | bytes 153608 | tf_op jit(solution)/shard_map/ppermute | solution.py:314
  10.3 0.0 collective-permute-done.feats_core
  10.3 2.7 %cotangents.1 = (bf16[640,256]{1,0:T(8,128)(2,1)S(1)}, bf16[512,512]{1,0:T(8,128)(2,1)S(1)}, bf16[384,512]{1,0:T(8,128)(2,1)S(1)}, f32[25,19,256]{2,1,0:T(8,128)...) custom-call(s32[1,256]{1,0:T(1,128)} %source.1, s32[1,256]{1,0:T(1,128)} %target, ...), custom_call_target="tpu_custom_call" | custom-call | flops 1000 | bytes 1000 | tf_op jit(solution)/shard_map/cotangents/pallas_call | solution.py:348
  13.1 0.0 collective-permute-done.2.feats_far
  13.1 1.8 %collective-permute-start.4 = (bf16[2,600,128]{2,1,0:T(8,128)(2,1)S(1)}, bf16[2,600,128]{2,1,0:T(8,128)(2,1)S(1)}, u32[]{:S(2)}, u32[]{:S(2)}) collective-permute-start(bf16[2,600,128]{2,1,0:T(8,128)(2,1)S(1)} %pad_maximum_fusion.refs_0_), channel_id=1, source_target_pairs={{0,2},{1,3},{2,0},{3,1},{4,6},{5,7},{6,4},{7,5},{8,10},{9,11},{10,... | collective-permute-start | bytes 921608 | tf_op jit(solution)/shard_map/ppermute | solution.py:308
  14.9 0.9 %collective-permute-start.3 = (bf16[2,600,128]{2,1,0:T(8,128)(2,1)S(1)}, bf16[2,600,128]{2,1,0:T(8,128)(2,1)S(1)}, u32[]{:S(2)}, u32[]{:S(2)}) collective-permute-start(bf16[2,600,128]{2,1,0:T(8,128)(2,1)S(1)} %pad_maximum_fusion.refs_0_), channel_id=1, source_target_pairs={{0,4},{1,5},{2,6},{3,7},{4,0},{5,1},{6,2},{7,3},{8,12},{9,13},{10,... | collective-permute-start | bytes 921608 | tf_op jit(solution)/shard_map/ppermute | solution.py:308
  15.8 3.9 %gradients.1 = (f32[2,2,2,304,128]{4,3,2,1,0:T(8,128)S(1)}, f32[2,2,2,296,128]{4,3,2,1,0:T(8,128)S(1)}, bf16[2,2,2,304,128]{4,3,2,1,0:T(8,128)(2,1)S(1)}, bf16[2,2,2,296,128]{4,3,2,1,0:T(8,128)(2,1)S(1)}) custom-call(bf16[25,8,128]{2,1,0:T(8,128)(2,1)S(1)} %collective-permute-done.feats_core, bf16[25,8,128]{2,1,0:T(8,128)(2,1)S(1)} %get-tuple-element.62.feats_own, ...), custom_call_target="tpu_custom_call" | custom-call | flops 1000 | bytes 1000 | tf_op jit(solution)/shard_map/gradients/pallas_call | solution.py:385
  19.7 2.0 %collective-permute-done.4.refs_2_ = bf16[2,600,128]{2,1,0:T(8,128)(2,1)S(1)} collective-permute-done((bf16[2,600,128]{2,1,0:T(8,128)(2,1)S(1)}, bf16[2,600,128]{2,1,0:T(8,128)(2,1)S(1)}, u32[]{:S(2)}, u32[]{:S(2)}) %collective-permute-start.4) | collective-permute-done | bytes 307232 | tf_op jit(solution)/shard_map/ppermute | solution.py:308
  21.7 1.4 %collective-permute-done.3.refs_1_ = bf16[2,600,128]{2,1,0:T(8,128)(2,1)S(1)} collective-permute-done((bf16[2,600,128]{2,1,0:T(8,128)(2,1)S(1)}, bf16[2,600,128]{2,1,0:T(8,128)(2,1)S(1)}, u32[]{:S(2)}, u32[]{:S(2)}) %collective-permute-start.3) | collective-permute-done | bytes 307232 | tf_op jit(solution)/shard_map/ppermute | solution.py:308
  23.1 1.5 %collective-permute-start.7 = (bf16[2,2,2,296,128]{4,3,2,1,0:T(8,128)(2,1)S(1)}, bf16[2,2,2,296,128]{4,3,2,1,0:T(8,128)(2,1)S(1)}, u32[]{:S(2)}, u32[]{:S(2)}) collective-permute-start(bf16[2,2,2,296,128]{4,3,2,1,0:T(8,128)(2,1)S(1)} %get-tuple-element.81), channel_id=1, source_target_pairs={{0,1},{1,0},{2,3},{3,2},{4,5},{5,4},{6,7},{7,6},{8,9},{9,8},{10,11... | collective-permute-start | bytes 1818632 | tf_op jit(solution)/shard_map/ppermute | solution.py:308
  24.6 0.0 collective-permute-start.5
  24.6 1.7 %collective-permute-done.7.came = bf16[2,2,2,296,128]{4,3,2,1,0:T(8,128)(2,1)S(1)} collective-permute-done((bf16[2,2,2,296,128]{4,3,2,1,0:T(8,128)(2,1)S(1)}, bf16[2,2,2,296,128]{4,3,2,1,0:T(8,128)(2,1)S(1)}, u32[]{:S(2)}, u32[]{:S(2)}) %collective-permute-start.7) | collective-permute-done | bytes 606240 | tf_op jit(solution)/shard_map/ppermute | solution.py:308
  26.3 0.1 halve.8
  26.4 0.0 copy-start
  26.4 1.0 %collective-permute-start.8 = (bf16[2,2,296,128]{3,2,1,0:T(8,128)(2,1)S(1)}, bf16[2,2,296,128]{3,2,1,0:T(8,128)(2,1)S(1)}, u32[]{:S(2)}, u32[]{:S(2)}) collective-permute-start(bf16[2,2,296,128]{3,2,1,0:T(8,128)(2,1)S(1)} %get-tuple-element.83), channel_id=1, source_target_pairs={{0,4},{1,5},{2,6},{3,7},{4,0},{5,1},{6,2},{7,3},{8,12},{9,13},{10,... | collective-permute-start | bytes 909320 | tf_op jit(solution)/shard_map/ppermute | solution.py:308
  27.4 0.1 halve.6
  27.5 0.1 collective-permute-start.6
  27.6 0.9 %collective-permute-start.9 = (bf16[2,600,128]{2,1,0:T(8,128)(2,1)S(1)}, bf16[2,600,128]{2,1,0:T(8,128)(2,1)S(1)}, u32[]{:S(2)}, u32[]{:S(2)}) collective-permute-start(bf16[2,600,128]{2,1,0:T(8,128)(2,1)S(1)} %pad_maximum_fusion.refs_0_), channel_id=1, source_target_pairs={{0,1},{1,0},{2,3},{3,2},{4,5},{5,4},{6,7},{7,6},{8,9},{9,8},{10,11... | collective-permute-start | bytes 921608 | tf_op jit(solution)/shard_map/ppermute | solution.py:308
  28.6 0.0 collective-permute-start.11
  28.6 0.5 collective-permute-start.10
  29.1 5.8 %collective-permute-done.8.came = bf16[2,2,296,128]{3,2,1,0:T(8,128)(2,1)S(1)} collective-permute-done((bf16[2,2,296,128]{3,2,1,0:T(8,128)(2,1)S(1)}, bf16[2,2,296,128]{3,2,1,0:T(8,128)(2,1)S(1)}, u32[]{:S(2)}, u32[]{:S(2)}) %collective-permute-start.8) | collective-permute-done | bytes 303136 | tf_op jit(solution)/shard_map/ppermute | solution.py:308
  34.9 0.0 collective-permute-start.14
  34.9 0.1 halve.9
  34.9 0.9 %collective-permute-done.6.came = bf16[2,2,304,128]{3,2,1,0:T(8,128)(2,1)S(1)} collective-permute-done((bf16[2,2,304,128]{3,2,1,0:T(8,128)(2,1)S(1)}, bf16[2,2,304,128]{3,2,1,0:T(8,128)(2,1)S(1)}, u32[]{:S(2)}, u32[]{:S(2)}) %collective-permute-start.6) | collective-permute-done | bytes 311328 | tf_op jit(solution)/shard_map/ppermute | solution.py:308
  35.8 0.1 halve.7
  35.9 0.0 collective-permute-done.9.refs_3_
  35.9 0.0 collective-permute-done.10.refs_4_
  35.9 0.9 %collective-permute-start.12 = (bf16[2,304,128]{2,1,0:T(8,128)(2,1)S(1)}, bf16[2,304,128]{2,1,0:T(8,128)(2,1)S(1)}, u32[]{:S(2)}, u32[]{:S(2)}) collective-permute-start(bf16[2,304,128]{2,1,0:T(8,128)(2,1)S(1)} %get-tuple-element.87), channel_id=1, source_target_pairs={{0,4},{1,5},{2,6},{3,7},{4,0},{5,1},{6,2},{7,3},{8,12},{9,13},{10,... | collective-permute-start | bytes 466952 | tf_op jit(solution)/shard_map/ppermute | solution.py:308
  36.8 2.6 %collective-permute-start.13 = (bf16[2,296,128]{2,1,0:T(8,128)(2,1)S(1)}, bf16[2,296,128]{2,1,0:T(8,128)(2,1)S(1)}, u32[]{:S(2)}, u32[]{:S(2)}) collective-permute-start(bf16[2,296,128]{2,1,0:T(8,128)(2,1)S(1)} %get-tuple-element.90), channel_id=1, source_target_pairs={{0,8},{1,9},{2,10},{3,11},{4,12},{5,13},{6,14},{7,15},{8,0},{9,1},... | collective-permute-start | bytes 454664 | tf_op jit(solution)/shard_map/ppermute | solution.py:308
  39.4 3.5 %collective-permute-done.13.came = bf16[2,296,128]{2,1,0:T(8,128)(2,1)S(1)} collective-permute-done((bf16[2,296,128]{2,1,0:T(8,128)(2,1)S(1)}, bf16[2,296,128]{2,1,0:T(8,128)(2,1)S(1)}, u32[]{:S(2)}, u32[]{:S(2)}) %collective-permute-start.13) | collective-permute-done | bytes 151584 | tf_op jit(solution)/shard_map/ppermute | solution.py:308
  43.0 0.0 collective-permute-done.12.came
  43.0 3.3 %collective-permute-start.15 = (bf16[2,600,128]{2,1,0:T(8,128)(2,1)S(1)}, bf16[2,600,128]{2,1,0:T(8,128)(2,1)S(1)}, u32[]{:S(2)}, u32[]{:S(2)}) collective-permute-start(bf16[2,600,128]{2,1,0:T(8,128)(2,1)S(1)} %collective-permute-done.14.refs_6_), channel_id=1, source_target_pairs={{0,1},{1,0},{2,3},{3,2},{4,5},{5,4},{6,7},{7,6},{8,9},{9,8},{10,11... | collective-permute-start | bytes 921608 | tf_op jit(solution)/shard_map/ppermute | solution.py:308
  46.3 1.4 %collective-permute-start.18 = (bf16[304,128]{1,0:T(8,128)(2,1)S(1)}, bf16[304,128]{1,0:T(8,128)(2,1)S(1)}, u32[]{:S(2)}, u32[]{:S(2)}) collective-permute-start(bf16[304,128]{1,0:T(8,128)(2,1)S(1)} %get-tuple-element.104), channel_id=1, source_target_pairs={{0,8},{1,9},{2,10},{3,11},{4,12},{5,13},{6,14},{7,15},{8,0},{9,1},... | collective-permute-start | bytes 233480 | tf_op jit(solution)/shard_map/ppermute | solution.py:308
  47.7 0.8 %collective-permute-start.19 = (bf16[296,128]{1,0:T(8,128)(2,1)S(1)}, bf16[296,128]{1,0:T(8,128)(2,1)S(1)}, u32[]{:S(2)}, u32[]{:S(2)}) collective-permute-start(bf16[296,128]{1,0:T(8,128)(2,1)S(1)} %get-tuple-element.105), channel_id=1, source_target_pairs={{0,2},{1,3},{2,0},{3,1},{4,6},{5,7},{6,4},{7,5},{8,10},{9,11},{10,... | collective-permute-start | bytes 227336 | tf_op jit(solution)/shard_map/ppermute | solution.py:308
  48.5 2.8 %collective-permute-done.19.came = bf16[296,128]{1,0:T(8,128)(2,1)S(1)} collective-permute-done((bf16[296,128]{1,0:T(8,128)(2,1)S(1)}, bf16[296,128]{1,0:T(8,128)(2,1)S(1)}, u32[]{:S(2)}, u32[]{:S(2)}) %collective-permute-start.19) | collective-permute-done | bytes 75808 | tf_op jit(solution)/shard_map/ppermute | solution.py:308
  51.3 1.3 %collective-permute-start.21 = (bf16[304,128]{1,0:T(8,128)(2,1)S(1)}, bf16[304,128]{1,0:T(8,128)(2,1)S(1)}, u32[]{:S(2)}, u32[]{:S(2)}) collective-permute-start(bf16[304,128]{1,0:T(8,128)(2,1)S(1)} %get-tuple-element.117), channel_id=1, source_target_pairs={{0,16},{16,0},{1,17},{17,1},{2,18},{18,2},{3,19},{19,3},{4,20},{20... | collective-permute-start | bytes 233480 | tf_op jit(solution)/shard_map/ppermute | solution.py:500
  52.6 0.3 collective-permute-start.20
  53.0 3.5 %backward.1 = (bf16[25,8,128]{2,1,0:T(8,128)(2,1)S(1)}, f32[25,8,128]{2,1,0:T(8,128)S(1)}, bf16[25,8,128]{2,1,0:T(8,128)(2,1)S(1)}) custom-call(bf16[2,600,128]{2,1,0:T(8,128)(2,1)S(1)} %pad_maximum_fusion.refs_0_, bf16[2,600,128]{2,1,0:T(8,128)(2,1)S(1)} %collective-permute-done.3.refs_1_, bf16[2,600,128]{2,1,0:T(8,128)(2,1)S(1)} %collective-permute-done.4.refs_2_, ...), custom_call_target="tpu_custom_call" | custom-call | flops 1000 | bytes 1000 | tf_op jit(solution)/shard_map/backward/pallas_call | solution.py:476
  56.5 1.8 %collective-permute-start.16 = (bf16[25,8,128]{2,1,0:T(8,128)(2,1)S(1)}, bf16[25,8,128]{2,1,0:T(8,128)(2,1)S(1)}, u32[]{:S(2)}, u32[]{:S(2)}) collective-permute-start(bf16[25,8,128]{2,1,0:T(8,128)(2,1)S(1)} %get-tuple-element.108), channel_id=1, source_target_pairs={{0,1},{1,0},{2,3},{3,2},{4,5},{5,4},{6,7},{7,6},{8,9},{9,8},{10,11... | collective-permute-start | bytes 153608 | tf_op jit(solution)/shard_map/ppermute | solution.py:308
  58.3 4.9 %collective-permute-start.17 = (bf16[25,8,128]{2,1,0:T(8,128)(2,1)S(1)}, bf16[25,8,128]{2,1,0:T(8,128)(2,1)S(1)}, u32[]{:S(2)}, u32[]{:S(2)}) collective-permute-start(bf16[25,8,128]{2,1,0:T(8,128)(2,1)S(1)} %get-tuple-element.109), channel_id=1, source_target_pairs={{1,2},{3,4},{5,6},{7,8},{9,10},{11,12},{13,14},{2,1},{4,3},{6,5},{... | collective-permute-start | bytes 153608 | tf_op jit(solution)/shard_map/ppermute | solution.py:314
  63.2 0.0 collective-permute-done.21.refs_0_
  63.2 1.8 %experts.2.refs_1_ = f32[16,76800]{1,0:T(8,128)} custom-call(f32[2,32]{1,0:T(2,128)S(1)} %copy-done, f32[304,128]{1,0:T(8,128)S(1)} %get-tuple-element.116.own_rows, bf16[304,128]{1,0:T(8,128)(2,1)S(1)} %collective-permute-done.21.refs_0_), custom_call_target="tpu_custom_call" | custom-call | flops 1000 | bytes 1000 | tf_op jit(solution)/shard_map/experts/pallas_call | solution.py:505
  65.0 1.9 %experts.3 = f32[16,76800]{1,0:T(8,128)} custom-call(f32[2,32]{1,0:T(2,128)S(1)} %copy-done, f32[296,128]{1,0:T(8,128)S(1)} %get-tuple-element.112.own_rows, bf16[296,128]{1,0:T(8,128)(2,1)S(1)} %collective-permute-done.20.refs_0_, f32[16,76800]{1,0:T(8,128)} %experts.2.refs_1_), custom_call_target="tpu_custom_call", output_to_operand_aliasing={{}: (3, {})} | custom-call | flops 1000 | bytes 1000 | tf_op jit(solution)/shard_map/experts/pallas_call | solution.py:505
  67.0 0.0 collective-permute-done.16
  67.0 0.7 add_bitcast_fusion
  (14 shorter events, 0.2 us)
Async XLA Ops:
  2.4 10.6 %collective-permute-start.1 = (bf16[1,600,128]{2,1,0:T(8,128)(2,1)S(1)}, bf16[1,600,128]{2,1,0:T(8,128)(2,1)S(1)}, u32[]{:S(2)}, u32[]{:S(2)}) collective-permute-start(bf16[1,600,128]{2,1,0:T(8,128)(2,1)S(1)} %bitcast.15), channel_id=1, source_target_pairs={{0,8},{1,9},{2,10},{3,11},{4,12},{5,13},{6,14},{7,15},{8,0},{9,1},... | collective-permute-start | bytes 460808 | tf_op jit(solution)/shard_map/ppermute | solution.py:308
  5.7 4.6 %collective-permute-start = (bf16[25,8,128]{2,1,0:T(8,128)(2,1)}, bf16[25,8,128]{2,1,0:T(8,128)(2,1)S(1)}, u32[]{:S(2)}, u32[]{:S(2)}) collective-permute-start(bf16[25,8,128]{2,1,0:T(8,128)(2,1)} %bitcast.20), channel_id=1, source_target_pairs={{0,1},{1,0},{2,3},{3,2},{4,5},{5,4},{6,7},{7,6},{8,9},{9,8},{10,11... | collective-permute-start | bytes 153608 | tf_op jit(solution)/shard_map/ppermute | solution.py:308
  6.6 6.5 %collective-permute-start.2 = (bf16[25,8,128]{2,1,0:T(8,128)(2,1)}, bf16[25,8,128]{2,1,0:T(8,128)(2,1)S(1)}, u32[]{:S(2)}, u32[]{:S(2)}) collective-permute-start(bf16[25,8,128]{2,1,0:T(8,128)(2,1)} %bitcast.21), channel_id=1, source_target_pairs={{1,2},{3,4},{5,6},{7,8},{9,10},{11,12},{13,14},{2,1},{4,3},{6,5},{... | collective-permute-start | bytes 153608 | tf_op jit(solution)/shard_map/ppermute | solution.py:314
  13.1 8.6 %collective-permute-start.4 = (bf16[2,600,128]{2,1,0:T(8,128)(2,1)S(1)}, bf16[2,600,128]{2,1,0:T(8,128)(2,1)S(1)}, u32[]{:S(2)}, u32[]{:S(2)}) collective-permute-start(bf16[2,600,128]{2,1,0:T(8,128)(2,1)S(1)} %pad_maximum_fusion.refs_0_), channel_id=1, source_target_pairs={{0,2},{1,3},{2,0},{3,1},{4,6},{5,7},{6,4},{7,5},{8,10},{9,11},{10,... | collective-permute-start | bytes 921608 | tf_op jit(solution)/shard_map/ppermute | solution.py:308
  14.9 8.2 %collective-permute-start.3 = (bf16[2,600,128]{2,1,0:T(8,128)(2,1)S(1)}, bf16[2,600,128]{2,1,0:T(8,128)(2,1)S(1)}, u32[]{:S(2)}, u32[]{:S(2)}) collective-permute-start(bf16[2,600,128]{2,1,0:T(8,128)(2,1)S(1)} %pad_maximum_fusion.refs_0_), channel_id=1, source_target_pairs={{0,4},{1,5},{2,6},{3,7},{4,0},{5,1},{6,2},{7,3},{8,12},{9,13},{10,... | collective-permute-start | bytes 921608 | tf_op jit(solution)/shard_map/ppermute | solution.py:308
  23.1 3.2 %collective-permute-start.7 = (bf16[2,2,2,296,128]{4,3,2,1,0:T(8,128)(2,1)S(1)}, bf16[2,2,2,296,128]{4,3,2,1,0:T(8,128)(2,1)S(1)}, u32[]{:S(2)}, u32[]{:S(2)}) collective-permute-start(bf16[2,2,2,296,128]{4,3,2,1,0:T(8,128)(2,1)S(1)} %get-tuple-element.81), channel_id=1, source_target_pairs={{0,1},{1,0},{2,3},{3,2},{4,5},{5,4},{6,7},{7,6},{8,9},{9,8},{10,11... | collective-permute-start | bytes 1818632 | tf_op jit(solution)/shard_map/ppermute | solution.py:308
  24.6 2.7 %collective-permute-start.5 = (bf16[2,2,2,304,128]{4,3,2,1,0:T(8,128)(2,1)S(1)}, bf16[2,2,2,304,128]{4,3,2,1,0:T(8,128)(2,1)S(1)}, u32[]{:S(2)}, u32[]{:S(2)}) collective-permute-start(bf16[2,2,2,304,128]{4,3,2,1,0:T(8,128)(2,1)S(1)} %get-tuple-element.75), channel_id=1, source_target_pairs={{0,1},{1,0},{2,3},{3,2},{4,5},{5,4},{6,7},{7,6},{8,9},{9,8},{10,11... | collective-permute-start | bytes 1867784 | tf_op jit(solution)/shard_map/ppermute | solution.py:308
  26.4 36.8 %copy-start = (f32[2,32]{1,0:T(2,128)S(1)}, f32[2,32]{1,0:T(2,128)}, u32[]{:S(2)}) copy-start(f32[2,32]{1,0:T(2,128)} %mixing.3) | copy-start | bytes 772
  26.4 8.5 %collective-permute-start.8 = (bf16[2,2,296,128]{3,2,1,0:T(8,128)(2,1)S(1)}, bf16[2,2,296,128]{3,2,1,0:T(8,128)(2,1)S(1)}, u32[]{:S(2)}, u32[]{:S(2)}) collective-permute-start(bf16[2,2,296,128]{3,2,1,0:T(8,128)(2,1)S(1)} %get-tuple-element.83), channel_id=1, source_target_pairs={{0,4},{1,5},{2,6},{3,7},{4,0},{5,1},{6,2},{7,3},{8,12},{9,13},{10,... | collective-permute-start | bytes 909320 | tf_op jit(solution)/shard_map/ppermute | solution.py:308
  27.5 8.3 %collective-permute-start.6 = (bf16[2,2,304,128]{3,2,1,0:T(8,128)(2,1)S(1)}, bf16[2,2,304,128]{3,2,1,0:T(8,128)(2,1)S(1)}, u32[]{:S(2)}, u32[]{:S(2)}) collective-permute-start(bf16[2,2,304,128]{3,2,1,0:T(8,128)(2,1)S(1)} %get-tuple-element.77), channel_id=1, source_target_pairs={{0,2},{1,3},{2,0},{3,1},{4,6},{5,7},{6,4},{7,5},{8,10},{9,11},{10,... | collective-permute-start | bytes 933896 | tf_op jit(solution)/shard_map/ppermute | solution.py:308
  27.6 8.2 %collective-permute-start.9 = (bf16[2,600,128]{2,1,0:T(8,128)(2,1)S(1)}, bf16[2,600,128]{2,1,0:T(8,128)(2,1)S(1)}, u32[]{:S(2)}, u32[]{:S(2)}) collective-permute-start(bf16[2,600,128]{2,1,0:T(8,128)(2,1)S(1)} %pad_maximum_fusion.refs_0_), channel_id=1, source_target_pairs={{0,1},{1,0},{2,3},{3,2},{4,5},{5,4},{6,7},{7,6},{8,9},{9,8},{10,11... | collective-permute-start | bytes 921608 | tf_op jit(solution)/shard_map/ppermute | solution.py:308
  28.6 7.3 %collective-permute-start.11 = (bf16[2,600,128]{2,1,0:T(8,128)(2,1)S(1)}, bf16[2,600,128]{2,1,0:T(8,128)(2,1)S(1)}, u32[]{:S(2)}, u32[]{:S(2)}) collective-permute-start(bf16[2,600,128]{2,1,0:T(8,128)(2,1)S(1)} %collective-permute-done.4.refs_2_), channel_id=1, source_target_pairs={{0,1},{1,0},{2,3},{3,2},{4,5},{5,4},{6,7},{7,6},{8,9},{9,8},{10,11... | collective-permute-start | bytes 921608 | tf_op jit(solution)/shard_map/ppermute | solution.py:308
  28.6 7.3 %collective-permute-start.10 = (bf16[2,600,128]{2,1,0:T(8,128)(2,1)S(1)}, bf16[2,600,128]{2,1,0:T(8,128)(2,1)S(1)}, u32[]{:S(2)}, u32[]{:S(2)}) collective-permute-start(bf16[2,600,128]{2,1,0:T(8,128)(2,1)S(1)} %collective-permute-done.3.refs_1_), channel_id=1, source_target_pairs={{0,1},{1,0},{2,3},{3,2},{4,5},{5,4},{6,7},{7,6},{8,9},{9,8},{10,11... | collective-permute-start | bytes 921608 | tf_op jit(solution)/shard_map/ppermute | solution.py:308
  34.9 8.2 %collective-permute-start.14 = (bf16[2,600,128]{2,1,0:T(8,128)(2,1)S(1)}, bf16[2,600,128]{2,1,0:T(8,128)(2,1)S(1)}, u32[]{:S(2)}, u32[]{:S(2)}) collective-permute-start(bf16[2,600,128]{2,1,0:T(8,128)(2,1)S(1)} %collective-permute-done.3.refs_1_), channel_id=1, source_target_pairs={{0,2},{1,3},{2,0},{3,1},{4,6},{5,7},{6,4},{7,5},{8,10},{9,11},{10,... | collective-permute-start | bytes 921608 | tf_op jit(solution)/shard_map/ppermute | solution.py:308
  35.9 7.1 %collective-permute-start.12 = (bf16[2,304,128]{2,1,0:T(8,128)(2,1)S(1)}, bf16[2,304,128]{2,1,0:T(8,128)(2,1)S(1)}, u32[]{:S(2)}, u32[]{:S(2)}) collective-permute-start(bf16[2,304,128]{2,1,0:T(8,128)(2,1)S(1)} %get-tuple-element.87), channel_id=1, source_target_pairs={{0,4},{1,5},{2,6},{3,7},{4,0},{5,1},{6,2},{7,3},{8,12},{9,13},{10,... | collective-permute-start | bytes 466952 | tf_op jit(solution)/shard_map/ppermute | solution.py:308
  36.8 6.1 %collective-permute-start.13 = (bf16[2,296,128]{2,1,0:T(8,128)(2,1)S(1)}, bf16[2,296,128]{2,1,0:T(8,128)(2,1)S(1)}, u32[]{:S(2)}, u32[]{:S(2)}) collective-permute-start(bf16[2,296,128]{2,1,0:T(8,128)(2,1)S(1)} %get-tuple-element.90), channel_id=1, source_target_pairs={{0,8},{1,9},{2,10},{3,11},{4,12},{5,13},{6,14},{7,15},{8,0},{9,1},... | collective-permute-start | bytes 454664 | tf_op jit(solution)/shard_map/ppermute | solution.py:308
  43.0 9.9 %collective-permute-start.15 = (bf16[2,600,128]{2,1,0:T(8,128)(2,1)S(1)}, bf16[2,600,128]{2,1,0:T(8,128)(2,1)S(1)}, u32[]{:S(2)}, u32[]{:S(2)}) collective-permute-start(bf16[2,600,128]{2,1,0:T(8,128)(2,1)S(1)} %collective-permute-done.14.refs_6_), channel_id=1, source_target_pairs={{0,1},{1,0},{2,3},{3,2},{4,5},{5,4},{6,7},{7,6},{8,9},{9,8},{10,11... | collective-permute-start | bytes 921608 | tf_op jit(solution)/shard_map/ppermute | solution.py:308
  46.3 5.0 %collective-permute-start.18 = (bf16[304,128]{1,0:T(8,128)(2,1)S(1)}, bf16[304,128]{1,0:T(8,128)(2,1)S(1)}, u32[]{:S(2)}, u32[]{:S(2)}) collective-permute-start(bf16[304,128]{1,0:T(8,128)(2,1)S(1)} %get-tuple-element.104), channel_id=1, source_target_pairs={{0,8},{1,9},{2,10},{3,11},{4,12},{5,13},{6,14},{7,15},{8,0},{9,1},... | collective-permute-start | bytes 233480 | tf_op jit(solution)/shard_map/ppermute | solution.py:308
  47.7 3.6 %collective-permute-start.19 = (bf16[296,128]{1,0:T(8,128)(2,1)S(1)}, bf16[296,128]{1,0:T(8,128)(2,1)S(1)}, u32[]{:S(2)}, u32[]{:S(2)}) collective-permute-start(bf16[296,128]{1,0:T(8,128)(2,1)S(1)} %get-tuple-element.105), channel_id=1, source_target_pairs={{0,2},{1,3},{2,0},{3,1},{4,6},{5,7},{6,4},{7,5},{8,10},{9,11},{10,... | collective-permute-start | bytes 227336 | tf_op jit(solution)/shard_map/ppermute | solution.py:308
  51.3 11.9 %collective-permute-start.21 = (bf16[304,128]{1,0:T(8,128)(2,1)S(1)}, bf16[304,128]{1,0:T(8,128)(2,1)S(1)}, u32[]{:S(2)}, u32[]{:S(2)}) collective-permute-start(bf16[304,128]{1,0:T(8,128)(2,1)S(1)} %get-tuple-element.117), channel_id=1, source_target_pairs={{0,16},{16,0},{1,17},{17,1},{2,18},{18,2},{3,19},{19,3},{4,20},{20... | collective-permute-start | bytes 233480 | tf_op jit(solution)/shard_map/ppermute | solution.py:500
  52.6 12.4 %collective-permute-start.20 = (bf16[296,128]{1,0:T(8,128)(2,1)S(1)}, bf16[296,128]{1,0:T(8,128)(2,1)S(1)}, u32[]{:S(2)}, u32[]{:S(2)}) collective-permute-start(bf16[296,128]{1,0:T(8,128)(2,1)S(1)} %get-tuple-element.113), channel_id=1, source_target_pairs={{0,16},{16,0},{1,17},{17,1},{2,18},{18,2},{3,19},{19,3},{4,20},{20... | collective-permute-start | bytes 227336 | tf_op jit(solution)/shard_map/ppermute | solution.py:500
  56.5 10.5 %collective-permute-start.16 = (bf16[25,8,128]{2,1,0:T(8,128)(2,1)S(1)}, bf16[25,8,128]{2,1,0:T(8,128)(2,1)S(1)}, u32[]{:S(2)}, u32[]{:S(2)}) collective-permute-start(bf16[25,8,128]{2,1,0:T(8,128)(2,1)S(1)} %get-tuple-element.108), channel_id=1, source_target_pairs={{0,1},{1,0},{2,3},{3,2},{4,5},{5,4},{6,7},{7,6},{8,9},{9,8},{10,11... | collective-permute-start | bytes 153608 | tf_op jit(solution)/shard_map/ppermute | solution.py:308
  58.3 8.7 %collective-permute-start.17 = (bf16[25,8,128]{2,1,0:T(8,128)(2,1)S(1)}, bf16[25,8,128]{2,1,0:T(8,128)(2,1)S(1)}, u32[]{:S(2)}, u32[]{:S(2)}) collective-permute-start(bf16[25,8,128]{2,1,0:T(8,128)(2,1)S(1)} %get-tuple-element.109), channel_id=1, source_target_pairs={{1,2},{3,4},{5,6},{7,8},{9,10},{11,12},{13,14},{2,1},{4,3},{6,5},{... | collective-permute-start | bytes 153608 | tf_op jit(solution)/shard_map/ppermute | solution.py:314

commit v3 on v2

--- a/solution.py
+++ b/solution.py
@@ -454,22 +454,6 @@
         if turn == bits - 2:
             pieces.update(fan_out({1 << near | 1 << up: after(last, *aways)}))
         cames = exchange(turn, aways)
-    cames = lax.optimization_barrier(cames)
-
-    systems = lax.axis_size("dp")
-    shares, roundeds = [], []
-    for stay, came in zip(stays, cames):
-        share, rounded = pl.pallas_call(
-            finish_kernel,
-            out_shape=[pltpu.VMEM(came.shape, F32), jax.ShapeDtypeStruct(came.shape, BF16)],
-            in_specs=[spec()] * 2,
-            out_specs=[spec()] * 2,
-            compiler_params=limit(6),
-            cost_estimate=cost(KCOST, KCOST),
-            name="finish",
-        )(stay, came)
-        shares.append(share)
-        roundeds.append(rounded)
 
     masks = list(pieces)
     ready = list(pieces.values())
@@ -493,9 +477,25 @@
     total = grads_own + swap(grads_core, 0).astype(F32) + across(grads_far).astype(F32)
     atom_grads = jnp.transpose(total, (1, 0, 2))[None]
 
+    cames = lax.optimization_barrier((*cames, grads_own))[:2]
+    systems = lax.axis_size("dp")
+    shares, roundeds = [], []
+    for stay, came in zip(stays, cames):
+        share, rounded = pl.pallas_call(
+            finish_kernel,
+            out_shape=[pltpu.VMEM(came.shape, F32), jax.ShapeDtypeStruct(came.shape, BF16)],
+            in_specs=[spec()] * 2,
+            out_specs=[spec()] * 2,
+            compiler_params=limit(6),
+            cost_estimate=cost(KCOST, KCOST),
+            name="finish",
+        )(stay, came)
+        shares.append(share)
+        roundeds.append(rounded)
+
     own_experts = mixing.shape[1] // systems
     expert_part = None
-    for first_row, share, rounded in zip((0, rows_a), shares, roundeds):
+    for first_row, share, rounded in reversed(list(zip((0, rows_a), shares, roundeds))):
         others = [
             lax.ppermute(rounded, "dp", [(i, (i + n) % systems) for i in range(systems)])
             for n in range(1, systems)

time: 67.9 us -> 64.3 us (0.947)
  starting transfers between devices: 31.3 us -> 27.9 us
  waiting for transfers between devices: 18 us -> 17.3 us
    ppermute x18, waiting for transfers between devices: 18 us -> 15.2 us  [swap(): return lax.ppermute(x, 'graph', [(i, i ^ 1 << bit) for i in range(size)])]
    ppermute x2, starting transfers between devices: 7.93 us -> 5.67 us  [across(): return lax.ppermute(x, 'graph', pairs + [(j, i) for i, j in pairs])]
    ppermute x2, waiting for transfers between devices: 0.01 us -> 1.39 us  [across(): return lax.ppermute(x, 'graph', pairs + [(j, i) for i, j in pairs])]
    ppermute x18, starting transfers between devices: 21.8 us -> 20.7 us  [swap(): return lax.ppermute(x, 'graph', [(i, i ^ 1 << bit) for i in range(size)])]
  transfers between devices with their start and end apart: 22 -> 22, of which waited for: 7 -> 8; matrix products, arithmetic and copies ran while one was open for 0% -> 1% of each run, Pallas kernels for 21% -> 20%
where the time goes in v3:
time: 64.3 us; the launch traced here: 63.5 us
  starting transfers between devices  27.9 us (43%)
  waiting for transfers between devices  17.3 us (27%)
  Pallas kernels  14.3 us (22%)
  other arithmetic  2.51 us (4%)
  between operations  1.45 us (2%)
    ppermute x18, starting transfers between devices, swap(): return lax.ppermute(x, 'graph', [(i, i ^ 1 << bit) for i in range(size)])  20.7 us
    ppermute x18, waiting for transfers between devices, swap(): return lax.ppermute(x, 'graph', [(i, i ^ 1 << bit) for i in range(size)])  15.2 us
    ppermute x2, starting transfers between devices, across(): return lax.ppermute(x, 'graph', pairs + [(j, i) for i, j in pairs])  5.67 us
    pallas_call x1, Pallas kernels, on_device(): pl.pallas_call(grad_kernel, out_shape=[kind((2,) * (bits - 1) + (rows, LA...  3.86 us
    pallas_call x2, Pallas kernels, on_device(): pl.pallas_call(functools.partial(expert_kernel, first_row), out_shape=jax...  3.74 us
    pallas_call x1, Pallas kernels, on_device(): pl.pallas_call(functools.partial(backward_kernel, masks, 1 << bits - 1),...  3.53 us
    pallas_call x1, Pallas kernels, on_device(): pl.pallas_call(cot_kernel, out_shape=[pltpu.VMEM((5 * channels, edges), B...  2.7 us
    unnamed x1, other arithmetic  1.81 us
  transfers between devices with their start and end apart: 22, of which 8 were waited for; matrix products, arithmetic and copies ran while one was open for 1% of the time, Pallas kernels for 20%

profile of v3, /device:TPU:1, one launch (start us, length us, event | category | flops | bytes accessed | tf_op | source)
XLA Modules:
  0.0 63.5 jit_solution(11492228415476193979)
XLA Ops:
  0.6 1.8 %reduce = bf16[76800]{0:T(1024)(128)(2,1)S(1)} reduce(bf16[1,76800]{1,0:T(2,128)(2,1)} %param.16, bf16[]{:T(256)} %constant.8), dimensions={0}, to_apply=%param.16.reduce_sub_computation | reduce | bytes 307202 | tf_op args[7]
  2.4 3.2 %collective-permute-start.1 = (bf16[1,600,128]{2,1,0:T(8,128)(2,1)S(1)}, bf16[1,600,128]{2,1,0:T(8,128)(2,1)S(1)}, u32[]{:S(2)}, u32[]{:S(2)}) collective-permute-start(bf16[1,600,128]{2,1,0:T(8,128)(2,1)S(1)} %bitcast.15), channel_id=1, source_target_pairs={{0,8},{1,9},{2,10},{3,11},{4,12},{5,13},{6,14},{7,15},{8,0},{9,1},... | collective-permute-start | bytes 460808 | tf_op jit(solution)/shard_map/ppermute | solution.py:308
  5.7 1.0 %collective-permute-start = (bf16[25,8,128]{2,1,0:T(8,128)(2,1)}, bf16[25,8,128]{2,1,0:T(8,128)(2,1)S(1)}, u32[]{:S(2)}, u32[]{:S(2)}) collective-permute-start(bf16[25,8,128]{2,1,0:T(8,128)(2,1)} %bitcast.20), channel_id=1, source_target_pairs={{0,1},{1,0},{2,3},{3,2},{4,5},{5,4},{6,7},{7,6},{8,9},{9,8},{10,11... | collective-permute-start | bytes 153608 | tf_op jit(solution)/shard_map/ppermute | solution.py:308
  6.6 3.0 %collective-permute-start.2 = (bf16[25,8,128]{2,1,0:T(8,128)(2,1)}, bf16[25,8,128]{2,1,0:T(8,128)(2,1)S(1)}, u32[]{:S(2)}, u32[]{:S(2)}) collective-permute-start(bf16[25,8,128]{2,1,0:T(8,128)(2,1)} %bitcast.21), channel_id=1, source_target_pairs={{1,2},{3,4},{5,6},{7,8},{9,10},{11,12},{13,14},{2,1},{4,3},{6,5},{... | collective-permute-start | bytes 153608 | tf_op jit(solution)/shard_map/ppermute | solution.py:314
  10.3 0.0 collective-permute-done.feats_core
  10.3 2.7 %cotangents.1 = (bf16[640,256]{1,0:T(8,128)(2,1)S(1)}, bf16[512,512]{1,0:T(8,128)(2,1)S(1)}, bf16[384,512]{1,0:T(8,128)(2,1)S(1)}, f32[25,19,256]{2,1,0:T(8,128)...) custom-call(s32[1,256]{1,0:T(1,128)} %source.1, s32[1,256]{1,0:T(1,128)} %target, ...), custom_call_target="tpu_custom_call" | custom-call | flops 1000 | bytes 1000 | tf_op jit(solution)/shard_map/cotangents/pallas_call | solution.py:348
  13.0 0.0 collective-permute-done.1
  13.1 0.0 collective-permute-done.2.feats_far
  13.1 1.8 %collective-permute-start.4 = (bf16[2,600,128]{2,1,0:T(8,128)(2,1)S(1)}, bf16[2,600,128]{2,1,0:T(8,128)(2,1)S(1)}, u32[]{:S(2)}, u32[]{:S(2)}) collective-permute-start(bf16[2,600,128]{2,1,0:T(8,128)(2,1)S(1)} %pad_maximum_fusion.refs_0_), channel_id=1, source_target_pairs={{0,2},{1,3},{2,0},{3,1},{4,6},{5,7},{6,4},{7,5},{8,10},{9,11},{10,... | collective-permute-start | bytes 921608 | tf_op jit(solution)/shard_map/ppermute | solution.py:308
  14.9 0.9 %collective-permute-start.3 = (bf16[2,600,128]{2,1,0:T(8,128)(2,1)S(1)}, bf16[2,600,128]{2,1,0:T(8,128)(2,1)S(1)}, u32[]{:S(2)}, u32[]{:S(2)}) collective-permute-start(bf16[2,600,128]{2,1,0:T(8,128)(2,1)S(1)} %pad_maximum_fusion.refs_0_), channel_id=1, source_target_pairs={{0,4},{1,5},{2,6},{3,7},{4,0},{5,1},{6,2},{7,3},{8,12},{9,13},{10,... | collective-permute-start | bytes 921608 | tf_op jit(solution)/shard_map/ppermute | solution.py:308
  15.8 3.9 %gradients.1 = (f32[2,2,2,304,128]{4,3,2,1,0:T(8,128)S(1)}, f32[2,2,2,296,128]{4,3,2,1,0:T(8,128)S(1)}, bf16[2,2,2,304,128]{4,3,2,1,0:T(8,128)(2,1)S(1)}, bf16[2,2,2,296,128]{4,3,2,1,0:T(8,128)(2,1)S(1)}) custom-call(bf16[25,8,128]{2,1,0:T(8,128)(2,1)S(1)} %collective-permute-done.feats_core, bf16[25,8,128]{2,1,0:T(8,128)(2,1)S(1)} %get-tuple-element.62.feats_own, ...), custom_call_target="tpu_custom_call" | custom-call | flops 1000 | bytes 1000 | tf_op jit(solution)/shard_map/gradients/pallas_call | solution.py:385
  19.7 2.0 %collective-permute-done.4.refs_2_ = bf16[2,600,128]{2,1,0:T(8,128)(2,1)S(1)} collective-permute-done((bf16[2,600,128]{2,1,0:T(8,128)(2,1)S(1)}, bf16[2,600,128]{2,1,0:T(8,128)(2,1)S(1)}, u32[]{:S(2)}, u32[]{:S(2)}) %collective-permute-start.4) | collective-permute-done | bytes 307232 | tf_op jit(solution)/shard_map/ppermute | solution.py:308
  21.7 1.4 %collective-permute-done.3.refs_1_ = bf16[2,600,128]{2,1,0:T(8,128)(2,1)S(1)} collective-permute-done((bf16[2,600,128]{2,1,0:T(8,128)(2,1)S(1)}, bf16[2,600,128]{2,1,0:T(8,128)(2,1)S(1)}, u32[]{:S(2)}, u32[]{:S(2)}) %collective-permute-start.3) | collective-permute-done | bytes 307232 | tf_op jit(solution)/shard_map/ppermute | solution.py:308
  23.1 1.5 %collective-permute-start.7 = (bf16[2,2,2,296,128]{4,3,2,1,0:T(8,128)(2,1)S(1)}, bf16[2,2,2,296,128]{4,3,2,1,0:T(8,128)(2,1)S(1)}, u32[]{:S(2)}, u32[]{:S(2)}) collective-permute-start(bf16[2,2,2,296,128]{4,3,2,1,0:T(8,128)(2,1)S(1)} %get-tuple-element.81), channel_id=1, source_target_pairs={{0,1},{1,0},{2,3},{3,2},{4,5},{5,4},{6,7},{7,6},{8,9},{9,8},{10,11... | collective-permute-start | bytes 1818632 | tf_op jit(solution)/shard_map/ppermute | solution.py:308
  24.6 0.0 collective-permute-start.5
  24.6 1.7 %collective-permute-done.7.came = bf16[2,2,2,296,128]{4,3,2,1,0:T(8,128)(2,1)S(1)} collective-permute-done((bf16[2,2,2,296,128]{4,3,2,1,0:T(8,128)(2,1)S(1)}, bf16[2,2,2,296,128]{4,3,2,1,0:T(8,128)(2,1)S(1)}, u32[]{:S(2)}, u32[]{:S(2)}) %collective-permute-start.7) | collective-permute-done | bytes 606240 | tf_op jit(solution)/shard_map/ppermute | solution.py:308
  26.3 0.1 halve.8
  26.4 1.0 %collective-permute-start.8 = (bf16[2,2,296,128]{3,2,1,0:T(8,128)(2,1)S(1)}, bf16[2,2,296,128]{3,2,1,0:T(8,128)(2,1)S(1)}, u32[]{:S(2)}, u32[]{:S(2)}) collective-permute-start(bf16[2,2,296,128]{3,2,1,0:T(8,128)(2,1)S(1)} %get-tuple-element.83), channel_id=1, source_target_pairs={{0,4},{1,5},{2,6},{3,7},{4,0},{5,1},{6,2},{7,3},{8,12},{9,13},{10,... | collective-permute-start | bytes 909320 | tf_op jit(solution)/shard_map/ppermute | solution.py:308
  27.3 0.0 collective-permute-done.5.came
  27.3 0.1 halve.6
  27.5 0.1 collective-permute-start.6
  27.6 0.9 %collective-permute-start.9 = (bf16[2,600,128]{2,1,0:T(8,128)(2,1)S(1)}, bf16[2,600,128]{2,1,0:T(8,128)(2,1)S(1)}, u32[]{:S(2)}, u32[]{:S(2)}) collective-permute-start(bf16[2,600,128]{2,1,0:T(8,128)(2,1)S(1)} %pad_maximum_fusion.refs_0_), channel_id=1, source_target_pairs={{0,1},{1,0},{2,3},{3,2},{4,5},{5,4},{6,7},{7,6},{8,9},{9,8},{10,11... | collective-permute-start | bytes 921608 | tf_op jit(solution)/shard_map/ppermute | solution.py:308
  28.5 0.0 collective-permute-start.11
  28.5 0.5 collective-permute-start.10
  29.1 5.8 %collective-permute-done.8.came = bf16[2,2,296,128]{3,2,1,0:T(8,128)(2,1)S(1)} collective-permute-done((bf16[2,2,296,128]{3,2,1,0:T(8,128)(2,1)S(1)}, bf16[2,2,296,128]{3,2,1,0:T(8,128)(2,1)S(1)}, u32[]{:S(2)}, u32[]{:S(2)}) %collective-permute-start.8) | collective-permute-done | bytes 303136 | tf_op jit(solution)/shard_map/ppermute | solution.py:308
  34.8 0.0 collective-permute-start.14
  34.8 0.1 halve.9
  34.9 0.9 %collective-permute-done.6.came = bf16[2,2,304,128]{3,2,1,0:T(8,128)(2,1)S(1)} collective-permute-done((bf16[2,2,304,128]{3,2,1,0:T(8,128)(2,1)S(1)}, bf16[2,2,304,128]{3,2,1,0:T(8,128)(2,1)S(1)}, u32[]{:S(2)}, u32[]{:S(2)}) %collective-permute-start.6) | collective-permute-done | bytes 311328 | tf_op jit(solution)/shard_map/ppermute | solution.py:308
  35.8 0.1 halve.7
  35.9 0.0 collective-permute-done.9.refs_3_
  35.9 0.9 %collective-permute-start.12 = (bf16[2,304,128]{2,1,0:T(8,128)(2,1)S(1)}, bf16[2,304,128]{2,1,0:T(8,128)(2,1)S(1)}, u32[]{:S(2)}, u32[]{:S(2)}) collective-permute-start(bf16[2,304,128]{2,1,0:T(8,128)(2,1)S(1)} %get-tuple-element.87), channel_id=1, source_target_pairs={{0,4},{1,5},{2,6},{3,7},{4,0},{5,1},{6,2},{7,3},{8,12},{9,13},{10,... | collective-permute-start | bytes 466952 | tf_op jit(solution)/shard_map/ppermute | solution.py:308
  36.8 2.6 %collective-permute-start.13 = (bf16[2,296,128]{2,1,0:T(8,128)(2,1)S(1)}, bf16[2,296,128]{2,1,0:T(8,128)(2,1)S(1)}, u32[]{:S(2)}, u32[]{:S(2)}) collective-permute-start(bf16[2,296,128]{2,1,0:T(8,128)(2,1)S(1)} %get-tuple-element.90), channel_id=1, source_target_pairs={{0,8},{1,9},{2,10},{3,11},{4,12},{5,13},{6,14},{7,15},{8,0},{9,1},... | collective-permute-start | bytes 454664 | tf_op jit(solution)/shard_map/ppermute | solution.py:308
  39.4 3.5 %collective-permute-done.13.came = bf16[2,296,128]{2,1,0:T(8,128)(2,1)S(1)} collective-permute-done((bf16[2,296,128]{2,1,0:T(8,128)(2,1)S(1)}, bf16[2,296,128]{2,1,0:T(8,128)(2,1)S(1)}, u32[]{:S(2)}, u32[]{:S(2)}) %collective-permute-start.13) | collective-permute-done | bytes 151584 | tf_op jit(solution)/shard_map/ppermute | solution.py:308
  43.0 0.0 collective-permute-done.12.came
  43.0 3.3 %collective-permute-start.15 = (bf16[2,600,128]{2,1,0:T(8,128)(2,1)S(1)}, bf16[2,600,128]{2,1,0:T(8,128)(2,1)S(1)}, u32[]{:S(2)}, u32[]{:S(2)}) collective-permute-start(bf16[2,600,128]{2,1,0:T(8,128)(2,1)S(1)} %collective-permute-done.14.refs_6_), channel_id=1, source_target_pairs={{0,1},{1,0},{2,3},{3,2},{4,5},{5,4},{6,7},{7,6},{8,9},{9,8},{10,11... | collective-permute-start | bytes 921608 | tf_op jit(solution)/shard_map/ppermute | solution.py:308
  46.3 1.4 %collective-permute-start.18 = (bf16[304,128]{1,0:T(8,128)(2,1)S(1)}, bf16[304,128]{1,0:T(8,128)(2,1)S(1)}, u32[]{:S(2)}, u32[]{:S(2)}) collective-permute-start(bf16[304,128]{1,0:T(8,128)(2,1)S(1)} %get-tuple-element.104), channel_id=1, source_target_pairs={{0,8},{1,9},{2,10},{3,11},{4,12},{5,13},{6,14},{7,15},{8,0},{9,1},... | collective-permute-start | bytes 233480 | tf_op jit(solution)/shard_map/ppermute | solution.py:308
  47.7 0.8 %collective-permute-start.19 = (bf16[296,128]{1,0:T(8,128)(2,1)S(1)}, bf16[296,128]{1,0:T(8,128)(2,1)S(1)}, u32[]{:S(2)}, u32[]{:S(2)}) collective-permute-start(bf16[296,128]{1,0:T(8,128)(2,1)S(1)} %get-tuple-element.105), channel_id=1, source_target_pairs={{0,2},{1,3},{2,0},{3,1},{4,6},{5,7},{6,4},{7,5},{8,10},{9,11},{10,... | collective-permute-start | bytes 227336 | tf_op jit(solution)/shard_map/ppermute | solution.py:308
  48.5 3.5 %backward.1 = (bf16[25,8,128]{2,1,0:T(8,128)(2,1)S(1)}, f32[25,8,128]{2,1,0:T(8,128)S(1)}, bf16[25,8,128]{2,1,0:T(8,128)(2,1)S(1)}) custom-call(bf16[2,600,128]{2,1,0:T(8,128)(2,1)S(1)} %pad_maximum_fusion.refs_0_, bf16[2,600,128]{2,1,0:T(8,128)(2,1)S(1)} %collective-permute-done.3.refs_1_, bf16[2,600,128]{2,1,0:T(8,128)(2,1)S(1)} %collective-permute-done.4.refs_2_, ...), custom_call_target="tpu_custom_call" | custom-call | flops 1000 | bytes 1000 | tf_op jit(solution)/shard_map/backward/pallas_call | solution.py:460
  52.0 0.7 %collective-permute-start.16 = (bf16[25,8,128]{2,1,0:T(8,128)(2,1)S(1)}, bf16[25,8,128]{2,1,0:T(8,128)(2,1)S(1)}, u32[]{:S(2)}, u32[]{:S(2)}) collective-permute-start(bf16[25,8,128]{2,1,0:T(8,128)(2,1)S(1)} %get-tuple-element.108), channel_id=1, source_target_pairs={{0,1},{1,0},{2,3},{3,2},{4,5},{5,4},{6,7},{7,6},{8,9},{9,8},{10,11... | collective-permute-start | bytes 153608 | tf_op jit(solution)/shard_map/ppermute | solution.py:308
  52.7 2.6 %collective-permute-start.17 = (bf16[25,8,128]{2,1,0:T(8,128)(2,1)S(1)}, bf16[25,8,128]{2,1,0:T(8,128)(2,1)S(1)}, u32[]{:S(2)}, u32[]{:S(2)}) collective-permute-start(bf16[25,8,128]{2,1,0:T(8,128)(2,1)S(1)} %get-tuple-element.109), channel_id=1, source_target_pairs={{1,2},{3,4},{5,6},{7,8},{9,10},{11,12},{13,14},{2,1},{4,3},{6,5},{... | collective-permute-start | bytes 153608 | tf_op jit(solution)/shard_map/ppermute | solution.py:314
  55.4 0.0 collective-permute-done.19.came
  55.4 1.3 %collective-permute-start.21 = (bf16[296,128]{1,0:T(8,128)(2,1)S(1)}, bf16[296,128]{1,0:T(8,128)(2,1)S(1)}, u32[]{:S(2)}, u32[]{:S(2)}) collective-permute-start(bf16[296,128]{1,0:T(8,128)(2,1)S(1)} %get-tuple-element.117), channel_id=1, source_target_pairs={{0,16},{16,0},{1,17},{17,1},{2,18},{18,2},{3,19},{19,3},{4,20},{20... | collective-permute-start | bytes 227336 | tf_op jit(solution)/shard_map/ppermute | solution.py:500
  56.7 0.3 collective-permute-start.20
  57.0 1.4 %collective-permute-done.17 = bf16[25,8,128]{2,1,0:T(8,128)(2,1)S(1)} collective-permute-done((bf16[25,8,128]{2,1,0:T(8,128)(2,1)S(1)}, bf16[25,8,128]{2,1,0:T(8,128)(2,1)S(1)}, u32[]{:S(2)}, u32[]{:S(2)}) %collective-permute-start.17) | collective-permute-done | bytes 51232 | tf_op jit(solution)/shard_map/ppermute | solution.py:314
  58.4 0.7 %add_bitcast_fusion = f32[1,8,25,128]{3,1,2,0:T(8,128)} fusion(bf16[25,8,128]{2,1,0:T(8,128)(2,1)S(1)} %collective-permute-done.17, f32[25,8,128]{2,1,0:T(8,128)S(1)} %get-tuple-element.107, bf16[25,8,128]{2,1,0:T(8,128)(2,1)S(1)} %collective-permute-done.16), kind=kLoop, calls=%fused_computation.1 | loop fusion | flops 102400 | bytes 307200 | tf_op jit(solution)/shard_map/broadcast_in_dim | solution.py:478
  59.1 0.6 collective-permute-done.21.refs_0_
  59.7 1.9 %experts.2.refs_1_ = f32[16,76800]{1,0:T(8,128)} custom-call(f32[2,32]{1,0:T(2,128)S(1)} %copy-done, f32[296,128]{1,0:T(8,128)S(1)} %get-tuple-element.116.own_rows, bf16[296,128]{1,0:T(8,128)(2,1)S(1)} %collective-permute-done.21.refs_0_), custom_call_target="tpu_custom_call" | custom-call | flops 1000 | bytes 1000 | tf_op jit(solution)/shard_map/experts/pallas_call | solution.py:505
  61.7 1.8 %experts.3 = f32[16,76800]{1,0:T(8,128)} custom-call(f32[2,32]{1,0:T(2,128)S(1)} %copy-done, f32[304,128]{1,0:T(8,128)S(1)} %get-tuple-element.112.own_rows, bf16[304,128]{1,0:T(8,128)(2,1)S(1)} %collective-permute-done.20.refs_0_, f32[16,76800]{1,0:T(8,128)} %experts.2.refs_1_), custom_call_target="tpu_custom_call", output_to_operand_aliasing={{}: (3, {})} | custom-call | flops 1000 | bytes 1000 | tf_op jit(solution)/shard_map/experts/pallas_call | solution.py:505
  (14 shorter events, 0.2 us)
Async XLA Ops:
  2.4 10.6 %collective-permute-start.1 = (bf16[1,600,128]{2,1,0:T(8,128)(2,1)S(1)}, bf16[1,600,128]{2,1,0:T(8,128)(2,1)S(1)}, u32[]{:S(2)}, u32[]{:S(2)}) collective-permute-start(bf16[1,600,128]{2,1,0:T(8,128)(2,1)S(1)} %bitcast.15), channel_id=1, source_target_pairs={{0,8},{1,9},{2,10},{3,11},{4,12},{5,13},{6,14},{7,15},{8,0},{9,1},... | collective-permute-start | bytes 460808 | tf_op jit(solution)/shard_map/ppermute | solution.py:308
  5.7 4.6 %collective-permute-start = (bf16[25,8,128]{2,1,0:T(8,128)(2,1)}, bf16[25,8,128]{2,1,0:T(8,128)(2,1)S(1)}, u32[]{:S(2)}, u32[]{:S(2)}) collective-permute-start(bf16[25,8,128]{2,1,0:T(8,128)(2,1)} %bitcast.20), channel_id=1, source_target_pairs={{0,1},{1,0},{2,3},{3,2},{4,5},{5,4},{6,7},{7,6},{8,9},{9,8},{10,11... | collective-permute-start | bytes 153608 | tf_op jit(solution)/shard_map/ppermute | solution.py:308
  6.6 6.5 %collective-permute-start.2 = (bf16[25,8,128]{2,1,0:T(8,128)(2,1)}, bf16[25,8,128]{2,1,0:T(8,128)(2,1)S(1)}, u32[]{:S(2)}, u32[]{:S(2)}) collective-permute-start(bf16[25,8,128]{2,1,0:T(8,128)(2,1)} %bitcast.21), channel_id=1, source_target_pairs={{1,2},{3,4},{5,6},{7,8},{9,10},{11,12},{13,14},{2,1},{4,3},{6,5},{... | collective-permute-start | bytes 153608 | tf_op jit(solution)/shard_map/ppermute | solution.py:314
  13.1 8.6 %collective-permute-start.4 = (bf16[2,600,128]{2,1,0:T(8,128)(2,1)S(1)}, bf16[2,600,128]{2,1,0:T(8,128)(2,1)S(1)}, u32[]{:S(2)}, u32[]{:S(2)}) collective-permute-start(bf16[2,600,128]{2,1,0:T(8,128)(2,1)S(1)} %pad_maximum_fusion.refs_0_), channel_id=1, source_target_pairs={{0,2},{1,3},{2,0},{3,1},{4,6},{5,7},{6,4},{7,5},{8,10},{9,11},{10,... | collective-permute-start | bytes 921608 | tf_op jit(solution)/shard_map/ppermute | solution.py:308
  14.9 8.2 %collective-permute-start.3 = (bf16[2,600,128]{2,1,0:T(8,128)(2,1)S(1)}, bf16[2,600,128]{2,1,0:T(8,128)(2,1)S(1)}, u32[]{:S(2)}, u32[]{:S(2)}) collective-permute-start(bf16[2,600,128]{2,1,0:T(8,128)(2,1)S(1)} %pad_maximum_fusion.refs_0_), channel_id=1, source_target_pairs={{0,4},{1,5},{2,6},{3,7},{4,0},{5,1},{6,2},{7,3},{8,12},{9,13},{10,... | collective-permute-start | bytes 921608 | tf_op jit(solution)/shard_map/ppermute | solution.py:308
  23.1 3.2 %collective-permute-start.7 = (bf16[2,2,2,296,128]{4,3,2,1,0:T(8,128)(2,1)S(1)}, bf16[2,2,2,296,128]{4,3,2,1,0:T(8,128)(2,1)S(1)}, u32[]{:S(2)}, u32[]{:S(2)}) collective-permute-start(bf16[2,2,2,296,128]{4,3,2,1,0:T(8,128)(2,1)S(1)} %get-tuple-element.81), channel_id=1, source_target_pairs={{0,1},{1,0},{2,3},{3,2},{4,5},{5,4},{6,7},{7,6},{8,9},{9,8},{10,11... | collective-permute-start | bytes 1818632 | tf_op jit(solution)/shard_map/ppermute | solution.py:308
  24.6 2.7 %collective-permute-start.5 = (bf16[2,2,2,304,128]{4,3,2,1,0:T(8,128)(2,1)S(1)}, bf16[2,2,2,304,128]{4,3,2,1,0:T(8,128)(2,1)S(1)}, u32[]{:S(2)}, u32[]{:S(2)}) collective-permute-start(bf16[2,2,2,304,128]{4,3,2,1,0:T(8,128)(2,1)S(1)} %get-tuple-element.75), channel_id=1, source_target_pairs={{0,1},{1,0},{2,3},{3,2},{4,5},{5,4},{6,7},{7,6},{8,9},{9,8},{10,11... | collective-permute-start | bytes 1867784 | tf_op jit(solution)/shard_map/ppermute | solution.py:308
  26.4 8.5 %collective-permute-start.8 = (bf16[2,2,296,128]{3,2,1,0:T(8,128)(2,1)S(1)}, bf16[2,2,296,128]{3,2,1,0:T(8,128)(2,1)S(1)}, u32[]{:S(2)}, u32[]{:S(2)}) collective-permute-start(bf16[2,2,296,128]{3,2,1,0:T(8,128)(2,1)S(1)} %get-tuple-element.83), channel_id=1, source_target_pairs={{0,4},{1,5},{2,6},{3,7},{4,0},{5,1},{6,2},{7,3},{8,12},{9,13},{10,... | collective-permute-start | bytes 909320 | tf_op jit(solution)/shard_map/ppermute | solution.py:308
  27.3 32.4 %copy-start = (f32[2,32]{1,0:T(2,128)S(1)}, f32[2,32]{1,0:T(2,128)}, u32[]{:S(2)}) copy-start(f32[2,32]{1,0:T(2,128)} %mixing.3) | copy-start | bytes 772
  27.5 8.3 %collective-permute-start.6 = (bf16[2,2,304,128]{3,2,1,0:T(8,128)(2,1)S(1)}, bf16[2,2,304,128]{3,2,1,0:T(8,128)(2,1)S(1)}, u32[]{:S(2)}, u32[]{:S(2)}) collective-permute-start(bf16[2,2,304,128]{3,2,1,0:T(8,128)(2,1)S(1)} %get-tuple-element.77), channel_id=1, source_target_pairs={{0,2},{1,3},{2,0},{3,1},{4,6},{5,7},{6,4},{7,5},{8,10},{9,11},{10,... | collective-permute-start | bytes 933896 | tf_op jit(solution)/shard_map/ppermute | solution.py:308
  27.6 8.2 %collective-permute-start.9 = (bf16[2,600,128]{2,1,0:T(8,128)(2,1)S(1)}, bf16[2,600,128]{2,1,0:T(8,128)(2,1)S(1)}, u32[]{:S(2)}, u32[]{:S(2)}) collective-permute-start(bf16[2,600,128]{2,1,0:T(8,128)(2,1)S(1)} %pad_maximum_fusion.refs_0_), channel_id=1, source_target_pairs={{0,1},{1,0},{2,3},{3,2},{4,5},{5,4},{6,7},{7,6},{8,9},{9,8},{10,11... | collective-permute-start | bytes 921608 | tf_op jit(solution)/shard_map/ppermute | solution.py:308
  28.5 7.3 %collective-permute-start.11 = (bf16[2,600,128]{2,1,0:T(8,128)(2,1)S(1)}, bf16[2,600,128]{2,1,0:T(8,128)(2,1)S(1)}, u32[]{:S(2)}, u32[]{:S(2)}) collective-permute-start(bf16[2,600,128]{2,1,0:T(8,128)(2,1)S(1)} %collective-permute-done.4.refs_2_), channel_id=1, source_target_pairs={{0,1},{1,0},{2,3},{3,2},{4,5},{5,4},{6,7},{7,6},{8,9},{9,8},{10,11... | collective-permute-start | bytes 921608 | tf_op jit(solution)/shard_map/ppermute | solution.py:308
  28.5 7.3 %collective-permute-start.10 = (bf16[2,600,128]{2,1,0:T(8,128)(2,1)S(1)}, bf16[2,600,128]{2,1,0:T(8,128)(2,1)S(1)}, u32[]{:S(2)}, u32[]{:S(2)}) collective-permute-start(bf16[2,600,128]{2,1,0:T(8,128)(2,1)S(1)} %collective-permute-done.3.refs_1_), channel_id=1, source_target_pairs={{0,1},{1,0},{2,3},{3,2},{4,5},{5,4},{6,7},{7,6},{8,9},{9,8},{10,11... | collective-permute-start | bytes 921608 | tf_op jit(solution)/shard_map/ppermute | solution.py:308
  34.8 8.2 %collective-permute-start.14 = (bf16[2,600,128]{2,1,0:T(8,128)(2,1)S(1)}, bf16[2,600,128]{2,1,0:T(8,128)(2,1)S(1)}, u32[]{:S(2)}, u32[]{:S(2)}) collective-permute-start(bf16[2,600,128]{2,1,0:T(8,128)(2,1)S(1)} %collective-permute-done.3.refs_1_), channel_id=1, source_target_pairs={{0,2},{1,3},{2,0},{3,1},{4,6},{5,7},{6,4},{7,5},{8,10},{9,11},{10,... | collective-permute-start | bytes 921608 | tf_op jit(solution)/shard_map/ppermute | solution.py:308
  35.9 7.1 %collective-permute-start.12 = (bf16[2,304,128]{2,1,0:T(8,128)(2,1)S(1)}, bf16[2,304,128]{2,1,0:T(8,128)(2,1)S(1)}, u32[]{:S(2)}, u32[]{:S(2)}) collective-permute-start(bf16[2,304,128]{2,1,0:T(8,128)(2,1)S(1)} %get-tuple-element.87), channel_id=1, source_target_pairs={{0,4},{1,5},{2,6},{3,7},{4,0},{5,1},{6,2},{7,3},{8,12},{9,13},{10,... | collective-permute-start | bytes 466952 | tf_op jit(solution)/shard_map/ppermute | solution.py:308
  36.8 6.1 %collective-permute-start.13 = (bf16[2,296,128]{2,1,0:T(8,128)(2,1)S(1)}, bf16[2,296,128]{2,1,0:T(8,128)(2,1)S(1)}, u32[]{:S(2)}, u32[]{:S(2)}) collective-permute-start(bf16[2,296,128]{2,1,0:T(8,128)(2,1)S(1)} %get-tuple-element.90), channel_id=1, source_target_pairs={{0,8},{1,9},{2,10},{3,11},{4,12},{5,13},{6,14},{7,15},{8,0},{9,1},... | collective-permute-start | bytes 454664 | tf_op jit(solution)/shard_map/ppermute | solution.py:308
  43.0 5.5 %collective-permute-start.15 = (bf16[2,600,128]{2,1,0:T(8,128)(2,1)S(1)}, bf16[2,600,128]{2,1,0:T(8,128)(2,1)S(1)}, u32[]{:S(2)}, u32[]{:S(2)}) collective-permute-start(bf16[2,600,128]{2,1,0:T(8,128)(2,1)S(1)} %collective-permute-done.14.refs_6_), channel_id=1, source_target_pairs={{0,1},{1,0},{2,3},{3,2},{4,5},{5,4},{6,7},{7,6},{8,9},{9,8},{10,11... | collective-permute-start | bytes 921608 | tf_op jit(solution)/shard_map/ppermute | solution.py:308
  46.3 9.1 %collective-permute-start.18 = (bf16[304,128]{1,0:T(8,128)(2,1)S(1)}, bf16[304,128]{1,0:T(8,128)(2,1)S(1)}, u32[]{:S(2)}, u32[]{:S(2)}) collective-permute-start(bf16[304,128]{1,0:T(8,128)(2,1)S(1)} %get-tuple-element.104), channel_id=1, source_target_pairs={{0,8},{1,9},{2,10},{3,11},{4,12},{5,13},{6,14},{7,15},{8,0},{9,1},... | collective-permute-start | bytes 233480 | tf_op jit(solution)/shard_map/ppermute | solution.py:308
  47.7 7.6 %collective-permute-start.19 = (bf16[296,128]{1,0:T(8,128)(2,1)S(1)}, bf16[296,128]{1,0:T(8,128)(2,1)S(1)}, u32[]{:S(2)}, u32[]{:S(2)}) collective-permute-start(bf16[296,128]{1,0:T(8,128)(2,1)S(1)} %get-tuple-element.105), channel_id=1, source_target_pairs={{0,2},{1,3},{2,0},{3,1},{4,6},{5,7},{6,4},{7,5},{8,10},{9,11},{10,... | collective-permute-start | bytes 227336 | tf_op jit(solution)/shard_map/ppermute | solution.py:308
  52.0 5.0 %collective-permute-start.16 = (bf16[25,8,128]{2,1,0:T(8,128)(2,1)S(1)}, bf16[25,8,128]{2,1,0:T(8,128)(2,1)S(1)}, u32[]{:S(2)}, u32[]{:S(2)}) collective-permute-start(bf16[25,8,128]{2,1,0:T(8,128)(2,1)S(1)} %get-tuple-element.108), channel_id=1, source_target_pairs={{0,1},{1,0},{2,3},{3,2},{4,5},{5,4},{6,7},{7,6},{8,9},{9,8},{10,11... | collective-permute-start | bytes 153608 | tf_op jit(solution)/shard_map/ppermute | solution.py:308
  52.7 5.7 %collective-permute-start.17 = (bf16[25,8,128]{2,1,0:T(8,128)(2,1)S(1)}, bf16[25,8,128]{2,1,0:T(8,128)(2,1)S(1)}, u32[]{:S(2)}, u32[]{:S(2)}) collective-permute-start(bf16[25,8,128]{2,1,0:T(8,128)(2,1)S(1)} %get-tuple-element.109), channel_id=1, source_target_pairs={{1,2},{3,4},{5,6},{7,8},{9,10},{11,12},{13,14},{2,1},{4,3},{6,5},{... | collective-permute-start | bytes 153608 | tf_op jit(solution)/shard_map/ppermute | solution.py:314
  55.4 4.3 %collective-permute-start.21 = (bf16[296,128]{1,0:T(8,128)(2,1)S(1)}, bf16[296,128]{1,0:T(8,128)(2,1)S(1)}, u32[]{:S(2)}, u32[]{:S(2)}) collective-permute-start(bf16[296,128]{1,0:T(8,128)(2,1)S(1)} %get-tuple-element.117), channel_id=1, source_target_pairs={{0,16},{16,0},{1,17},{17,1},{2,18},{18,2},{3,19},{19,3},{4,20},{20... | collective-permute-start | bytes 227336 | tf_op jit(solution)/shard_map/ppermute | solution.py:500
  56.7 4.9 %collective-permute-start.20 = (bf16[304,128]{1,0:T(8,128)(2,1)S(1)}, bf16[304,128]{1,0:T(8,128)(2,1)S(1)}, u32[]{:S(2)}, u32[]{:S(2)}) collective-permute-start(bf16[304,128]{1,0:T(8,128)(2,1)S(1)} %get-tuple-element.113), channel_id=1, source_target_pairs={{0,16},{16,0},{1,17},{17,1},{2,18},{18,2},{3,19},{19,3},{4,20},{20... | collective-permute-start | bytes 233480 | tf_op jit(solution)/shard_map/ppermute | solution.py:500

commit v4 on v3

--- a/solution.py
+++ b/solution.py
@@ -178,6 +178,16 @@
         keep_b[spot] = grad[pl.ds(at + rows_a, rows_b), :]
 
 
+def unroll_kernel(flat, out, line, wide, sem):
+    copy = pltpu.make_async_copy(flat, line, sem)
+    copy.start()
+    copy.wait()
+    rows = out.shape[1]
+    for row in range(rows):
+        wide[row : row + 1, :] = line[:, row * LANES : (row + 1) * LANES].astype(F32)
+    out[0] = wide[...].astype(BF16)
+
+
 def spots(ref):
     return itertools.product(*(range(n) for n in ref.shape[:-2]))
 
@@ -340,7 +350,20 @@
     feats_core = swap(feats, 0)
     target, feats_core = lax.optimization_barrier((target_index, feats_core))
 
-    held = merged_weights.reshape(1, shard_rows, LANES)
+    held = pl.pallas_call(
+        unroll_kernel,
+        out_shape=jax.ShapeDtypeStruct((1, shard_rows, LANES), BF16),
+        in_specs=[spec(pltpu.HBM)],
+        out_specs=spec(),
+        scratch_shapes=[
+            pltpu.VMEM(merged_weights.shape, BF16),
+            pltpu.VMEM((shard_rows, LANES), F32),
+            pltpu.SemaphoreType.DMA,
+        ],
+        compiler_params=limit(6),
+        cost_estimate=cost(KCOST, KCOST),
+        name="rows",
+    )(in_hbm(merged_weights))
     came = swap(held, bits - 1)
 
     hbm = spec(pltpu.HBM)

time: 64.3 us -> 63.7 us (level)
  other arithmetic: 2.51 us -> 0.7 us
  Pallas kernels: 14.3 us -> 15.5 us
    unnamed x1 -> x0, other arithmetic: 1.81 us -> none
    pallas_call x0 -> x1, Pallas kernels: none -> 1.2 us  [on_device(): pl.pallas_call(unroll_kernel, out_shape=jax.ShapeDtypeStruct((1, shard_ro...]
where the time goes in v4:
time: 63.7 us; the launch traced here: 62.9 us
  starting transfers between devices  27.9 us (44%)
  waiting for transfers between devices  17.3 us (27%)
  Pallas kernels  15.5 us (24%)
  between operations  1.46 us (2%)
  other arithmetic  0.7 us (1%)
    ppermute x18, starting transfers between devices, swap(): return lax.ppermute(x, 'graph', [(i, i ^ 1 << bit) for i in range(size)])  20.7 us
    ppermute x18, waiting for transfers between devices, swap(): return lax.ppermute(x, 'graph', [(i, i ^ 1 << bit) for i in range(size)])  15.3 us
    ppermute x2, starting transfers between devices, across(): return lax.ppermute(x, 'graph', pairs + [(j, i) for i, j in pairs])  5.67 us
    pallas_call x1, Pallas kernels, on_device(): pl.pallas_call(grad_kernel, out_shape=[kind((2,) * (bits - 1) + (rows, LA...  3.85 us
    pallas_call x2, Pallas kernels, on_device(): pl.pallas_call(functools.partial(expert_kernel, first_row), out_shape=jax...  3.74 us
    pallas_call x1, Pallas kernels, on_device(): pl.pallas_call(functools.partial(backward_kernel, masks, 1 << bits - 1),...  3.53 us
    pallas_call x1, Pallas kernels, on_device(): pl.pallas_call(cot_kernel, out_shape=[pltpu.VMEM((5 * channels, edges), B...  2.7 us
    ppermute x2, starting transfers between devices, on_device(): lax.ppermute(rounded, 'dp', [(i, (i + n) % systems) for i in range(system...  1.6 us
  transfers between devices with their start and end apart: 22, of which 8 were waited for; matrix products, arithmetic and copies ran while one was open for 1% of the time, Pallas kernels for 20%

profile of v4, /device:TPU:1, one launch (start us, length us, event | category | flops | bytes accessed | tf_op | source)
XLA Modules:
  0.0 62.9 jit_solution(18281290718660582848)
XLA Ops:
  0.6 1.2 %rows.1 = bf16[1,600,128]{2,1,0:T(8,128)(2,1)S(1)} custom-call(bf16[1,76800]{1,0:T(2,128)(2,1)} %flat.1), custom_call_target="tpu_custom_call" | custom-call | flops 1000 | bytes 1000 | tf_op jit(solution)/shard_map/rows/pallas_call | solution.py:353
  1.8 3.2 %collective-permute-start.1 = (bf16[1,600,128]{2,1,0:T(8,128)(2,1)S(1)}, bf16[1,600,128]{2,1,0:T(8,128)(2,1)S(1)}, u32[]{:S(2)}, u32[]{:S(2)}) collective-permute-start(bf16[1,600,128]{2,1,0:T(8,128)(2,1)S(1)} %rows.1), channel_id=1, source_target_pairs={{0,8},{1,9},{2,10},{3,11},{4,12},{5,13},{6,14},{7,15},{8,0},{9,1},... | collective-permute-start | bytes 460808 | tf_op jit(solution)/shard_map/ppermute | solution.py:318
  5.0 1.0 %collective-permute-start = (bf16[25,8,128]{2,1,0:T(8,128)(2,1)}, bf16[25,8,128]{2,1,0:T(8,128)(2,1)S(1)}, u32[]{:S(2)}, u32[]{:S(2)}) collective-permute-start(bf16[25,8,128]{2,1,0:T(8,128)(2,1)} %bitcast.17), channel_id=1, source_target_pairs={{0,1},{1,0},{2,3},{3,2},{4,5},{5,4},{6,7},{7,6},{8,9},{9,8},{10,11... | collective-permute-start | bytes 153608 | tf_op jit(solution)/shard_map/ppermute | solution.py:318
  6.0 3.0 %collective-permute-start.2 = (bf16[25,8,128]{2,1,0:T(8,128)(2,1)}, bf16[25,8,128]{2,1,0:T(8,128)(2,1)S(1)}, u32[]{:S(2)}, u32[]{:S(2)}) collective-permute-start(bf16[25,8,128]{2,1,0:T(8,128)(2,1)} %bitcast.18), channel_id=1, source_target_pairs={{1,2},{3,4},{5,6},{7,8},{9,10},{11,12},{13,14},{2,1},{4,3},{6,5},{... | collective-permute-start | bytes 153608 | tf_op jit(solution)/shard_map/ppermute | solution.py:324
  9.7 0.0 collective-permute-done.feats_core
  9.7 2.7 %cotangents.1 = (bf16[640,256]{1,0:T(8,128)(2,1)S(1)}, bf16[512,512]{1,0:T(8,128)(2,1)S(1)}, bf16[384,512]{1,0:T(8,128)(2,1)S(1)}, f32[25,19,256]{2,1,0:T(8,128)...) custom-call(s32[1,256]{1,0:T(1,128)} %source.1, s32[1,256]{1,0:T(1,128)} %target, ...), custom_call_target="tpu_custom_call" | custom-call | flops 1000 | bytes 1000 | tf_op jit(solution)/shard_map/cotangents/pallas_call | solution.py:371
  12.4 0.0 collective-permute-done.1
  12.4 0.0 collective-permute-done.2.feats_far
  12.5 1.9 %collective-permute-start.4 = (bf16[2,600,128]{2,1,0:T(8,128)(2,1)S(1)}, bf16[2,600,128]{2,1,0:T(8,128)(2,1)S(1)}, u32[]{:S(2)}, u32[]{:S(2)}) collective-permute-start(bf16[2,600,128]{2,1,0:T(8,128)(2,1)S(1)} %pad_maximum_fusion.refs_0_), channel_id=1, source_target_pairs={{0,2},{1,3},{2,0},{3,1},{4,6},{5,7},{6,4},{7,5},{8,10},{9,11},{10,... | collective-permute-start | bytes 921608 | tf_op jit(solution)/shard_map/ppermute | solution.py:318
  14.3 0.9 %collective-permute-start.3 = (bf16[2,600,128]{2,1,0:T(8,128)(2,1)S(1)}, bf16[2,600,128]{2,1,0:T(8,128)(2,1)S(1)}, u32[]{:S(2)}, u32[]{:S(2)}) collective-permute-start(bf16[2,600,128]{2,1,0:T(8,128)(2,1)S(1)} %pad_maximum_fusion.refs_0_), channel_id=1, source_target_pairs={{0,4},{1,5},{2,6},{3,7},{4,0},{5,1},{6,2},{7,3},{8,12},{9,13},{10,... | collective-permute-start | bytes 921608 | tf_op jit(solution)/shard_map/ppermute | solution.py:318
  15.2 3.9 %gradients.1 = (f32[2,2,2,304,128]{4,3,2,1,0:T(8,128)S(1)}, f32[2,2,2,296,128]{4,3,2,1,0:T(8,128)S(1)}, bf16[2,2,2,304,128]{4,3,2,1,0:T(8,128)(2,1)S(1)}, bf16[2,2,2,296,128]{4,3,2,1,0:T(8,128)(2,1)S(1)}) custom-call(bf16[25,8,128]{2,1,0:T(8,128)(2,1)S(1)} %collective-permute-done.feats_core, bf16[25,8,128]{2,1,0:T(8,128)(2,1)S(1)} %get-tuple-element.62.feats_own, ...), custom_call_target="tpu_custom_call" | custom-call | flops 1000 | bytes 1000 | tf_op jit(solution)/shard_map/gradients/pallas_call | solution.py:408
  19.1 2.0 %collective-permute-done.4.refs_2_ = bf16[2,600,128]{2,1,0:T(8,128)(2,1)S(1)} collective-permute-done((bf16[2,600,128]{2,1,0:T(8,128)(2,1)S(1)}, bf16[2,600,128]{2,1,0:T(8,128)(2,1)S(1)}, u32[]{:S(2)}, u32[]{:S(2)}) %collective-permute-start.4) | collective-permute-done | bytes 307232 | tf_op jit(solution)/shard_map/ppermute | solution.py:318
  21.1 1.4 %collective-permute-done.3.refs_1_ = bf16[2,600,128]{2,1,0:T(8,128)(2,1)S(1)} collective-permute-done((bf16[2,600,128]{2,1,0:T(8,128)(2,1)S(1)}, bf16[2,600,128]{2,1,0:T(8,128)(2,1)S(1)}, u32[]{:S(2)}, u32[]{:S(2)}) %collective-permute-start.3) | collective-permute-done | bytes 307232 | tf_op jit(solution)/shard_map/ppermute | solution.py:318
  22.5 1.5 %collective-permute-start.7 = (bf16[2,2,2,296,128]{4,3,2,1,0:T(8,128)(2,1)S(1)}, bf16[2,2,2,296,128]{4,3,2,1,0:T(8,128)(2,1)S(1)}, u32[]{:S(2)}, u32[]{:S(2)}) collective-permute-start(bf16[2,2,2,296,128]{4,3,2,1,0:T(8,128)(2,1)S(1)} %get-tuple-element.81), channel_id=1, source_target_pairs={{0,1},{1,0},{2,3},{3,2},{4,5},{5,4},{6,7},{7,6},{8,9},{9,8},{10,11... | collective-permute-start | bytes 1818632 | tf_op jit(solution)/shard_map/ppermute | solution.py:318
  24.0 0.0 collective-permute-start.5
  24.0 1.7 %collective-permute-done.7.came = bf16[2,2,2,296,128]{4,3,2,1,0:T(8,128)(2,1)S(1)} collective-permute-done((bf16[2,2,2,296,128]{4,3,2,1,0:T(8,128)(2,1)S(1)}, bf16[2,2,2,296,128]{4,3,2,1,0:T(8,128)(2,1)S(1)}, u32[]{:S(2)}, u32[]{:S(2)}) %collective-permute-start.7) | collective-permute-done | bytes 606240 | tf_op jit(solution)/shard_map/ppermute | solution.py:318
  25.7 0.1 halve.8
  25.8 1.0 %collective-permute-start.8 = (bf16[2,2,296,128]{3,2,1,0:T(8,128)(2,1)S(1)}, bf16[2,2,296,128]{3,2,1,0:T(8,128)(2,1)S(1)}, u32[]{:S(2)}, u32[]{:S(2)}) collective-permute-start(bf16[2,2,296,128]{3,2,1,0:T(8,128)(2,1)S(1)} %get-tuple-element.83), channel_id=1, source_target_pairs={{0,4},{1,5},{2,6},{3,7},{4,0},{5,1},{6,2},{7,3},{8,12},{9,13},{10,... | collective-permute-start | bytes 909320 | tf_op jit(solution)/shard_map/ppermute | solution.py:318
  26.7 0.1 halve.6
  26.9 0.1 collective-permute-start.6
  27.0 0.9 %collective-permute-start.9 = (bf16[2,600,128]{2,1,0:T(8,128)(2,1)S(1)}, bf16[2,600,128]{2,1,0:T(8,128)(2,1)S(1)}, u32[]{:S(2)}, u32[]{:S(2)}) collective-permute-start(bf16[2,600,128]{2,1,0:T(8,128)(2,1)S(1)} %pad_maximum_fusion.refs_0_), channel_id=1, source_target_pairs={{0,1},{1,0},{2,3},{3,2},{4,5},{5,4},{6,7},{7,6},{8,9},{9,8},{10,11... | collective-permute-start | bytes 921608 | tf_op jit(solution)/shard_map/ppermute | solution.py:318
  27.9 0.5 collective-permute-start.10
  28.4 5.8 %collective-permute-done.8.came = bf16[2,2,296,128]{3,2,1,0:T(8,128)(2,1)S(1)} collective-permute-done((bf16[2,2,296,128]{3,2,1,0:T(8,128)(2,1)S(1)}, bf16[2,2,296,128]{3,2,1,0:T(8,128)(2,1)S(1)}, u32[]{:S(2)}, u32[]{:S(2)}) %collective-permute-start.8) | collective-permute-done | bytes 303136 | tf_op jit(solution)/shard_map/ppermute | solution.py:318
  34.2 0.0 collective-permute-start.14
  34.2 0.1 halve.9
  34.3 0.9 %collective-permute-done.6.came = bf16[2,2,304,128]{3,2,1,0:T(8,128)(2,1)S(1)} collective-permute-done((bf16[2,2,304,128]{3,2,1,0:T(8,128)(2,1)S(1)}, bf16[2,2,304,128]{3,2,1,0:T(8,128)(2,1)S(1)}, u32[]{:S(2)}, u32[]{:S(2)}) %collective-permute-start.6) | collective-permute-done | bytes 311328 | tf_op jit(solution)/shard_map/ppermute | solution.py:318
  35.2 0.1 halve.7
  35.2 0.0 collective-permute-done.9.refs_3_
  35.3 0.0 collective-permute-done.10.refs_4_
  35.3 0.9 %collective-permute-start.12 = (bf16[2,304,128]{2,1,0:T(8,128)(2,1)S(1)}, bf16[2,304,128]{2,1,0:T(8,128)(2,1)S(1)}, u32[]{:S(2)}, u32[]{:S(2)}) collective-permute-start(bf16[2,304,128]{2,1,0:T(8,128)(2,1)S(1)} %get-tuple-element.87), channel_id=1, source_target_pairs={{0,4},{1,5},{2,6},{3,7},{4,0},{5,1},{6,2},{7,3},{8,12},{9,13},{10,... | collective-permute-start | bytes 466952 | tf_op jit(solution)/shard_map/ppermute | solution.py:318
  36.2 2.6 %collective-permute-start.13 = (bf16[2,296,128]{2,1,0:T(8,128)(2,1)S(1)}, bf16[2,296,128]{2,1,0:T(8,128)(2,1)S(1)}, u32[]{:S(2)}, u32[]{:S(2)}) collective-permute-start(bf16[2,296,128]{2,1,0:T(8,128)(2,1)S(1)} %get-tuple-element.90), channel_id=1, source_target_pairs={{0,8},{1,9},{2,10},{3,11},{4,12},{5,13},{6,14},{7,15},{8,0},{9,1},... | collective-permute-start | bytes 454664 | tf_op jit(solution)/shard_map/ppermute | solution.py:318
  38.8 3.5 %collective-permute-done.13.came = bf16[2,296,128]{2,1,0:T(8,128)(2,1)S(1)} collective-permute-done((bf16[2,296,128]{2,1,0:T(8,128)(2,1)S(1)}, bf16[2,296,128]{2,1,0:T(8,128)(2,1)S(1)}, u32[]{:S(2)}, u32[]{:S(2)}) %collective-permute-start.13) | collective-permute-done | bytes 151584 | tf_op jit(solution)/shard_map/ppermute | solution.py:318
  42.4 0.0 collective-permute-done.14.refs_6_
  42.4 3.3 %collective-permute-start.15 = (bf16[2,600,128]{2,1,0:T(8,128)(2,1)S(1)}, bf16[2,600,128]{2,1,0:T(8,128)(2,1)S(1)}, u32[]{:S(2)}, u32[]{:S(2)}) collective-permute-start(bf16[2,600,128]{2,1,0:T(8,128)(2,1)S(1)} %collective-permute-done.14.refs_6_), channel_id=1, source_target_pairs={{0,1},{1,0},{2,3},{3,2},{4,5},{5,4},{6,7},{7,6},{8,9},{9,8},{10,11... | collective-permute-start | bytes 921608 | tf_op jit(solution)/shard_map/ppermute | solution.py:318
  45.7 1.4 %collective-permute-start.18 = (bf16[304,128]{1,0:T(8,128)(2,1)S(1)}, bf16[304,128]{1,0:T(8,128)(2,1)S(1)}, u32[]{:S(2)}, u32[]{:S(2)}) collective-permute-start(bf16[304,128]{1,0:T(8,128)(2,1)S(1)} %get-tuple-element.104), channel_id=1, source_target_pairs={{0,8},{1,9},{2,10},{3,11},{4,12},{5,13},{6,14},{7,15},{8,0},{9,1},... | collective-permute-start | bytes 233480 | tf_op jit(solution)/shard_map/ppermute | solution.py:318
  47.1 0.8 %collective-permute-start.19 = (bf16[296,128]{1,0:T(8,128)(2,1)S(1)}, bf16[296,128]{1,0:T(8,128)(2,1)S(1)}, u32[]{:S(2)}, u32[]{:S(2)}) collective-permute-start(bf16[296,128]{1,0:T(8,128)(2,1)S(1)} %get-tuple-element.105), channel_id=1, source_target_pairs={{0,2},{1,3},{2,0},{3,1},{4,6},{5,7},{6,4},{7,5},{8,10},{9,11},{10,... | collective-permute-start | bytes 227336 | tf_op jit(solution)/shard_map/ppermute | solution.py:318
  47.9 0.0 collective-permute-done.15.refs_7_
  47.9 3.5 %backward.1 = (bf16[25,8,128]{2,1,0:T(8,128)(2,1)S(1)}, f32[25,8,128]{2,1,0:T(8,128)S(1)}, bf16[25,8,128]{2,1,0:T(8,128)(2,1)S(1)}) custom-call(bf16[2,600,128]{2,1,0:T(8,128)(2,1)S(1)} %pad_maximum_fusion.refs_0_, bf16[2,600,128]{2,1,0:T(8,128)(2,1)S(1)} %collective-permute-done.3.refs_1_, bf16[2,600,128]{2,1,0:T(8,128)(2,1)S(1)} %collective-permute-done.4.refs_2_, ...), custom_call_target="tpu_custom_call" | custom-call | flops 1000 | bytes 1000 | tf_op jit(solution)/shard_map/backward/pallas_call | solution.py:483
  51.4 0.7 %collective-permute-start.16 = (bf16[25,8,128]{2,1,0:T(8,128)(2,1)S(1)}, bf16[25,8,128]{2,1,0:T(8,128)(2,1)S(1)}, u32[]{:S(2)}, u32[]{:S(2)}) collective-permute-start(bf16[25,8,128]{2,1,0:T(8,128)(2,1)S(1)} %get-tuple-element.108), channel_id=1, source_target_pairs={{0,1},{1,0},{2,3},{3,2},{4,5},{5,4},{6,7},{7,6},{8,9},{9,8},{10,11... | collective-permute-start | bytes 153608 | tf_op jit(solution)/shard_map/ppermute | solution.py:318
  52.1 2.6 %collective-permute-start.17 = (bf16[25,8,128]{2,1,0:T(8,128)(2,1)S(1)}, bf16[25,8,128]{2,1,0:T(8,128)(2,1)S(1)}, u32[]{:S(2)}, u32[]{:S(2)}) collective-permute-start(bf16[25,8,128]{2,1,0:T(8,128)(2,1)S(1)} %get-tuple-element.109), channel_id=1, source_target_pairs={{1,2},{3,4},{5,6},{7,8},{9,10},{11,12},{13,14},{2,1},{4,3},{6,5},{... | collective-permute-start | bytes 153608 | tf_op jit(solution)/shard_map/ppermute | solution.py:324
  54.7 0.0 collective-permute-done.19.came
  54.8 1.3 %collective-permute-start.21 = (bf16[296,128]{1,0:T(8,128)(2,1)S(1)}, bf16[296,128]{1,0:T(8,128)(2,1)S(1)}, u32[]{:S(2)}, u32[]{:S(2)}) collective-permute-start(bf16[296,128]{1,0:T(8,128)(2,1)S(1)} %get-tuple-element.117), channel_id=1, source_target_pairs={{0,16},{16,0},{1,17},{17,1},{2,18},{18,2},{3,19},{19,3},{4,20},{20... | collective-permute-start | bytes 227336 | tf_op jit(solution)/shard_map/ppermute | solution.py:523
  56.1 0.3 collective-permute-start.20
  56.4 1.4 %collective-permute-done.17 = bf16[25,8,128]{2,1,0:T(8,128)(2,1)S(1)} collective-permute-done((bf16[25,8,128]{2,1,0:T(8,128)(2,1)S(1)}, bf16[25,8,128]{2,1,0:T(8,128)(2,1)S(1)}, u32[]{:S(2)}, u32[]{:S(2)}) %collective-permute-start.17) | collective-permute-done | bytes 51232 | tf_op jit(solution)/shard_map/ppermute | solution.py:324
  57.8 0.7 %add_bitcast_fusion = f32[1,8,25,128]{3,1,2,0:T(8,128)} fusion(bf16[25,8,128]{2,1,0:T(8,128)(2,1)S(1)} %collective-permute-done.17, f32[25,8,128]{2,1,0:T(8,128)S(1)} %get-tuple-element.107, bf16[25,8,128]{2,1,0:T(8,128)(2,1)S(1)} %collective-permute-done.16), kind=kLoop, calls=%fused_computation.1 | loop fusion | flops 102400 | bytes 307200 | tf_op jit(solution)/shard_map/broadcast_in_dim | solution.py:501
  58.5 0.6 %collective-permute-done.21.refs_0_ = bf16[296,128]{1,0:T(8,128)(2,1)S(1)} collective-permute-done((bf16[296,128]{1,0:T(8,128)(2,1)S(1)}, bf16[296,128]{1,0:T(8,128)(2,1)S(1)}, u32[]{:S(2)}, u32[]{:S(2)}) %collective-permute-start.21) | collective-permute-done | bytes 75808 | tf_op jit(solution)/shard_map/ppermute | solution.py:523
  59.1 1.9 %experts.2.refs_1_ = f32[16,76800]{1,0:T(8,128)} custom-call(f32[2,32]{1,0:T(2,128)S(1)} %copy-done, f32[296,128]{1,0:T(8,128)S(1)} %get-tuple-element.116.own_rows, bf16[296,128]{1,0:T(8,128)(2,1)S(1)} %collective-permute-done.21.refs_0_), custom_call_target="tpu_custom_call" | custom-call | flops 1000 | bytes 1000 | tf_op jit(solution)/shard_map/experts/pallas_call | solution.py:528
  61.1 1.8 %experts.3 = f32[16,76800]{1,0:T(8,128)} custom-call(f32[2,32]{1,0:T(2,128)S(1)} %copy-done, f32[304,128]{1,0:T(8,128)S(1)} %get-tuple-element.112.own_rows, bf16[304,128]{1,0:T(8,128)(2,1)S(1)} %collective-permute-done.20.refs_0_, f32[16,76800]{1,0:T(8,128)} %experts.2.refs_1_), custom_call_target="tpu_custom_call", output_to_operand_aliasing={{}: (3, {})} | custom-call | flops 1000 | bytes 1000 | tf_op jit(solution)/shard_map/experts/pallas_call | solution.py:528
  (14 shorter events, 0.2 us)
Async XLA Ops:
  1.8 10.6 %collective-permute-start.1 = (bf16[1,600,128]{2,1,0:T(8,128)(2,1)S(1)}, bf16[1,600,128]{2,1,0:T(8,128)(2,1)S(1)}, u32[]{:S(2)}, u32[]{:S(2)}) collective-permute-start(bf16[1,600,128]{2,1,0:T(8,128)(2,1)S(1)} %rows.1), channel_id=1, source_target_pairs={{0,8},{1,9},{2,10},{3,11},{4,12},{5,13},{6,14},{7,15},{8,0},{9,1},... | collective-permute-start | bytes 460808 | tf_op jit(solution)/shard_map/ppermute | solution.py:318
  5.0 4.6 %collective-permute-start = (bf16[25,8,128]{2,1,0:T(8,128)(2,1)}, bf16[25,8,128]{2,1,0:T(8,128)(2,1)S(1)}, u32[]{:S(2)}, u32[]{:S(2)}) collective-permute-start(bf16[25,8,128]{2,1,0:T(8,128)(2,1)} %bitcast.17), channel_id=1, source_target_pairs={{0,1},{1,0},{2,3},{3,2},{4,5},{5,4},{6,7},{7,6},{8,9},{9,8},{10,11... | collective-permute-start | bytes 153608 | tf_op jit(solution)/shard_map/ppermute | solution.py:318
  6.0 6.5 %collective-permute-start.2 = (bf16[25,8,128]{2,1,0:T(8,128)(2,1)}, bf16[25,8,128]{2,1,0:T(8,128)(2,1)S(1)}, u32[]{:S(2)}, u32[]{:S(2)}) collective-permute-start(bf16[25,8,128]{2,1,0:T(8,128)(2,1)} %bitcast.18), channel_id=1, source_target_pairs={{1,2},{3,4},{5,6},{7,8},{9,10},{11,12},{13,14},{2,1},{4,3},{6,5},{... | collective-permute-start | bytes 153608 | tf_op jit(solution)/shard_map/ppermute | solution.py:324
  12.5 8.6 %collective-permute-start.4 = (bf16[2,600,128]{2,1,0:T(8,128)(2,1)S(1)}, bf16[2,600,128]{2,1,0:T(8,128)(2,1)S(1)}, u32[]{:S(2)}, u32[]{:S(2)}) collective-permute-start(bf16[2,600,128]{2,1,0:T(8,128)(2,1)S(1)} %pad_maximum_fusion.refs_0_), channel_id=1, source_target_pairs={{0,2},{1,3},{2,0},{3,1},{4,6},{5,7},{6,4},{7,5},{8,10},{9,11},{10,... | collective-permute-start | bytes 921608 | tf_op jit(solution)/shard_map/ppermute | solution.py:318
  14.3 8.2 %collective-permute-start.3 = (bf16[2,600,128]{2,1,0:T(8,128)(2,1)S(1)}, bf16[2,600,128]{2,1,0:T(8,128)(2,1)S(1)}, u32[]{:S(2)}, u32[]{:S(2)}) collective-permute-start(bf16[2,600,128]{2,1,0:T(8,128)(2,1)S(1)} %pad_maximum_fusion.refs_0_), channel_id=1, source_target_pairs={{0,4},{1,5},{2,6},{3,7},{4,0},{5,1},{6,2},{7,3},{8,12},{9,13},{10,... | collective-permute-start | bytes 921608 | tf_op jit(solution)/shard_map/ppermute | solution.py:318
  22.5 3.2 %collective-permute-start.7 = (bf16[2,2,2,296,128]{4,3,2,1,0:T(8,128)(2,1)S(1)}, bf16[2,2,2,296,128]{4,3,2,1,0:T(8,128)(2,1)S(1)}, u32[]{:S(2)}, u32[]{:S(2)}) collective-permute-start(bf16[2,2,2,296,128]{4,3,2,1,0:T(8,128)(2,1)S(1)} %get-tuple-element.81), channel_id=1, source_target_pairs={{0,1},{1,0},{2,3},{3,2},{4,5},{5,4},{6,7},{7,6},{8,9},{9,8},{10,11... | collective-permute-start | bytes 1818632 | tf_op jit(solution)/shard_map/ppermute | solution.py:318
  24.0 2.7 %collective-permute-start.5 = (bf16[2,2,2,304,128]{4,3,2,1,0:T(8,128)(2,1)S(1)}, bf16[2,2,2,304,128]{4,3,2,1,0:T(8,128)(2,1)S(1)}, u32[]{:S(2)}, u32[]{:S(2)}) collective-permute-start(bf16[2,2,2,304,128]{4,3,2,1,0:T(8,128)(2,1)S(1)} %get-tuple-element.75), channel_id=1, source_target_pairs={{0,1},{1,0},{2,3},{3,2},{4,5},{5,4},{6,7},{7,6},{8,9},{9,8},{10,11... | collective-permute-start | bytes 1867784 | tf_op jit(solution)/shard_map/ppermute | solution.py:318
  25.8 8.5 %collective-permute-start.8 = (bf16[2,2,296,128]{3,2,1,0:T(8,128)(2,1)S(1)}, bf16[2,2,296,128]{3,2,1,0:T(8,128)(2,1)S(1)}, u32[]{:S(2)}, u32[]{:S(2)}) collective-permute-start(bf16[2,2,296,128]{3,2,1,0:T(8,128)(2,1)S(1)} %get-tuple-element.83), channel_id=1, source_target_pairs={{0,4},{1,5},{2,6},{3,7},{4,0},{5,1},{6,2},{7,3},{8,12},{9,13},{10,... | collective-permute-start | bytes 909320 | tf_op jit(solution)/shard_map/ppermute | solution.py:318
  26.7 32.4 %copy-start = (f32[2,32]{1,0:T(2,128)S(1)}, f32[2,32]{1,0:T(2,128)}, u32[]{:S(2)}) copy-start(f32[2,32]{1,0:T(2,128)} %mixing.3) | copy-start | bytes 772
  26.9 8.3 %collective-permute-start.6 = (bf16[2,2,304,128]{3,2,1,0:T(8,128)(2,1)S(1)}, bf16[2,2,304,128]{3,2,1,0:T(8,128)(2,1)S(1)}, u32[]{:S(2)}, u32[]{:S(2)}) collective-permute-start(bf16[2,2,304,128]{3,2,1,0:T(8,128)(2,1)S(1)} %get-tuple-element.77), channel_id=1, source_target_pairs={{0,2},{1,3},{2,0},{3,1},{4,6},{5,7},{6,4},{7,5},{8,10},{9,11},{10,... | collective-permute-start | bytes 933896 | tf_op jit(solution)/shard_map/ppermute | solution.py:318
  27.0 8.2 %collective-permute-start.9 = (bf16[2,600,128]{2,1,0:T(8,128)(2,1)S(1)}, bf16[2,600,128]{2,1,0:T(8,128)(2,1)S(1)}, u32[]{:S(2)}, u32[]{:S(2)}) collective-permute-start(bf16[2,600,128]{2,1,0:T(8,128)(2,1)S(1)} %pad_maximum_fusion.refs_0_), channel_id=1, source_target_pairs={{0,1},{1,0},{2,3},{3,2},{4,5},{5,4},{6,7},{7,6},{8,9},{9,8},{10,11... | collective-permute-start | bytes 921608 | tf_op jit(solution)/shard_map/ppermute | solution.py:318
  27.9 7.3 %collective-permute-start.11 = (bf16[2,600,128]{2,1,0:T(8,128)(2,1)S(1)}, bf16[2,600,128]{2,1,0:T(8,128)(2,1)S(1)}, u32[]{:S(2)}, u32[]{:S(2)}) collective-permute-start(bf16[2,600,128]{2,1,0:T(8,128)(2,1)S(1)} %collective-permute-done.4.refs_2_), channel_id=1, source_target_pairs={{0,1},{1,0},{2,3},{3,2},{4,5},{5,4},{6,7},{7,6},{8,9},{9,8},{10,11... | collective-permute-start | bytes 921608 | tf_op jit(solution)/shard_map/ppermute | solution.py:318
  27.9 7.3 %collective-permute-start.10 = (bf16[2,600,128]{2,1,0:T(8,128)(2,1)S(1)}, bf16[2,600,128]{2,1,0:T(8,128)(2,1)S(1)}, u32[]{:S(2)}, u32[]{:S(2)}) collective-permute-start(bf16[2,600,128]{2,1,0:T(8,128)(2,1)S(1)} %collective-permute-done.3.refs_1_), channel_id=1, source_target_pairs={{0,1},{1,0},{2,3},{3,2},{4,5},{5,4},{6,7},{7,6},{8,9},{9,8},{10,11... | collective-permute-start | bytes 921608 | tf_op jit(solution)/shard_map/ppermute | solution.py:318
  34.2 8.2 %collective-permute-start.14 = (bf16[2,600,128]{2,1,0:T(8,128)(2,1)S(1)}, bf16[2,600,128]{2,1,0:T(8,128)(2,1)S(1)}, u32[]{:S(2)}, u32[]{:S(2)}) collective-permute-start(bf16[2,600,128]{2,1,0:T(8,128)(2,1)S(1)} %collective-permute-done.3.refs_1_), channel_id=1, source_target_pairs={{0,2},{1,3},{2,0},{3,1},{4,6},{5,7},{6,4},{7,5},{8,10},{9,11},{10,... | collective-permute-start | bytes 921608 | tf_op jit(solution)/shard_map/ppermute | solution.py:318
  35.3 7.1 %collective-permute-start.12 = (bf16[2,304,128]{2,1,0:T(8,128)(2,1)S(1)}, bf16[2,304,128]{2,1,0:T(8,128)(2,1)S(1)}, u32[]{:S(2)}, u32[]{:S(2)}) collective-permute-start(bf16[2,304,128]{2,1,0:T(8,128)(2,1)S(1)} %get-tuple-element.87), channel_id=1, source_target_pairs={{0,4},{1,5},{2,6},{3,7},{4,0},{5,1},{6,2},{7,3},{8,12},{9,13},{10,... | collective-permute-start | bytes 466952 | tf_op jit(solution)/shard_map/ppermute | solution.py:318
  36.2 6.1 %collective-permute-start.13 = (bf16[2,296,128]{2,1,0:T(8,128)(2,1)S(1)}, bf16[2,296,128]{2,1,0:T(8,128)(2,1)S(1)}, u32[]{:S(2)}, u32[]{:S(2)}) collective-permute-start(bf16[2,296,128]{2,1,0:T(8,128)(2,1)S(1)} %get-tuple-element.90), channel_id=1, source_target_pairs={{0,8},{1,9},{2,10},{3,11},{4,12},{5,13},{6,14},{7,15},{8,0},{9,1},... | collective-permute-start | bytes 454664 | tf_op jit(solution)/shard_map/ppermute | solution.py:318
  42.4 5.5 %collective-permute-start.15 = (bf16[2,600,128]{2,1,0:T(8,128)(2,1)S(1)}, bf16[2,600,128]{2,1,0:T(8,128)(2,1)S(1)}, u32[]{:S(2)}, u32[]{:S(2)}) collective-permute-start(bf16[2,600,128]{2,1,0:T(8,128)(2,1)S(1)} %collective-permute-done.14.refs_6_), channel_id=1, source_target_pairs={{0,1},{1,0},{2,3},{3,2},{4,5},{5,4},{6,7},{7,6},{8,9},{9,8},{10,11... | collective-permute-start | bytes 921608 | tf_op jit(solution)/shard_map/ppermute | solution.py:318
  45.7 9.1 %collective-permute-start.18 = (bf16[304,128]{1,0:T(8,128)(2,1)S(1)}, bf16[304,128]{1,0:T(8,128)(2,1)S(1)}, u32[]{:S(2)}, u32[]{:S(2)}) collective-permute-start(bf16[304,128]{1,0:T(8,128)(2,1)S(1)} %get-tuple-element.104), channel_id=1, source_target_pairs={{0,8},{1,9},{2,10},{3,11},{4,12},{5,13},{6,14},{7,15},{8,0},{9,1},... | collective-permute-start | bytes 233480 | tf_op jit(solution)/shard_map/ppermute | solution.py:318
  47.1 7.6 %collective-permute-start.19 = (bf16[296,128]{1,0:T(8,128)(2,1)S(1)}, bf16[296,128]{1,0:T(8,128)(2,1)S(1)}, u32[]{:S(2)}, u32[]{:S(2)}) collective-permute-start(bf16[296,128]{1,0:T(8,128)(2,1)S(1)} %get-tuple-element.105), channel_id=1, source_target_pairs={{0,2},{1,3},{2,0},{3,1},{4,6},{5,7},{6,4},{7,5},{8,10},{9,11},{10,... | collective-permute-start | bytes 227336 | tf_op jit(solution)/shard_map/ppermute | solution.py:318
  51.4 5.0 %collective-permute-start.16 = (bf16[25,8,128]{2,1,0:T(8,128)(2,1)S(1)}, bf16[25,8,128]{2,1,0:T(8,128)(2,1)S(1)}, u32[]{:S(2)}, u32[]{:S(2)}) collective-permute-start(bf16[25,8,128]{2,1,0:T(8,128)(2,1)S(1)} %get-tuple-element.108), channel_id=1, source_target_pairs={{0,1},{1,0},{2,3},{3,2},{4,5},{5,4},{6,7},{7,6},{8,9},{9,8},{10,11... | collective-permute-start | bytes 153608 | tf_op jit(solution)/shard_map/ppermute | solution.py:318
  52.1 5.7 %collective-permute-start.17 = (bf16[25,8,128]{2,1,0:T(8,128)(2,1)S(1)}, bf16[25,8,128]{2,1,0:T(8,128)(2,1)S(1)}, u32[]{:S(2)}, u32[]{:S(2)}) collective-permute-start(bf16[25,8,128]{2,1,0:T(8,128)(2,1)S(1)} %get-tuple-element.109), channel_id=1, source_target_pairs={{1,2},{3,4},{5,6},{7,8},{9,10},{11,12},{13,14},{2,1},{4,3},{6,5},{... | collective-permute-start | bytes 153608 | tf_op jit(solution)/shard_map/ppermute | solution.py:324
  54.8 4.3 %collective-permute-start.21 = (bf16[296,128]{1,0:T(8,128)(2,1)S(1)}, bf16[296,128]{1,0:T(8,128)(2,1)S(1)}, u32[]{:S(2)}, u32[]{:S(2)}) collective-permute-start(bf16[296,128]{1,0:T(8,128)(2,1)S(1)} %get-tuple-element.117), channel_id=1, source_target_pairs={{0,16},{16,0},{1,17},{17,1},{2,18},{18,2},{3,19},{19,3},{4,20},{20... | collective-permute-start | bytes 227336 | tf_op jit(solution)/shard_map/ppermute | solution.py:523
  56.1 4.9 %collective-permute-start.20 = (bf16[304,128]{1,0:T(8,128)(2,1)S(1)}, bf16[304,128]{1,0:T(8,128)(2,1)S(1)}, u32[]{:S(2)}, u32[]{:S(2)}) collective-permute-start(bf16[304,128]{1,0:T(8,128)(2,1)S(1)} %get-tuple-element.113), channel_id=1, source_target_pairs={{0,16},{16,0},{1,17},{17,1},{2,18},{18,2},{3,19},{19,3},{4,20},{20... | collective-permute-start | bytes 233480 | tf_op jit(solution)/shard_map/ppermute | solution.py:523

commit v5 on v4

--- a/solution.py
+++ b/solution.py
@@ -471,9 +471,10 @@
     cames = exchange(0, aways)
     for turn in range(1, bits - 1):
         stays, aways = halve(turn, stays, cames)
-        masks = list(pieces)
-        together = lax.optimization_barrier((*aways, *pieces.values()))
-        aways, pieces = together[:2], dict(zip(masks, together[2:]))
+        if turn == 1:
+            masks = list(pieces)
+            together = lax.optimization_barrier((*aways, *pieces.values()))
+            aways, pieces = together[:2], dict(zip(masks, together[2:]))
         if turn == bits - 2:
             pieces.update(fan_out({1 << near | 1 << up: after(last, *aways)}))
         cames = exchange(turn, aways)
@@ -497,8 +498,6 @@
         cost_estimate=cost(KCOST, KCOST),
         name="backward",
     )(*ready[: len(masks)], *bmats, rot, gate, pick)
-    total = grads_own + swap(grads_core, 0).astype(F32) + across(grads_far).astype(F32)
-    atom_grads = jnp.transpose(total, (1, 0, 2))[None]
 
     cames = lax.optimization_barrier((*cames, grads_own))[:2]
     systems = lax.axis_size("dp")
@@ -516,13 +515,18 @@
         shares.append(share)
         roundeds.append(rounded)
 
+    from_core = swap(grads_core, 0)
+    from_far = across(after(grads_far, from_core))
+
     own_experts = mixing.shape[1] // systems
     expert_part = None
-    for first_row, share, rounded in reversed(list(zip((0, rows_a), shares, roundeds))):
+    arrived = []
+    for first_row, share, rounded in zip((0, rows_a), shares, roundeds):
         others = [
             lax.ppermute(rounded, "dp", [(i, (i + n) % systems) for i in range(systems)])
             for n in range(1, systems)
         ]
+        arrived += others
         rows = share.shape[0]
         before = [] if expert_part is None else [expert_part]
         expert_part = pl.pallas_call(
@@ -540,6 +544,9 @@
             cost_estimate=cost(KCOST, KCOST),
             name="experts",
         )(mixing, share, *others, *before)
+    from_far = after(from_far, *arrived)
+    total = grads_own + from_core.astype(F32) + from_far.astype(F32)
+    atom_grads = jnp.transpose(total, (1, 0, 2))[None]
     return (atom_grads, expert_part)
 
 

time: 63.7 us -> 63.6 us (level); the launches traced: 62.9 us -> 63.4 us
  starting transfers between devices: 27.9 us -> 30.5 us
  waiting for transfers between devices: 17.3 us -> 15.3 us
    ppermute x2, starting transfers between devices: 5.67 us -> 8.21 us  [across(): return lax.ppermute(x, 'graph', pairs + [(j, i) for i, j in pairs])]
    ppermute x2, waiting for transfers between devices: 1.39 us -> 0.01 us  [across(): return lax.ppermute(x, 'graph', pairs + [(j, i) for i, j in pairs])]
  transfers between devices with their start and end apart: 22 -> 22, of which waited for: 8 -> 6; matrix products, arithmetic and copies ran while one was open for 1% -> 0% of each run, Pallas kernels for 20% -> 23%
where the time goes in v5:
time: 63.6 us; the launch traced here: 63.4 us
  starting transfers between devices  30.5 us (48%)
  Pallas kernels  15.5 us (24%)
  waiting for transfers between devices  15.3 us (24%)
  between operations  1.48 us (2%)
  other arithmetic  0.7 us (1%)
    ppermute x18, starting transfers between devices, swap(): return lax.ppermute(x, 'graph', [(i, i ^ 1 << bit) for i in range(size)])  20.7 us
    ppermute x18, waiting for transfers between devices, swap(): return lax.ppermute(x, 'graph', [(i, i ^ 1 << bit) for i in range(size)])  15.3 us
    ppermute x2, starting transfers between devices, across(): return lax.ppermute(x, 'graph', pairs + [(j, i) for i, j in pairs])  8.21 us
    pallas_call x1, Pallas kernels, on_device(): pl.pallas_call(grad_kernel, out_shape=[kind((2,) * (bits - 1) + (rows, LA...  3.85 us
    pallas_call x2, Pallas kernels, on_device(): pl.pallas_call(functools.partial(expert_kernel, first_row), out_shape=jax...  3.74 us
    pallas_call x1, Pallas kernels, on_device(): pl.pallas_call(functools.partial(backward_kernel, masks, 1 << bits - 1),...  3.53 us
    pallas_call x1, Pallas kernels, on_device(): pl.pallas_call(cot_kernel, out_shape=[pltpu.VMEM((5 * channels, edges), B...  2.7 us
    ppermute x2, starting transfers between devices, on_device(): lax.ppermute(rounded, 'dp', [(i, (i + n) % systems) for i in range(system...  1.6 us
  transfers between devices with their start and end apart: 22, of which 6 were waited for; matrix products, arithmetic and copies ran while one was open for 0% of the time, Pallas kernels for 23%

profile of v5, /device:TPU:1, one launch (start us, length us, event | category | flops | bytes accessed | tf_op | source)
XLA Modules:
  0.0 63.4 jit_solution(10533769077618479764)
XLA Ops:
  0.6 1.2 %rows.1 = bf16[1,600,128]{2,1,0:T(8,128)(2,1)S(1)} custom-call(bf16[1,76800]{1,0:T(2,128)(2,1)} %flat.1), custom_call_target="tpu_custom_call" | custom-call | flops 1000 | bytes 1000 | tf_op jit(solution)/shard_map/rows/pallas_call | solution.py:353
  1.8 3.2 %collective-permute-start.1 = (bf16[1,600,128]{2,1,0:T(8,128)(2,1)S(1)}, bf16[1,600,128]{2,1,0:T(8,128)(2,1)S(1)}, u32[]{:S(2)}, u32[]{:S(2)}) collective-permute-start(bf16[1,600,128]{2,1,0:T(8,128)(2,1)S(1)} %rows.1), channel_id=1, source_target_pairs={{0,8},{1,9},{2,10},{3,11},{4,12},{5,13},{6,14},{7,15},{8,0},{9,1},... | collective-permute-start | bytes 460808 | tf_op jit(solution)/shard_map/ppermute | solution.py:318
  5.0 1.0 %collective-permute-start = (bf16[25,8,128]{2,1,0:T(8,128)(2,1)}, bf16[25,8,128]{2,1,0:T(8,128)(2,1)S(1)}, u32[]{:S(2)}, u32[]{:S(2)}) collective-permute-start(bf16[25,8,128]{2,1,0:T(8,128)(2,1)} %bitcast.17), channel_id=1, source_target_pairs={{0,1},{1,0},{2,3},{3,2},{4,5},{5,4},{6,7},{7,6},{8,9},{9,8},{10,11... | collective-permute-start | bytes 153608 | tf_op jit(solution)/shard_map/ppermute | solution.py:318
  6.0 3.0 %collective-permute-start.2 = (bf16[25,8,128]{2,1,0:T(8,128)(2,1)}, bf16[25,8,128]{2,1,0:T(8,128)(2,1)S(1)}, u32[]{:S(2)}, u32[]{:S(2)}) collective-permute-start(bf16[25,8,128]{2,1,0:T(8,128)(2,1)} %bitcast.18), channel_id=1, source_target_pairs={{1,2},{3,4},{5,6},{7,8},{9,10},{11,12},{13,14},{2,1},{4,3},{6,5},{... | collective-permute-start | bytes 153608 | tf_op jit(solution)/shard_map/ppermute | solution.py:324
  9.7 0.0 collective-permute-done.feats_core
  9.7 2.7 %cotangents.1 = (bf16[640,256]{1,0:T(8,128)(2,1)S(1)}, bf16[512,512]{1,0:T(8,128)(2,1)S(1)}, bf16[384,512]{1,0:T(8,128)(2,1)S(1)}, f32[25,19,256]{2,1,0:T(8,128)...) custom-call(s32[1,256]{1,0:T(1,128)} %source.1, s32[1,256]{1,0:T(1,128)} %target, ...), custom_call_target="tpu_custom_call" | custom-call | flops 1000 | bytes 1000 | tf_op jit(solution)/shard_map/cotangents/pallas_call | solution.py:371
  12.4 0.0 collective-permute-done.1
  12.4 0.0 collective-permute-done.2.feats_far
  12.5 1.9 %collective-permute-start.4 = (bf16[2,600,128]{2,1,0:T(8,128)(2,1)S(1)}, bf16[2,600,128]{2,1,0:T(8,128)(2,1)S(1)}, u32[]{:S(2)}, u32[]{:S(2)}) collective-permute-start(bf16[2,600,128]{2,1,0:T(8,128)(2,1)S(1)} %pad_maximum_fusion.refs_0_), channel_id=1, source_target_pairs={{0,2},{1,3},{2,0},{3,1},{4,6},{5,7},{6,4},{7,5},{8,10},{9,11},{10,... | collective-permute-start | bytes 921608 | tf_op jit(solution)/shard_map/ppermute | solution.py:318
  14.3 0.9 %collective-permute-start.3 = (bf16[2,600,128]{2,1,0:T(8,128)(2,1)S(1)}, bf16[2,600,128]{2,1,0:T(8,128)(2,1)S(1)}, u32[]{:S(2)}, u32[]{:S(2)}) collective-permute-start(bf16[2,600,128]{2,1,0:T(8,128)(2,1)S(1)} %pad_maximum_fusion.refs_0_), channel_id=1, source_target_pairs={{0,4},{1,5},{2,6},{3,7},{4,0},{5,1},{6,2},{7,3},{8,12},{9,13},{10,... | collective-permute-start | bytes 921608 | tf_op jit(solution)/shard_map/ppermute | solution.py:318
  15.2 3.9 %gradients.1 = (f32[2,2,2,304,128]{4,3,2,1,0:T(8,128)S(1)}, f32[2,2,2,296,128]{4,3,2,1,0:T(8,128)S(1)}, bf16[2,2,2,304,128]{4,3,2,1,0:T(8,128)(2,1)S(1)}, bf16[2,2,2,296,128]{4,3,2,1,0:T(8,128)(2,1)S(1)}) custom-call(bf16[25,8,128]{2,1,0:T(8,128)(2,1)S(1)} %collective-permute-done.feats_core, bf16[25,8,128]{2,1,0:T(8,128)(2,1)S(1)} %get-tuple-element.56.feats_own, ...), custom_call_target="tpu_custom_call" | custom-call | flops 1000 | bytes 1000 | tf_op jit(solution)/shard_map/gradients/pallas_call | solution.py:408
  19.1 2.0 %collective-permute-done.4.refs_2_ = bf16[2,600,128]{2,1,0:T(8,128)(2,1)S(1)} collective-permute-done((bf16[2,600,128]{2,1,0:T(8,128)(2,1)S(1)}, bf16[2,600,128]{2,1,0:T(8,128)(2,1)S(1)}, u32[]{:S(2)}, u32[]{:S(2)}) %collective-permute-start.4) | collective-permute-done | bytes 307232 | tf_op jit(solution)/shard_map/ppermute | solution.py:318
  21.1 1.4 %collective-permute-done.3.refs_1_ = bf16[2,600,128]{2,1,0:T(8,128)(2,1)S(1)} collective-permute-done((bf16[2,600,128]{2,1,0:T(8,128)(2,1)S(1)}, bf16[2,600,128]{2,1,0:T(8,128)(2,1)S(1)}, u32[]{:S(2)}, u32[]{:S(2)}) %collective-permute-start.3) | collective-permute-done | bytes 307232 | tf_op jit(solution)/shard_map/ppermute | solution.py:318
  22.5 1.5 %collective-permute-start.7 = (bf16[2,2,2,296,128]{4,3,2,1,0:T(8,128)(2,1)S(1)}, bf16[2,2,2,296,128]{4,3,2,1,0:T(8,128)(2,1)S(1)}, u32[]{:S(2)}, u32[]{:S(2)}) collective-permute-start(bf16[2,2,2,296,128]{4,3,2,1,0:T(8,128)(2,1)S(1)} %get-tuple-element.74), channel_id=1, source_target_pairs={{0,1},{1,0},{2,3},{3,2},{4,5},{5,4},{6,7},{7,6},{8,9},{9,8},{10,11... | collective-permute-start | bytes 1818632 | tf_op jit(solution)/shard_map/ppermute | solution.py:318
  24.0 0.0 collective-permute-start.5
  24.0 1.7 %collective-permute-done.7.came = bf16[2,2,2,296,128]{4,3,2,1,0:T(8,128)(2,1)S(1)} collective-permute-done((bf16[2,2,2,296,128]{4,3,2,1,0:T(8,128)(2,1)S(1)}, bf16[2,2,2,296,128]{4,3,2,1,0:T(8,128)(2,1)S(1)}, u32[]{:S(2)}, u32[]{:S(2)}) %collective-permute-start.7) | collective-permute-done | bytes 606240 | tf_op jit(solution)/shard_map/ppermute | solution.py:318
  25.7 0.1 halve.8
  25.8 0.0 copy-start
  25.8 1.0 %collective-permute-start.8 = (bf16[2,2,296,128]{3,2,1,0:T(8,128)(2,1)S(1)}, bf16[2,2,296,128]{3,2,1,0:T(8,128)(2,1)S(1)}, u32[]{:S(2)}, u32[]{:S(2)}) collective-permute-start(bf16[2,2,296,128]{3,2,1,0:T(8,128)(2,1)S(1)} %get-tuple-element.76), channel_id=1, source_target_pairs={{0,4},{1,5},{2,6},{3,7},{4,0},{5,1},{6,2},{7,3},{8,12},{9,13},{10,... | collective-permute-start | bytes 909320 | tf_op jit(solution)/shard_map/ppermute | solution.py:318
  26.7 0.1 halve.6
  26.9 0.1 collective-permute-start.6
  27.0 0.9 %collective-permute-start.9 = (bf16[2,600,128]{2,1,0:T(8,128)(2,1)S(1)}, bf16[2,600,128]{2,1,0:T(8,128)(2,1)S(1)}, u32[]{:S(2)}, u32[]{:S(2)}) collective-permute-start(bf16[2,600,128]{2,1,0:T(8,128)(2,1)S(1)} %pad_maximum_fusion.refs_0_), channel_id=1, source_target_pairs={{0,1},{1,0},{2,3},{3,2},{4,5},{5,4},{6,7},{7,6},{8,9},{9,8},{10,11... | collective-permute-start | bytes 921608 | tf_op jit(solution)/shard_map/ppermute | solution.py:318
  27.9 0.0 collective-permute-start.11
  27.9 0.5 collective-permute-start.10
  28.5 5.8 %collective-permute-done.8.came = bf16[2,2,296,128]{3,2,1,0:T(8,128)(2,1)S(1)} collective-permute-done((bf16[2,2,296,128]{3,2,1,0:T(8,128)(2,1)S(1)}, bf16[2,2,296,128]{3,2,1,0:T(8,128)(2,1)S(1)}, u32[]{:S(2)}, u32[]{:S(2)}) %collective-permute-start.8) | collective-permute-done | bytes 303136 | tf_op jit(solution)/shard_map/ppermute | solution.py:318
  34.2 0.0 collective-permute-start.12
  34.2 0.1 halve.9
  34.3 0.9 %collective-permute-done.6.came = bf16[2,2,304,128]{3,2,1,0:T(8,128)(2,1)S(1)} collective-permute-done((bf16[2,2,304,128]{3,2,1,0:T(8,128)(2,1)S(1)}, bf16[2,2,304,128]{3,2,1,0:T(8,128)(2,1)S(1)}, u32[]{:S(2)}, u32[]{:S(2)}) %collective-permute-start.6) | collective-permute-done | bytes 311328 | tf_op jit(solution)/shard_map/ppermute | solution.py:318
  35.2 0.1 halve.7
  35.3 0.0 collective-permute-done.10.refs_4_
  35.3 0.9 %collective-permute-start.13 = (bf16[2,304,128]{2,1,0:T(8,128)(2,1)S(1)}, bf16[2,304,128]{2,1,0:T(8,128)(2,1)S(1)}, u32[]{:S(2)}, u32[]{:S(2)}) collective-permute-start(bf16[2,304,128]{2,1,0:T(8,128)(2,1)S(1)} %get-tuple-element.87), channel_id=1, source_target_pairs={{0,4},{1,5},{2,6},{3,7},{4,0},{5,1},{6,2},{7,3},{8,12},{9,13},{10,... | collective-permute-start | bytes 466952 | tf_op jit(solution)/shard_map/ppermute | solution.py:318
  36.2 2.6 %collective-permute-start.14 = (bf16[2,296,128]{2,1,0:T(8,128)(2,1)S(1)}, bf16[2,296,128]{2,1,0:T(8,128)(2,1)S(1)}, u32[]{:S(2)}, u32[]{:S(2)}) collective-permute-start(bf16[2,296,128]{2,1,0:T(8,128)(2,1)S(1)} %get-tuple-element.90), channel_id=1, source_target_pairs={{0,8},{1,9},{2,10},{3,11},{4,12},{5,13},{6,14},{7,15},{8,0},{9,1},... | collective-permute-start | bytes 454664 | tf_op jit(solution)/shard_map/ppermute | solution.py:318
  38.8 3.5 %collective-permute-done.14.came = bf16[2,296,128]{2,1,0:T(8,128)(2,1)S(1)} collective-permute-done((bf16[2,296,128]{2,1,0:T(8,128)(2,1)S(1)}, bf16[2,296,128]{2,1,0:T(8,128)(2,1)S(1)}, u32[]{:S(2)}, u32[]{:S(2)}) %collective-permute-start.14) | collective-permute-done | bytes 151584 | tf_op jit(solution)/shard_map/ppermute | solution.py:318
  42.4 0.0 collective-permute-done.13.came
  42.4 3.3 %collective-permute-start.15 = (bf16[2,600,128]{2,1,0:T(8,128)(2,1)S(1)}, bf16[2,600,128]{2,1,0:T(8,128)(2,1)S(1)}, u32[]{:S(2)}, u32[]{:S(2)}) collective-permute-start(bf16[2,600,128]{2,1,0:T(8,128)(2,1)S(1)} %collective-permute-done.12.refs_6_), channel_id=1, source_target_pairs={{0,1},{1,0},{2,3},{3,2},{4,5},{5,4},{6,7},{7,6},{8,9},{9,8},{10,11... | collective-permute-start | bytes 921608 | tf_op jit(solution)/shard_map/ppermute | solution.py:318
  45.7 1.4 %collective-permute-start.18 = (bf16[304,128]{1,0:T(8,128)(2,1)S(1)}, bf16[304,128]{1,0:T(8,128)(2,1)S(1)}, u32[]{:S(2)}, u32[]{:S(2)}) collective-permute-start(bf16[304,128]{1,0:T(8,128)(2,1)S(1)} %get-tuple-element.88), channel_id=1, source_target_pairs={{0,8},{1,9},{2,10},{3,11},{4,12},{5,13},{6,14},{7,15},{8,0},{9,1},... | collective-permute-start | bytes 233480 | tf_op jit(solution)/shard_map/ppermute | solution.py:318
  47.1 0.8 %collective-permute-start.19 = (bf16[296,128]{1,0:T(8,128)(2,1)S(1)}, bf16[296,128]{1,0:T(8,128)(2,1)S(1)}, u32[]{:S(2)}, u32[]{:S(2)}) collective-permute-start(bf16[296,128]{1,0:T(8,128)(2,1)S(1)} %get-tuple-element.91), channel_id=1, source_target_pairs={{0,2},{1,3},{2,0},{3,1},{4,6},{5,7},{6,4},{7,5},{8,10},{9,11},{10,... | collective-permute-start | bytes 227336 | tf_op jit(solution)/shard_map/ppermute | solution.py:318
  47.9 0.0 collective-permute-done.15.refs_7_
  47.9 3.5 %backward.1 = (bf16[25,8,128]{2,1,0:T(8,128)(2,1)S(1)}, f32[25,8,128]{2,1,0:T(8,128)S(1)}, bf16[25,8,128]{2,1,0:T(8,128)(2,1)S(1)}) custom-call(bf16[2,600,128]{2,1,0:T(8,128)(2,1)S(1)} %pad_maximum_fusion.refs_0_, bf16[2,600,128]{2,1,0:T(8,128)(2,1)S(1)} %collective-permute-done.3.refs_1_, bf16[2,600,128]{2,1,0:T(8,128)(2,1)S(1)} %collective-permute-done.4.refs_2_, ...), custom_call_target="tpu_custom_call" | custom-call | flops 1000 | bytes 1000 | tf_op jit(solution)/shard_map/backward/pallas_call | solution.py:484
  51.4 0.7 %collective-permute-start.16 = (bf16[25,8,128]{2,1,0:T(8,128)(2,1)S(1)}, bf16[25,8,128]{2,1,0:T(8,128)(2,1)S(1)}, u32[]{:S(2)}, u32[]{:S(2)}) collective-permute-start(bf16[25,8,128]{2,1,0:T(8,128)(2,1)S(1)} %get-tuple-element.94), channel_id=1, source_target_pairs={{0,1},{1,0},{2,3},{3,2},{4,5},{5,4},{6,7},{7,6},{8,9},{9,8},{10,11... | collective-permute-start | bytes 153608 | tf_op jit(solution)/shard_map/ppermute | solution.py:318
  52.1 0.0 collective-permute-done.19.came
  52.1 0.0 collective-permute-done.18.came
  52.1 1.3 %collective-permute-start.20 = (bf16[304,128]{1,0:T(8,128)(2,1)S(1)}, bf16[304,128]{1,0:T(8,128)(2,1)S(1)}, u32[]{:S(2)}, u32[]{:S(2)}) collective-permute-start(bf16[304,128]{1,0:T(8,128)(2,1)S(1)} %get-tuple-element.99), channel_id=1, source_target_pairs={{0,16},{16,0},{1,17},{17,1},{2,18},{18,2},{3,19},{19,3},{4,20},{20... | collective-permute-start | bytes 233480 | tf_op jit(solution)/shard_map/ppermute | solution.py:526
  53.4 0.3 collective-permute-start.21
  53.8 5.2 %collective-permute-start.17 = (bf16[25,8,128]{2,1,0:T(8,128)(2,1)S(1)}, bf16[25,8,128]{2,1,0:T(8,128)(2,1)S(1)}, u32[]{:S(2)}, u32[]{:S(2)}) collective-permute-start(bf16[25,8,128]{2,1,0:T(8,128)(2,1)S(1)} %get-tuple-element.96), channel_id=1, source_target_pairs={{1,2},{3,4},{5,6},{7,8},{9,10},{11,12},{13,14},{2,1},{4,3},{6,5},{... | collective-permute-start | bytes 153608 | tf_op jit(solution)/shard_map/ppermute | solution.py:324
  59.0 1.8 %experts.2.refs_1_ = f32[16,76800]{1,0:T(8,128)} custom-call(f32[2,32]{1,0:T(2,128)S(1)} %copy-done, f32[304,128]{1,0:T(8,128)S(1)} %get-tuple-element.105.own_rows, bf16[304,128]{1,0:T(8,128)(2,1)S(1)} %collective-permute-done.20.refs_0_), custom_call_target="tpu_custom_call" | custom-call | flops 1000 | bytes 1000 | tf_op jit(solution)/shard_map/experts/pallas_call | solution.py:532
  60.8 1.9 %experts.3 = f32[16,76800]{1,0:T(8,128)} custom-call(f32[2,32]{1,0:T(2,128)S(1)} %copy-done, f32[296,128]{1,0:T(8,128)S(1)} %get-tuple-element.104.own_rows, bf16[296,128]{1,0:T(8,128)(2,1)S(1)} %collective-permute-done.21.refs_0_, f32[16,76800]{1,0:T(8,128)} %experts.2.refs_1_), custom_call_target="tpu_custom_call", output_to_operand_aliasing={{}: (3, {})} | custom-call | flops 1000 | bytes 1000 | tf_op jit(solution)/shard_map/experts/pallas_call | solution.py:532
  62.8 0.7 %add_bitcast_fusion = f32[1,8,25,128]{3,1,2,0:T(8,128)} fusion(bf16[25,8,128]{2,1,0:T(8,128)(2,1)S(1)} %collective-permute-done.17, f32[25,8,128]{2,1,0:T(8,128)S(1)} %get-tuple-element.93, bf16[25,8,128]{2,1,0:T(8,128)(2,1)S(1)} %collective-permute-done.16), kind=kLoop, calls=%fused_computation.1 | loop fusion | flops 102400 | bytes 307200 | tf_op jit(solution)/shard_map/broadcast_in_dim | solution.py:549
  (14 shorter events, 0.2 us)
Async XLA Ops:
  1.8 10.6 %collective-permute-start.1 = (bf16[1,600,128]{2,1,0:T(8,128)(2,1)S(1)}, bf16[1,600,128]{2,1,0:T(8,128)(2,1)S(1)}, u32[]{:S(2)}, u32[]{:S(2)}) collective-permute-start(bf16[1,600,128]{2,1,0:T(8,128)(2,1)S(1)} %rows.1), channel_id=1, source_target_pairs={{0,8},{1,9},{2,10},{3,11},{4,12},{5,13},{6,14},{7,15},{8,0},{9,1},... | collective-permute-start | bytes 460808 | tf_op jit(solution)/shard_map/ppermute | solution.py:318
  5.0 4.6 %collective-permute-start = (bf16[25,8,128]{2,1,0:T(8,128)(2,1)}, bf16[25,8,128]{2,1,0:T(8,128)(2,1)S(1)}, u32[]{:S(2)}, u32[]{:S(2)}) collective-permute-start(bf16[25,8,128]{2,1,0:T(8,128)(2,1)} %bitcast.17), channel_id=1, source_target_pairs={{0,1},{1,0},{2,3},{3,2},{4,5},{5,4},{6,7},{7,6},{8,9},{9,8},{10,11... | collective-permute-start | bytes 153608 | tf_op jit(solution)/shard_map/ppermute | solution.py:318
  6.0 6.5 %collective-permute-start.2 = (bf16[25,8,128]{2,1,0:T(8,128)(2,1)}, bf16[25,8,128]{2,1,0:T(8,128)(2,1)S(1)}, u32[]{:S(2)}, u32[]{:S(2)}) collective-permute-start(bf16[25,8,128]{2,1,0:T(8,128)(2,1)} %bitcast.18), channel_id=1, source_target_pairs={{1,2},{3,4},{5,6},{7,8},{9,10},{11,12},{13,14},{2,1},{4,3},{6,5},{... | collective-permute-start | bytes 153608 | tf_op jit(solution)/shard_map/ppermute | solution.py:324
  12.5 8.6 %collective-permute-start.4 = (bf16[2,600,128]{2,1,0:T(8,128)(2,1)S(1)}, bf16[2,600,128]{2,1,0:T(8,128)(2,1)S(1)}, u32[]{:S(2)}, u32[]{:S(2)}) collective-permute-start(bf16[2,600,128]{2,1,0:T(8,128)(2,1)S(1)} %pad_maximum_fusion.refs_0_), channel_id=1, source_target_pairs={{0,2},{1,3},{2,0},{3,1},{4,6},{5,7},{6,4},{7,5},{8,10},{9,11},{10,... | collective-permute-start | bytes 921608 | tf_op jit(solution)/shard_map/ppermute | solution.py:318
  14.3 8.2 %collective-permute-start.3 = (bf16[2,600,128]{2,1,0:T(8,128)(2,1)S(1)}, bf16[2,600,128]{2,1,0:T(8,128)(2,1)S(1)}, u32[]{:S(2)}, u32[]{:S(2)}) collective-permute-start(bf16[2,600,128]{2,1,0:T(8,128)(2,1)S(1)} %pad_maximum_fusion.refs_0_), channel_id=1, source_target_pairs={{0,4},{1,5},{2,6},{3,7},{4,0},{5,1},{6,2},{7,3},{8,12},{9,13},{10,... | collective-permute-start | bytes 921608 | tf_op jit(solution)/shard_map/ppermute | solution.py:318
  22.5 3.2 %collective-permute-start.7 = (bf16[2,2,2,296,128]{4,3,2,1,0:T(8,128)(2,1)S(1)}, bf16[2,2,2,296,128]{4,3,2,1,0:T(8,128)(2,1)S(1)}, u32[]{:S(2)}, u32[]{:S(2)}) collective-permute-start(bf16[2,2,2,296,128]{4,3,2,1,0:T(8,128)(2,1)S(1)} %get-tuple-element.74), channel_id=1, source_target_pairs={{0,1},{1,0},{2,3},{3,2},{4,5},{5,4},{6,7},{7,6},{8,9},{9,8},{10,11... | collective-permute-start | bytes 1818632 | tf_op jit(solution)/shard_map/ppermute | solution.py:318
  24.0 2.7 %collective-permute-start.5 = (bf16[2,2,2,304,128]{4,3,2,1,0:T(8,128)(2,1)S(1)}, bf16[2,2,2,304,128]{4,3,2,1,0:T(8,128)(2,1)S(1)}, u32[]{:S(2)}, u32[]{:S(2)}) collective-permute-start(bf16[2,2,2,304,128]{4,3,2,1,0:T(8,128)(2,1)S(1)} %get-tuple-element.69), channel_id=1, source_target_pairs={{0,1},{1,0},{2,3},{3,2},{4,5},{5,4},{6,7},{7,6},{8,9},{9,8},{10,11... | collective-permute-start | bytes 1867784 | tf_op jit(solution)/shard_map/ppermute | solution.py:318
  25.8 33.2 %copy-start = (f32[2,32]{1,0:T(2,128)S(1)}, f32[2,32]{1,0:T(2,128)}, u32[]{:S(2)}) copy-start(f32[2,32]{1,0:T(2,128)} %mixing.3) | copy-start | bytes 772
  25.8 8.5 %collective-permute-start.8 = (bf16[2,2,296,128]{3,2,1,0:T(8,128)(2,1)S(1)}, bf16[2,2,296,128]{3,2,1,0:T(8,128)(2,1)S(1)}, u32[]{:S(2)}, u32[]{:S(2)}) collective-permute-start(bf16[2,2,296,128]{3,2,1,0:T(8,128)(2,1)S(1)} %get-tuple-element.76), channel_id=1, source_target_pairs={{0,4},{1,5},{2,6},{3,7},{4,0},{5,1},{6,2},{7,3},{8,12},{9,13},{10,... | collective-permute-start | bytes 909320 | tf_op jit(solution)/shard_map/ppermute | solution.py:318
  26.9 8.3 %collective-permute-start.6 = (bf16[2,2,304,128]{3,2,1,0:T(8,128)(2,1)S(1)}, bf16[2,2,304,128]{3,2,1,0:T(8,128)(2,1)S(1)}, u32[]{:S(2)}, u32[]{:S(2)}) collective-permute-start(bf16[2,2,304,128]{3,2,1,0:T(8,128)(2,1)S(1)} %get-tuple-element.71), channel_id=1, source_target_pairs={{0,2},{1,3},{2,0},{3,1},{4,6},{5,7},{6,4},{7,5},{8,10},{9,11},{10,... | collective-permute-start | bytes 933896 | tf_op jit(solution)/shard_map/ppermute | solution.py:318
  27.0 8.2 %collective-permute-start.9 = (bf16[2,600,128]{2,1,0:T(8,128)(2,1)S(1)}, bf16[2,600,128]{2,1,0:T(8,128)(2,1)S(1)}, u32[]{:S(2)}, u32[]{:S(2)}) collective-permute-start(bf16[2,600,128]{2,1,0:T(8,128)(2,1)S(1)} %pad_maximum_fusion.refs_0_), channel_id=1, source_target_pairs={{0,1},{1,0},{2,3},{3,2},{4,5},{5,4},{6,7},{7,6},{8,9},{9,8},{10,11... | collective-permute-start | bytes 921608 | tf_op jit(solution)/shard_map/ppermute | solution.py:318
  27.9 7.3 %collective-permute-start.11 = (bf16[2,600,128]{2,1,0:T(8,128)(2,1)S(1)}, bf16[2,600,128]{2,1,0:T(8,128)(2,1)S(1)}, u32[]{:S(2)}, u32[]{:S(2)}) collective-permute-start(bf16[2,600,128]{2,1,0:T(8,128)(2,1)S(1)} %collective-permute-done.4.refs_2_), channel_id=1, source_target_pairs={{0,1},{1,0},{2,3},{3,2},{4,5},{5,4},{6,7},{7,6},{8,9},{9,8},{10,11... | collective-permute-start | bytes 921608 | tf_op jit(solution)/shard_map/ppermute | solution.py:318
  27.9 7.3 %collective-permute-start.10 = (bf16[2,600,128]{2,1,0:T(8,128)(2,1)S(1)}, bf16[2,600,128]{2,1,0:T(8,128)(2,1)S(1)}, u32[]{:S(2)}, u32[]{:S(2)}) collective-permute-start(bf16[2,600,128]{2,1,0:T(8,128)(2,1)S(1)} %collective-permute-done.3.refs_1_), channel_id=1, source_target_pairs={{0,1},{1,0},{2,3},{3,2},{4,5},{5,4},{6,7},{7,6},{8,9},{9,8},{10,11... | collective-permute-start | bytes 921608 | tf_op jit(solution)/shard_map/ppermute | solution.py:318
  34.2 8.2 %collective-permute-start.12 = (bf16[2,600,128]{2,1,0:T(8,128)(2,1)S(1)}, bf16[2,600,128]{2,1,0:T(8,128)(2,1)S(1)}, u32[]{:S(2)}, u32[]{:S(2)}) collective-permute-start(bf16[2,600,128]{2,1,0:T(8,128)(2,1)S(1)} %collective-permute-done.3.refs_1_), channel_id=1, source_target_pairs={{0,2},{1,3},{2,0},{3,1},{4,6},{5,7},{6,4},{7,5},{8,10},{9,11},{10,... | collective-permute-start | bytes 921608 | tf_op jit(solution)/shard_map/ppermute | solution.py:318
  35.3 7.1 %collective-permute-start.13 = (bf16[2,304,128]{2,1,0:T(8,128)(2,1)S(1)}, bf16[2,304,128]{2,1,0:T(8,128)(2,1)S(1)}, u32[]{:S(2)}, u32[]{:S(2)}) collective-permute-start(bf16[2,304,128]{2,1,0:T(8,128)(2,1)S(1)} %get-tuple-element.87), channel_id=1, source_target_pairs={{0,4},{1,5},{2,6},{3,7},{4,0},{5,1},{6,2},{7,3},{8,12},{9,13},{10,... | collective-permute-start | bytes 466952 | tf_op jit(solution)/shard_map/ppermute | solution.py:318
  36.2 6.1 %collective-permute-start.14 = (bf16[2,296,128]{2,1,0:T(8,128)(2,1)S(1)}, bf16[2,296,128]{2,1,0:T(8,128)(2,1)S(1)}, u32[]{:S(2)}, u32[]{:S(2)}) collective-permute-start(bf16[2,296,128]{2,1,0:T(8,128)(2,1)S(1)} %get-tuple-element.90), channel_id=1, source_target_pairs={{0,8},{1,9},{2,10},{3,11},{4,12},{5,13},{6,14},{7,15},{8,0},{9,1},... | collective-permute-start | bytes 454664 | tf_op jit(solution)/shard_map/ppermute | solution.py:318
  42.4 5.5 %collective-permute-start.15 = (bf16[2,600,128]{2,1,0:T(8,128)(2,1)S(1)}, bf16[2,600,128]{2,1,0:T(8,128)(2,1)S(1)}, u32[]{:S(2)}, u32[]{:S(2)}) collective-permute-start(bf16[2,600,128]{2,1,0:T(8,128)(2,1)S(1)} %collective-permute-done.12.refs_6_), channel_id=1, source_target_pairs={{0,1},{1,0},{2,3},{3,2},{4,5},{5,4},{6,7},{7,6},{8,9},{9,8},{10,11... | collective-permute-start | bytes 921608 | tf_op jit(solution)/shard_map/ppermute | solution.py:318
  45.7 6.4 %collective-permute-start.18 = (bf16[304,128]{1,0:T(8,128)(2,1)S(1)}, bf16[304,128]{1,0:T(8,128)(2,1)S(1)}, u32[]{:S(2)}, u32[]{:S(2)}) collective-permute-start(bf16[304,128]{1,0:T(8,128)(2,1)S(1)} %get-tuple-element.88), channel_id=1, source_target_pairs={{0,8},{1,9},{2,10},{3,11},{4,12},{5,13},{6,14},{7,15},{8,0},{9,1},... | collective-permute-start | bytes 233480 | tf_op jit(solution)/shard_map/ppermute | solution.py:318
  47.1 5.0 %collective-permute-start.19 = (bf16[296,128]{1,0:T(8,128)(2,1)S(1)}, bf16[296,128]{1,0:T(8,128)(2,1)S(1)}, u32[]{:S(2)}, u32[]{:S(2)}) collective-permute-start(bf16[296,128]{1,0:T(8,128)(2,1)S(1)} %get-tuple-element.91), channel_id=1, source_target_pairs={{0,2},{1,3},{2,0},{3,1},{4,6},{5,7},{6,4},{7,5},{8,10},{9,11},{10,... | collective-permute-start | bytes 227336 | tf_op jit(solution)/shard_map/ppermute | solution.py:318
  51.4 2.3 %collective-permute-start.16 = (bf16[25,8,128]{2,1,0:T(8,128)(2,1)S(1)}, bf16[25,8,128]{2,1,0:T(8,128)(2,1)S(1)}, u32[]{:S(2)}, u32[]{:S(2)}) collective-permute-start(bf16[25,8,128]{2,1,0:T(8,128)(2,1)S(1)} %get-tuple-element.94), channel_id=1, source_target_pairs={{0,1},{1,0},{2,3},{3,2},{4,5},{5,4},{6,7},{7,6},{8,9},{9,8},{10,11... | collective-permute-start | bytes 153608 | tf_op jit(solution)/shard_map/ppermute | solution.py:318
  52.1 6.8 %collective-permute-start.20 = (bf16[304,128]{1,0:T(8,128)(2,1)S(1)}, bf16[304,128]{1,0:T(8,128)(2,1)S(1)}, u32[]{:S(2)}, u32[]{:S(2)}) collective-permute-start(bf16[304,128]{1,0:T(8,128)(2,1)S(1)} %get-tuple-element.99), channel_id=1, source_target_pairs={{0,16},{16,0},{1,17},{17,1},{2,18},{18,2},{3,19},{19,3},{4,20},{20... | collective-permute-start | bytes 233480 | tf_op jit(solution)/shard_map/ppermute | solution.py:526
  53.4 7.4 %collective-permute-start.21 = (bf16[296,128]{1,0:T(8,128)(2,1)S(1)}, bf16[296,128]{1,0:T(8,128)(2,1)S(1)}, u32[]{:S(2)}, u32[]{:S(2)}) collective-permute-start(bf16[296,128]{1,0:T(8,128)(2,1)S(1)} %get-tuple-element.102), channel_id=1, source_target_pairs={{0,16},{16,0},{1,17},{17,1},{2,18},{18,2},{3,19},{19,3},{4,20},{20... | collective-permute-start | bytes 227336 | tf_op jit(solution)/shard_map/ppermute | solution.py:526
  53.8 9.0 %collective-permute-start.17 = (bf16[25,8,128]{2,1,0:T(8,128)(2,1)S(1)}, bf16[25,8,128]{2,1,0:T(8,128)(2,1)S(1)}, u32[]{:S(2)}, u32[]{:S(2)}) collective-permute-start(bf16[25,8,128]{2,1,0:T(8,128)(2,1)S(1)} %get-tuple-element.96), channel_id=1, source_target_pairs={{1,2},{3,4},{5,6},{7,8},{9,10},{11,12},{13,14},{2,1},{4,3},{6,5},{... | collective-permute-start | bytes 153608 | tf_op jit(solution)/shard_map/ppermute | solution.py:324
